TPU v7x, 512 devices: a whole 4x8x8 slice. The times are simulated.
512 devices in a mesh: ctx: 64 (over x, y, core), kvh: 8 (over z).
Axes of the slice: x: 4, y: 8, z: 8, core: 2. Of those that a mesh axis runs over, the one named last changes fastest.
Arguments:
- queries: bfloat16 [8192, 8, 2, 128], P('ctx', 'kvh'), may hold values from -48 to 48
- keys: bfloat16 [8192, 8, 128], P('ctx', 'kvh'), may hold values from -6 to 6
- values: bfloat16 [8192, 8, 128], P('ctx', 'kvh'), may hold values from -6 to 6
- w_query: float32 [128, 128], replicated, may hold values from -0.5 to 0.5
- w_key: float32 [128, 128], replicated, may hold values from -0.5 to 0.5
Outputs:
- student_out: bfloat16 [8192, 8, 2, 128], P('ctx', 'kvh')
- grad_query: float32 [128, 128], replicated
- grad_key: float32 [128, 128], replicated
- loss: float32 [], replicated
All inputs are finite; a program needn't handle non-finite values.
Results may differ from a plain program's by a relative error of at most 0.0035.
Values may be sent and summed in bfloat16 or wider, within the bound.
No kernel may reach another device: no remote copies, remote signals or barrier semaphores. Data moves between devices by JAX's collectives and lax.ppermute only.
A program may use at most 64 MiB of HBM per device.

v0:
```python
import jax
import jax.numpy as jnp
from jax import lax
from jax.sharding import PartitionSpec as P

HIGH = lax.Precision.HIGHEST


def entering(shard, axis, join, neutral):
    place = lax.axis_index(axis)
    gathered = jax.tree.map(
        lambda a, kind: lax.all_gather(a.astype(kind), axis), shard, (jnp.bfloat16, jnp.bfloat16)
    )
    state = jax.tree.map(lambda a, e: jnp.zeros_like(a) + jnp.asarray(e, a.dtype), shard, neutral)

    def one(step, state):
        return join(
            state,
            jax.tree.map(
                lambda a, own: lax.dynamic_index_in_dim(a, step, 0, False).astype(own.dtype),
                gathered,
                shard,
            ),
        )

    return lax.fori_loop(0, place, one, state)


def entering_2(shard, axis, combine, identity):
    length, position = (lax.axis_size(axis), lax.axis_index(axis))
    everything = jax.tree.map(
        lambda part, kind: lax.all_gather(part.astype(kind), axis),
        shard,
        jax.tree.map(lambda a: jnp.bfloat16 if a.dtype == jnp.float32 else a.dtype, shard),
    )
    start = jax.tree.map(
        lambda part, zero: jnp.broadcast_to(jnp.asarray(zero, part.dtype), part.shape),
        shard,
        identity,
    )

    def step(k, before):
        at = length - 1 - k
        reached = at > position
        new = combine(
            before, jax.tree.map(lambda part, own: part[at].astype(own.dtype), everything, shard)
        )
        return jax.tree.map(lambda a, b: jnp.where(reached, a, b), new, before)

    return lax.fori_loop(0, length, step, start)


def features(rows, weight):
    pre = jnp.einsum("...h,he->...e", rows.astype(jnp.float32), weight, precision=HIGH)
    return (pre, jnp.concatenate([jax.nn.softplus(pre), jax.nn.softplus(-pre)], -1))


def teacher_step(carry, queries, query_pos, kblock, vblock, key_pos, scale):
    best, total, accum = carry
    scores = (
        jnp.einsum("tgph,ngh->tgpn", queries, kblock, preferred_element_type=jnp.float32) * scale
    )
    allowed = key_pos[None, None, None, :] <= query_pos[:, None, None, None]
    scores = jnp.where(allowed, scores, -1e30)
    newbest = jnp.maximum(best, scores.max(-1))
    weights = jnp.where(allowed, jnp.exp(scores - newbest[..., None]), 0.0).astype(jnp.bfloat16)
    factor = jnp.exp(best - newbest)
    total = total * factor + weights.astype(jnp.float32).sum(-1)
    accum = accum * factor[..., None] + jnp.einsum(
        "tgpn,ngh->tgph", weights, vblock, preferred_element_type=jnp.float32
    )
    return (newbest, total, accum)


def run_fold(carry, piece, query_sets):
    key_piece, val_piece = piece
    count = key_piece.shape[0]
    width = 512
    scale = query_sets[0][0].shape[3] ** (-0.5)

    def one_block(index, inner):
        begin = index * width
        kblock = lax.dynamic_slice_in_dim(key_piece, index * width, width, 0)
        vblock = lax.dynamic_slice_in_dim(val_piece, index * width, width, 0)
        key_pos = begin + jnp.arange(width, dtype=jnp.int32)
        results = ()
        rows_q, pos_q, last_q = query_sets[0]

        def work(state, rows_q=rows_q, pos_q=pos_q):
            return teacher_step(state, rows_q, pos_q, kblock, vblock, key_pos, scale)

        def keep(state):
            return state

        results = results + lax.cond(begin <= last_q, work, keep, inner[0:3])
        return results

    return lax.fori_loop(0, count // width, one_block, carry)


def add_states(earlier, later):
    return (earlier[0] + later[0], earlier[1] + later[1])


def teacher_start(count, groups, per_group, head):
    return (
        jnp.full((count, groups, per_group), -1e30, jnp.float32),
        jnp.zeros((count, groups, per_group), jnp.float32),
        jnp.zeros((count, groups, per_group, head), jnp.float32),
    )


def shards(queries, keys, values, w_query, w_key):
    rows, groups, per_group, head = queries.shape
    feats = 2 * w_query.shape[1]
    half = w_query.shape[1]
    first = lax.axis_index("ctx") * rows
    last = first + rows - 1
    query_pos = first + jnp.arange(rows, dtype=jnp.int32)
    zero_states = (
        jnp.zeros((groups, feats, head), jnp.float32),
        jnp.zeros((groups, feats), jnp.float32),
    )
    pre_key, key_feats = features(keys, w_key)
    val_rows = values.astype(jnp.float32)
    query_sets = [(queries, query_pos, last)]
    start_teacher = teacher_start(rows, groups, per_group, head)
    folded = run_fold(
        start_teacher,
        (
            lax.all_gather(keys, "ctx", axis=0, tiled=True),
            lax.all_gather(values, "ctx", axis=0, tiled=True),
        ),
        query_sets,
    )
    local_sum = jnp.einsum("ngf,ngh->gfh", key_feats, val_rows, precision=HIGH)
    summed, normer = entering((local_sum, key_feats.sum(0)), "ctx", add_states, zero_states)
    targets = (folded[2] / folded[1][..., None]).astype(jnp.bfloat16)
    pre_query, query_feats = features(queries, w_query)
    causal = (jnp.arange(rows)[:, None] >= jnp.arange(rows)[None, :])[:, None, None, :]
    attn = jnp.where(
        causal, jnp.einsum("tgpf,ngf->tgpn", query_feats, key_feats, precision=HIGH), 0.0
    )
    num = jnp.einsum("tgpn,ngh->tgph", attn, val_rows, precision=HIGH) + jnp.einsum(
        "tgpf,gfh->tgph", query_feats, summed, precision=HIGH
    )
    den = attn.sum(-1) + jnp.einsum("tgpf,gf->tgp", query_feats, normer, precision=HIGH)
    outs = num / den[..., None]
    diff = outs - targets.astype(jnp.float32)
    count = float(rows * lax.axis_size("ctx") * groups * lax.axis_size("kvh") * per_group)
    loss_part = jnp.sum(diff * diff) / count
    grad_out = 2.0 * diff / count
    d_num = grad_out / den[..., None]
    d_den = -jnp.sum(grad_out * outs, -1) / den
    d_attn = jnp.where(
        causal,
        jnp.einsum("tgph,ngh->tgpn", d_num, val_rows, precision=HIGH) + d_den[..., None],
        0.0,
    )
    d_query = jnp.einsum("tgpn,ngf->tgpf", d_attn, key_feats, precision=HIGH)
    d_query = (
        d_query
        + jnp.einsum("tgph,gfh->tgpf", d_num, summed, precision=HIGH)
        + d_den[..., None] * normer[None, :, None, :]
    )
    d_key = jnp.einsum("tgpn,tgpf->ngf", d_attn, query_feats, precision=HIGH)
    later_sum = jnp.einsum("tgpf,tgph->gfh", query_feats, d_num, precision=HIGH)
    later_norm = jnp.einsum("tgpf,tgp->gf", query_feats, d_den, precision=HIGH)
    after_sum, after_norm = entering_2((later_sum, later_norm), "ctx", add_states, zero_states)
    d_key = (
        d_key + jnp.einsum("gfh,ngh->ngf", after_sum, val_rows, precision=HIGH) + after_norm[None]
    )
    d_pre_query = d_query[..., :half] * jax.nn.sigmoid(pre_query) - d_query[
        ..., half:
    ] * jax.nn.sigmoid(-pre_query)
    d_pre_key = d_key[..., :half] * jax.nn.sigmoid(pre_key) - d_key[..., half:] * jax.nn.sigmoid(
        -pre_key
    )
    grad_query = jnp.einsum(
        "tgph,tgpe->he", queries.astype(jnp.float32), d_pre_query, precision=HIGH
    )
    grad_key = jnp.einsum("tgh,tge->he", keys.astype(jnp.float32), d_pre_key, precision=HIGH)
    grad_query, grad_key, loss = lax.psum((grad_query, grad_key, loss_part), ("ctx", "kvh"))
    return (outs.astype(jnp.bfloat16), grad_query, grad_key, loss)


def solution(mesh):
    placed = (P("ctx", "kvh", None, None), P("ctx", "kvh", None), P("ctx", "kvh", None), P(), P())
    return jax.shard_map(
        shards,
        mesh=mesh,
        in_specs=placed,
        out_specs=(P("ctx", "kvh", None, None), P(), P(), P()),
        check_vma=False,
    )
```

profile of v0, /device:TPU:1, one launch (start us, length us, event | category | flops | bytes accessed | tf_op | source)
XLA Modules:
  0.0 738.5 jit_solution(812573305487829803)
XLA Ops:
  8.0 1.5 copy.42
  9.5 1.1 fusion.78
  10.7 1.6 convolution_convert_fusion
  13.4 43.3 %all-gather.4 = bf16[64,1,256]{2,1,0:T(2,128)(2,1)S(1)} all-gather(bf16[1,1,256]{2,1,0:T(2,128)(2,1)S(1)} %reshape.366), channel_id=3, replica_groups=mesh['ctx'=64,'kvh'=8] {'ctx'}, dimensions={0}, use_global_device_ids=true | all-gather | bytes 33280 | tf_op jit(solution)/shard_map/all_gather | solution.py:12
  56.7 1.1 fusion.60
  58.7 41.1 %all-gather.11.cloned.1.call-done = bf16[8192,1,128]{2,0,1:T(8,128)(2,1)} async-done(((bf16[128,1,128]{2,0,1:T(8,128)(2,1)}), bf16[8192,1,128]{2,0,1:T(8,128)(2,1)}) %all-gather.11.cloned.1.call-update) | async-done | bytes 2097168 | tf_op jit(solution)/shard_map/all_gather | solution.py:131
  99.8 79.5 %all-gather.13.cloned.1.call-done = bf16[8192,1,128]{0,2,1:T(8,128)(2,1)} async-done(((bf16[128,1,128]{0,2,1:T(8,128)(2,1)}), bf16[8192,1,128]{0,2,1:T(8,128)(2,1)}) %all-gather.13.cloned.1.call-update) | async-done | bytes 2097168 | tf_op jit(solution)/shard_map/all_gather | solution.py:132
  179.3 3.8 while.49
  179.3 2.7 conditional.3
  179.5 1.2 fusion.94
  180.8 1.2 fusion.4
  183.1 83.9 %all-gather.15.cloned.1.call-done = bf16[16384,128]{1,0:T(8,128)(2,1)} async-done(((bf16[256,128]{1,0:T(8,128)(2,1)}), bf16[16384,128]{1,0:T(8,128)(2,1)}) %all-gather.15.cloned.1.call-update) | async-done | bytes 4194320 | tf_op jit(solution)/shard_map/all_gather | solution.py:12
  267.0 0.9 while.48
  268.2 1.0 multiply_reduce_fusion
  269.2 1.0 fusion.24
  270.7 91.6 %all-gather.5 = bf16[64,1,256]{2,1,0:T(2,128)(2,1)S(1)} all-gather(bf16[1,1,256]{2,1,0:T(2,128)(2,1)S(1)} %reshape.368), channel_id=5, replica_groups=mesh['ctx'=64,'kvh'=8] {'ctx'}, dimensions={0}, use_global_device_ids=true | all-gather | bytes 33280 | tf_op jit(solution)/shard_map/all_gather | solution.py:32
  364.2 42.4 %all-gather.17.cloned.1.call-done = bf16[16384,128]{1,0:T(8,128)(2,1)} async-done(((bf16[256,128]{1,0:T(8,128)(2,1)}), bf16[16384,128]{1,0:T(8,128)(2,1)}) %all-gather.17.cloned.1.call-update) | async-done | bytes 4194320 | tf_op jit(solution)/shard_map/all_gather | solution.py:32
  406.6 60.9 %while.50 = (s32[]{:T(128)}, f32[1,256,128]{2,1,0:T(8,128)S(1)}, f32[1,256]{1,0:T(1,128)S(1)}, s32[]{:T(128)}, bf16[64,1,256,128]{3,2,1,0:T(8,128)(2,1)}, /*inde...) while((s32[]{:T(128)}, f32[1,256,128]{2,1,0:T(8,128)S(1)}, ...), condition=%wide.region_13.14_spmd.clone, body=%wide.region_12.13_spmd.clone.sunk | while | flops 132104 | bytes 330425 | solution.py:50
  409.4 0.9 add_select_fusion.2
  410.4 0.9 add_select_fusion.2
  469.6 97.6 %psum.23 = f32[]{:T(128)} all-reduce(f32[]{:T(128)S(6)} %div.85), channel_id=1, replica_groups=mesh['ctx'=64,'kvh'=8] {'ctx','kvh'}, use_global_device_ids=true, to_apply=%region_16.17 | all-reduce | flops 1 | bytes 8 | tf_op jit(solution)/shard_map/psum | solution.py:183
  568.0 160.8 %all-reduce.3.cloned.1.call-done = (f32[128,128]{0,1:T(8,128)}, f32[128,128]{0,1:T(8,128)}) async-done(((f32[128,128]{0,1:T(8,128)}, f32[128,128]{0,1:T(8,128)}), (f32[128,128]{0,1:T(8,128)}, f32[128,128]{0,1:T(8,128)})) %all-reduce.3.cloned.1.call-update) | async-done | bytes 131088 | tf_op jit(solution)/shard_map/psum | solution.py:183
  728.8 1.6 copy.53
  730.4 1.6 copy.54
  (229 shorter events, 66.1 us)
Async XLA Ops:
  7.2 49.6 %copy-start = (f32[128,128]{1,0:T(8,128)S(1)}, f32[128,128]{1,0:T(8,128)}, u32[]{:S(2)}) copy-start(f32[128,128]{1,0:T(8,128)} %param.16) | copy-start | bytes 196612
  7.2 51.2 %copy-start.1 = (bf16[128,1,128]{2,0,1:T(8,128)(2,1)S(1)}, bf16[128,1,128]{2,0,1:T(8,128)(2,1)}, u32[]{:S(2)}) copy-start(bf16[128,1,128]{2,0,1:T(8,128)(2,1)} %param.15) | copy-start | bytes 98308
  7.2 92.6 %all-gather.11.cloned.1.call-start = ((), (), s32[]{:S(2)}) async-start(), calls=%async_computation | async-start | bytes 2129920 | tf_op jit(solution)/shard_map/all_gather | solution.py:131
  7.9 171.3 %all-gather.13.cloned.1.call-start = ((), (), s32[]{:S(2)}) async-start(), calls=%async_computation.1 | async-start | bytes 2129920 | tf_op jit(solution)/shard_map/all_gather | solution.py:132
  9.5 257.5 %all-gather.15.cloned.1.call-start = ((), (), s32[]{:S(2)}) async-start(), calls=%async_computation.2 | async-start | bytes 4259840 | tf_op jit(solution)/shard_map/all_gather | solution.py:12
  12.3 394.2 %all-gather.17.cloned.1.call-start = ((), (), s32[]{:S(2)}) async-start(), calls=%async_computation.3 | async-start | bytes 4259840 | tf_op jit(solution)/shard_map/all_gather | solution.py:32
  268.1 95.1 %copy-start.2 = (bf16[128,1,2,128]{3,2,1,0:T(2,128)(2,1)S(1)}, bf16[128,1,2,128]{3,2,1,0:T(2,128)(2,1)}, u32[]{:S(2)}) copy-start(bf16[128,1,2,128]{3,2,1,0:T(2,128)(2,1)} %param.13) | copy-start | bytes 196612
  270.2 458.6 %all-reduce.3.cloned.1.call-start = ((), (), s32[]{:S(2)}) async-start(), calls=%async_computation.4 | async-start | bytes 262144 | tf_op jit(solution)/shard_map/psum | solution.py:183
  363.3 104.8 %copy-start.3 = (bf16[128,1,128]{2,0,1:T(8,128)(2,1)S(1)}, bf16[128,1,128]{2,0,1:T(8,128)(2,1)}, u32[]{:S(2)}) copy-start(bf16[128,1,128]{2,0,1:T(8,128)(2,1)} %param.14) | copy-start | bytes 98308
Sparse Core Ops, SparseCore 0:
  11.4 88.3 all-gather.10
  103.5 75.7 all-gather.12
  183.2 83.7 all-gather.14
  270.8 135.7 all-gather.16
  469.1 259.7 all-reduce.2
where the time goes:
time: 745 us; the launch traced here: 738 us
  waiting for transfers between devices  408 us (55%)
  blocking collectives  233 us (31%)
  other arithmetic  60.4 us (8%)
  between operations  14.7 us (2%)
  matrix products  12.6 us (2%)
    psum x1, waiting for transfers between devices, shards(): lax.psum((grad_query, grad_key, loss_part), ('ctx', 'kvh'))  161 us
    psum x1, blocking collectives, shards(): lax.psum((grad_query, grad_key, loss_part), ('ctx', 'kvh'))  97.6 us
    all_gather x1, blocking collectives, entering_2(): lax.all_gather(part.astype(kind), axis)  91.6 us
    all_gather x1, waiting for transfers between devices, entering(): lax.all_gather(a.astype(kind), axis)  83.9 us
    all_gather x1, waiting for transfers between devices, shards(): lax.all_gather(values, 'ctx', axis=0, tiled=True)  79.5 us
    select_n x128, other arithmetic, step(): return jax.tree.map(lambda a, b: jnp.where(reached, a, b), new, before)  58.9 us
    all_gather x1, blocking collectives, entering(): lax.all_gather(a.astype(kind), axis)  43.3 us
    all_gather x1, waiting for transfers between devices, entering_2(): lax.all_gather(part.astype(kind), axis)  42.4 us
  transfers between devices with their start and end apart: 5, of which 5 were waited for; matrix products, arithmetic and copies ran while one was open for 2% of the time, Pallas kernels for 0%

commit v1 on v0

v1 whole, which is shorter than its diff:
```python
import functools

import jax
import jax.numpy as jnp
from jax import lax
from jax.experimental import pallas as pl
from jax.experimental.pallas import tpu as pltpu
from jax.sharding import PartitionSpec as P

F32, BF16 = jnp.float32, jnp.bfloat16
NN = (((1,), (0,)), ((), ()))
NT = (((1,), (1,)), ((), ()))
LOG2E = 1.4426950408889634
CORES = 2


def dot(a, b, dims=NN):
    return lax.dot_general(a, b, dims, preferred_element_type=F32)


def halves(a):
    high = a.astype(BF16)
    return high, (a - high.astype(F32)).astype(BF16)


def dot3(a, b, dims=NN):
    ah, al = halves(a)
    bh, bl = halves(b)
    return dot(ah, bh, dims) + (dot(ah, bl, dims) + dot(al, bh, dims))


def dot2(a, b, dims=NN):
    ah, al = halves(a)
    return dot(ah, b, dims) + dot(al, b, dims)


def log1p(e):
    return jnp.where(e < 1e-3, e * (1.0 - e * (0.5 - e * (1.0 / 3.0))), jnp.log(1.0 + e))


def feature_parts(pre):
    e = jnp.exp(-jnp.abs(pre))
    t = log1p(e)
    r = 1.0 / (1.0 + e)
    return jnp.maximum(pre, 0.0) + t, jnp.maximum(-pre, 0.0) + t, jnp.where(pre >= 0.0, r, e * r)


def pair(a):
    return jnp.concatenate([a, a], 1)


def with_ones(v):
    return jnp.concatenate([v, jnp.ones_like(v)], 1)


def fold(q, keys, vals, w2, mrow, accl, state, sig, scale, allowed, full):
    scores = dot(q, keys, NT)
    if allowed is not None:
        scores = jnp.where(allowed, scores, -1e30)
    old = mrow[...]
    new = jnp.maximum(old, scores.max(-1, keepdims=True))
    mrow[...] = new
    c = scale * LOG2E
    weights = jnp.exp2((scores - new) * c).astype(BF16)
    values1 = with_ones(vals)
    accl[...] = accl[...] * jnp.exp2((old - new) * c) + dot(weights, values1)
    pre = dot(w2, pair(keys), NT)
    sp, sm, sig[...] = feature_parts(pre)
    feats = jnp.concatenate([sp, sm], 0)
    if full is not None:
        feats = jnp.where(full, feats, 0.0)
    state[...] += dot2(feats, values1)


def flat(ref, which):
    blocks, rows, head = ref.shape[0], ref.shape[2], ref.shape[3]
    return ref[:, which].reshape(blocks * rows, head)


def place(ny):
    me = lax.axis_index("ctx")
    return me // (ny * CORES), (me // CORES) % ny, me % CORES


def own_plane(ny, scale, q_ref, same_ref, other_ref, wk_ref, m_ref, accl_ref, state_ref, sig_ref):
    _, y, core = place(ny)
    rows = same_ref.shape[2]
    keys_n = ny * rows
    q = q_ref[...]
    w2 = jnp.concatenate(halves(wk_ref[...].T), 1)
    m_ref[...] = jnp.full(m_ref.shape, -1e30, F32)
    accl_ref[...] = jnp.zeros_like(accl_ref)
    state_ref[...] = jnp.zeros_like(state_ref)
    per = q.shape[0] // rows
    col = lax.broadcasted_iota(jnp.int32, (q.shape[0], keys_n), 1)
    row = lax.broadcasted_iota(jnp.int32, (q.shape[0], keys_n), 0) // per
    key = lax.broadcasted_iota(jnp.int32, (1, keys_n), 1)
    fold(
        q, flat(same_ref, 0), flat(same_ref, 1), w2, m_ref, accl_ref, state_ref, sig_ref.at[0], scale,
        col <= row + y * rows, key < y * rows,
    )
    fold(
        q, flat(other_ref, 0), flat(other_ref, 1), w2, m_ref, accl_ref, state_ref, sig_ref.at[1], scale,
        col < (y + core) * rows, key < (y + core) * rows,
    )


def finish(
    ny, shifts, scale, count,
    q_ref, same_ref, other_ref, *rest,
):
    got = rest[: 2 * shifts]
    (wq_ref, wk_ref, m_in, accl_in, state_in, sig_own, out_ref, grad_ref, m_ref, accl_ref, state_ref, sig_ref) = rest[2 * shifts :]
    x, y, core = place(ny)
    rows, head = same_ref.shape[2], same_ref.shape[3]
    keys_n = ny * rows
    q = q_ref[...]
    per = q.shape[0] // rows
    w2 = jnp.concatenate(halves(wk_ref[...].T), 1)
    m_ref[...] = m_in[...]
    accl_ref[...] = accl_in[...]
    state_ref[...] = state_in[...]
    for s in range(1, shifts + 1):

        @pl.when(x >= s)
        def _(s=s):
            for half in range(2):
                ref = got[2 * (s - 1) + half]
                fold(
                    q, flat(ref, 0), flat(ref, 1), w2, m_ref, accl_ref, state_ref,
                    sig_ref.at[2 * (s - 1) + half], scale, None, None,
                )

    accl = accl_ref[...]
    targets = (accl[:, :head] / accl[:, head:]).astype(BF16).astype(F32)
    wq = wq_ref[...]
    wqh, wql = halves(wq)
    sp, sm, _ = feature_parts(dot(q, wqh) + dot(q, wql))
    fq = jnp.concatenate([sp, sm], 1)
    wqt = jnp.concatenate(halves(wq.T), 1)
    sp, sm, sig_q = feature_parts(dot(wqt, pair(q), NT))
    fq_t = jnp.concatenate([sp, sm], 0)
    kd, vd = same_ref[y, 0], same_ref[y, 1]
    sp, sm, sig_d = feature_parts(dot(w2, pair(kd), NT))
    fk_t = jnp.concatenate([sp, sm], 0)
    causal = lax.broadcasted_iota(jnp.int32, (q.shape[0], rows), 1) <= (
        lax.broadcasted_iota(jnp.int32, (q.shape[0], rows), 0) // per
    )
    attn = jnp.where(causal, dot3(fq, fk_t), 0.0)
    state = state_ref[...]
    numden = dot3(fq, state) + dot2(attn, with_ones(vd))
    den = numden[:, head:]
    outs = numden[:, :head] / den
    out_ref[...] = outs.astype(BF16)
    diff = outs - targets
    loss = jnp.sum(diff * diff) / count
    grad_out = diff * (2.0 / count)
    d_num = grad_out / den
    d_den = -jnp.sum(grad_out * outs, -1, keepdims=True) / den
    back = dot3(fq_t, jnp.concatenate([d_num, d_den], 1))
    d_attn = jnp.where(causal, dot2(d_num, vd, NT) + d_den[:, :rows], 0.0)
    lane = lax.broadcasted_iota(jnp.int32, d_den.shape, 1)
    d_aug = jnp.concatenate([d_num, jnp.where(lane == 0, d_den, 0.0)], 1)
    d_fq = dot3(state, d_aug, NT) + dot3(fk_t, d_attn, NT)
    d_pre = d_fq[:head] * sig_q - d_fq[head:] * (1.0 - sig_q)
    grad_q = dot2(d_pre, q)
    d_fk = dot3(fq_t, d_attn)
    d_pre = d_fk[:head] * sig_d - d_fk[head:] * (1.0 - sig_d)
    grad_k = dot2(d_pre, kd)
    both = jnp.concatenate([back[:head, :head] + back[head:, :head], back[head:, :head]], 0)
    both_n = back[:head, head : head + 1] + back[head:, head : head + 1]
    low_n = back[head:, head : head + 1]
    both2 = jnp.concatenate(halves(both), 1)

    def key_grad(keys, vals, sig, full):
        z = dot(both2, pair(vals), NT)
        d_pre = sig * (z[:head] + both_n) - (z[head:] + low_n)
        if full is not None:
            d_pre = jnp.where(full, d_pre, 0.0)
        return dot2(d_pre, keys)

    key = lax.broadcasted_iota(jnp.int32, (1, keys_n), 1)
    grad_k += key_grad(flat(same_ref, 0), flat(same_ref, 1), sig_own[0], key < y * rows)
    grad_k += key_grad(flat(other_ref, 0), flat(other_ref, 1), sig_own[1], key < (y + core) * rows)
    state_ref[:, :head] = jnp.concatenate([grad_q, grad_k], 0)
    for s in range(1, shifts + 1):

        @pl.when(x >= s)
        def _(s=s):
            for half in range(2):
                ref = got[2 * (s - 1) + half]
                state_ref[head:, :head] += key_grad(
                    flat(ref, 0), flat(ref, 1), sig_ref[2 * (s - 1) + half], None
                )

    n = grad_ref.shape[0]
    grads = jnp.concatenate([state_ref[:head, :head].T, state_ref[head:, :head].T], 0)
    parts = 2 * head // n
    for r in range(parts):
        grad_ref[:, r, :] = grads[r * n : (r + 1) * n]
    grad_ref[:, parts, :] = jnp.full((n, head), loss, F32)
    for r in range(parts + 1, grad_ref.shape[1]):
        grad_ref[:, r, :] = jnp.zeros((n, head), F32)


VMEM = pl.BlockSpec(memory_space=pltpu.VMEM)
PARAMS = pltpu.CompilerParams(vmem_limit_bytes=56 * 1024 * 1024)


def spread(a, axis, groups=None, ways=None):
    ways = ways or lax.axis_size(axis)
    copies = jnp.broadcast_to(a[None], (ways, *a.shape))
    return lax.all_to_all(copies, axis, 0, 0, tiled=True, axis_index_groups=groups)


def shards(nx, ny, queries, keys, values, w_query, w_key):
    rows, groups, per, head = queries.shape
    n_ctx, n_kvh = lax.axis_size("ctx"), lax.axis_size("kvh")
    scale = head**-0.5
    count = float(rows * n_ctx * groups * n_kvh * per)
    at = lambda x, y, c: (x * ny + y) * CORES + c
    every = [(x, y, c) for x in range(nx) for y in range(ny) for c in range(CORES)]
    y_groups = [[at(x, y, c) for y in range(ny)] for x in range(nx) for c in range(CORES)]
    swap = [(at(x, y, c), at(x, y, 1 - c)) for x, y, c in every]
    q = queries.reshape(rows * per, head)
    kv = jnp.stack([keys.reshape(rows, head), values.reshape(rows, head)])
    same = spread(kv, "ctx", y_groups, ny)
    got = [
        lax.ppermute(same, "ctx", [(at(x, y, c), at(x + s, y, c)) for x, y, c in every if x + s < nx])
        for s in range(1, nx)
    ]
    other = lax.ppermute(same, "ctx", swap)
    keys_n = ny * rows
    carry = (
        jax.ShapeDtypeStruct((rows * per, 1), F32),
        jax.ShapeDtypeStruct((rows * per, 2 * head), F32),
        jax.ShapeDtypeStruct((2 * head, 2 * head), F32),
        jax.ShapeDtypeStruct((2, head, keys_n), F32),
    )
    carried = pl.pallas_call(
        functools.partial(own_plane, ny, scale),
        out_shape=carry,
        in_specs=[VMEM] * 4,
        out_specs=[VMEM] * 4,
        compiler_params=PARAMS,
        cost_estimate=pl.CostEstimate(flops=3_000_000_000, bytes_accessed=3_000_000, transcendentals=1_000_000),
        name="own_plane",
    )(q, same, other, w_key)
    both = []
    for a in got:
        both += [a, lax.ppermute(a, "ctx", swap)]
    out, grads = pl.pallas_call(
        functools.partial(finish, ny, nx - 1, scale, count),
        out_shape=(
            jax.ShapeDtypeStruct((rows * per, head), BF16),
            jax.ShapeDtypeStruct((n_ctx, 8, head), F32),
        ),
        in_specs=[VMEM] * (9 + len(both)),
        out_specs=[VMEM] * 2,
        scratch_shapes=[
            pltpu.VMEM((rows * per, 1), F32),
            pltpu.VMEM((rows * per, 2 * head), F32),
            pltpu.VMEM((2 * head, 2 * head), F32),
            pltpu.VMEM((2 * (nx - 1), head, keys_n), F32),
        ],
        compiler_params=PARAMS,
        cost_estimate=pl.CostEstimate(flops=9_000_000_000, bytes_accessed=6_000_000, transcendentals=3_000_000),
        name="finish",
    )(q, same, other, *both, w_query, w_key, *carried)
    mine = lax.all_to_all(grads, "ctx", 0, 0, tiled=True).sum(0)
    mine = spread(mine, "kvh").sum(0)
    summed = spread(mine, "ctx")
    parts = 2 * head // n_ctx
    g = summed[:, :parts].transpose(1, 0, 2).reshape(2, head, head)
    return out.reshape(queries.shape), g[0], g[1], summed[0, parts, 0]


def solution(mesh):
    n_ctx = mesh.shape["ctx"]
    ny = min(8, n_ctx // CORES)
    nx = n_ctx // (CORES * ny)
    placed = (P("ctx", "kvh", None, None), P("ctx", "kvh", None), P("ctx", "kvh", None), P(), P())
    return jax.shard_map(
        functools.partial(shards, nx, ny),
        mesh=mesh,
        in_specs=placed,
        out_specs=(P("ctx", "kvh", None, None), P(), P(), P()),
        check_vma=False,
    )
```

time: 745 us -> 141 us (0.19)
  waiting for transfers between devices: 408 us -> 12.4 us
  blocking collectives: 233 us -> 88.6 us
  other arithmetic: 60.4 us -> 0.86 us
  starting transfers between devices: 0.2 us -> 22.8 us
  between operations: 14.7 us -> 0.83 us
  matrix products: 12.6 us -> 0 us
  Pallas kernels: 0 us -> 12 us
    all_gather x4 -> x0, waiting for transfers between devices: 247 us -> none  [the longest x1 83.9 us: entering(): lax.all_gather(a.astype(kind), axis)]
    psum x1 -> x0, waiting for transfers between devices: 161 us -> none  [shards(): lax.psum((grad_query, grad_key, loss_part), ('ctx', 'kvh'))]
    all_gather x2 -> x0, blocking collectives: 135 us -> none  [the longest x1 91.6 us: entering_2(): lax.all_gather(part.astype(kind), axis)]
    psum x1 -> x0, blocking collectives: 97.6 us -> none  [shards(): lax.psum((grad_query, grad_key, loss_part), ('ctx', 'kvh'))]
    all_to_all x0 -> x4, blocking collectives: none -> 88.6 us  [the longest x3 58.2 us: spread(): lax.all_to_all(copies, axis, 0, 0, tiled=True, axis_index_groups=groups)]
    select_n x130 -> x0, other arithmetic: 59.1 us -> none  [the longest x128 58.9 us: step(): return jax.tree.map(lambda a, b: jnp.where(reached, a, b), new, before)]
    ppermute x0 -> x7, starting transfers between devices: none -> 22.8 us  [the longest x3 9.46 us: shards(): lax.ppermute(same, 'ctx', [(at(x, y, c), at(x + s, y, c)) for x, y, c in...]
    dot_general x18 -> x0, matrix products: 12.6 us -> none  [the longest x2 2.21 us: features(): jnp.einsum('...h,he->...e', rows.astype(jnp.float32), weight, precision=H...]
  transfers between devices with their start and end apart: 5 -> 7, of which waited for: 5 -> 1; matrix products, arithmetic and copies ran while one was open for 2% -> 0% of each run, Pallas kernels for 0% -> 4%
where the time goes in v1:
time: 141 us
  blocking collectives  88.6 us (63%)
  starting transfers between devices  22.8 us (16%)
  waiting for transfers between devices  12.4 us (9%)
  Pallas kernels  12 us (9%)
  local copies, waits for them, and re-layouts  3.23 us (2%)
    all_to_all x3, blocking collectives, spread(): lax.all_to_all(copies, axis, 0, 0, tiled=True, axis_index_groups=groups)  58.2 us
    all_to_all x1, blocking collectives, shards(): mine = lax.all_to_all(grads, 'ctx', 0, 0, tiled=True).sum(0)  30.5 us
    ppermute x3, waiting for transfers between devices, shards(): lax.ppermute(same, 'ctx', [(at(x, y, c), at(x + s, y, c)) for x, y, c in...  12.4 us
    ppermute x3, starting transfers between devices, shards(): lax.ppermute(same, 'ctx', [(at(x, y, c), at(x + s, y, c)) for x, y, c in...  9.46 us
    ppermute x3, starting transfers between devices, shards(): both += [a, lax.ppermute(a, 'ctx', swap)]  8.38 us
    pallas_call x1, Pallas kernels, shards(): pl.pallas_call(functools.partial(finish, ny, nx - 1, scale, count), out_s...  6.94 us
    pallas_call x1, Pallas kernels, shards(): pl.pallas_call(functools.partial(own_plane, ny, scale), out_shape=carry,...  5.09 us
    ppermute x1, starting transfers between devices, shards(): other = lax.ppermute(same, 'ctx', swap)  4.92 us
  transfers between devices with their start and end apart: 7, of which 1 were waited for; matrix products, arithmetic and copies ran while one was open for 0% of the time, Pallas kernels for 4%

profile of v1, /device:TPU:1, one launch (start us, length us, event | category | flops | bytes accessed | tf_op | source)
XLA Modules:
  0.0 140.8 jit_solution(13980782042936861575)
XLA Ops:
  0.6 0.8 pad_maximum_fusion
  1.4 0.1 broadcast_in_dim.6
  1.5 22.2 %all_to_all.20.same_ref = bf16[8,2,128,128]{3,2,1,0:T(8,128)(2,1)S(1)} all-to-all(bf16[8,2,128,128]{3,2,1,0:T(8,128)(2,1)S(1)} %broadcast_in_dim.6), channel_id=1, replica_groups={{0,16,32,48,64,80,96,112},{8,24,40,56,72,88,104,120},{128,144,160,176,1..., dimensions={0} | all-to-all | bytes 1048576 | tf_op jit(solution)/shard_map/all_to_all | solution.py:213
  23.7 5.7 %collective-permute-start.5 = (bf16[8,2,128,128]{3,2,1,0:T(8,128)(2,1)S(1)}, bf16[8,2,128,128]{3,2,1,0:T(8,128)(2,1)S(1)}, u32[]{:S(2)}, u32[]{:S(2)}) collective-permute-start(bf16[8,2,128,128]{3,2,1,0:T(8,128)(2,1)S(1)} %all_to_all.20.same_ref), channel_id=1, source_target_pairs={{0,384},{8,392},{16,400},{24,408},{32,416},{40,424},{48,432},{56,4... | collective-permute-start | bytes 1572872 | tf_op jit(solution)/shard_map/ppermute | solution.py:229
  29.4 1.3 collective-permute-start.3
  30.7 2.5 %collective-permute-start.1 = (bf16[8,2,128,128]{3,2,1,0:T(8,128)(2,1)S(1)}, bf16[8,2,128,128]{3,2,1,0:T(8,128)(2,1)S(1)}, u32[]{:S(2)}, u32[]{:S(2)}) collective-permute-start(bf16[8,2,128,128]{3,2,1,0:T(8,128)(2,1)S(1)} %all_to_all.20.same_ref), channel_id=1, source_target_pairs={{0,128},{8,136},{16,144},{24,152},{32,160},{40,168},{48,176},{56,1... | collective-permute-start | bytes 1572872 | tf_op jit(solution)/shard_map/ppermute | solution.py:229
  33.2 4.9 %collective-permute-start = (bf16[8,2,128,128]{3,2,1,0:T(8,128)(2,1)S(1)}, bf16[8,2,128,128]{3,2,1,0:T(8,128)(2,1)S(1)}, u32[]{:S(2)}, u32[]{:S(2)}) collective-permute-start(bf16[8,2,128,128]{3,2,1,0:T(8,128)(2,1)S(1)} %all_to_all.20.same_ref), channel_id=1, source_target_pairs={{0,8},{8,0},{16,24},{24,16},{32,40},{40,32},{48,56},{56,48},{64,72... | collective-permute-start | bytes 1572872 | tf_op jit(solution)/shard_map/ppermute | solution.py:232
  38.1 12.4 %collective-permute-done.5.rest_4_ = bf16[8,2,128,128]{3,2,1,0:T(8,128)(2,1)S(1)} collective-permute-done((bf16[8,2,128,128]{3,2,1,0:T(8,128)(2,1)S(1)}, bf16[8,2,128,128]{3,2,1,0:T(8,128)(2,1)S(1)}, u32[]{:S(2)}, u32[]{:S(2)}) %collective-permute-start.5) | collective-permute-done | bytes 524320 | tf_op jit(solution)/shard_map/ppermute | solution.py:229
  50.5 4.1 %collective-permute-start.6 = (bf16[8,2,128,128]{3,2,1,0:T(8,128)(2,1)S(1)}, bf16[8,2,128,128]{3,2,1,0:T(8,128)(2,1)S(1)}, u32[]{:S(2)}, u32[]{:S(2)}) collective-permute-start(bf16[8,2,128,128]{3,2,1,0:T(8,128)(2,1)S(1)} %collective-permute-done.5.rest_4_), channel_id=1, source_target_pairs={{0,8},{8,0},{16,24},{24,16},{32,40},{40,32},{48,56},{56,48},{64,72... | collective-permute-start | bytes 1572872 | tf_op jit(solution)/shard_map/ppermute | solution.py:251
  54.6 0.0 collective-permute-done.3.rest_2_
  54.6 1.9 %collective-permute-start.4 = (bf16[8,2,128,128]{3,2,1,0:T(8,128)(2,1)S(1)}, bf16[8,2,128,128]{3,2,1,0:T(8,128)(2,1)S(1)}, u32[]{:S(2)}, u32[]{:S(2)}) collective-permute-start(bf16[8,2,128,128]{3,2,1,0:T(8,128)(2,1)S(1)} %collective-permute-done.3.rest_2_), channel_id=1, source_target_pairs={{0,8},{8,0},{16,24},{24,16},{32,40},{40,32},{48,56},{56,48},{64,72... | collective-permute-start | bytes 1572872 | tf_op jit(solution)/shard_map/ppermute | solution.py:251
  56.6 2.4 %collective-permute-start.2 = (bf16[8,2,128,128]{3,2,1,0:T(8,128)(2,1)S(1)}, bf16[8,2,128,128]{3,2,1,0:T(8,128)(2,1)S(1)}, u32[]{:S(2)}, u32[]{:S(2)}) collective-permute-start(bf16[8,2,128,128]{3,2,1,0:T(8,128)(2,1)S(1)} %collective-permute-done.1.rest_0_), channel_id=1, source_target_pairs={{0,8},{8,0},{16,24},{24,16},{32,40},{40,32},{48,56},{56,48},{64,72... | collective-permute-start | bytes 1572872 | tf_op jit(solution)/shard_map/ppermute | solution.py:251
  59.0 0.8 copy-done.4
  59.8 5.1 %own_plane.1 = (f32[256,1]{1,0:T(8,128)}, f32[256,256]{1,0:T(8,128)}, f32[256,256]{1,0:T(8,128)}, f32[2,128,1024]{2,1,0:T(8,128)}) custom-call(bf16[256,128]{1,0:T(8,128)(2,1)} %bitcast.17, bf16[8,2,128,128]{3,2,1,0:T(8,128)(2,1)} %copy-done, bf16[8,2,128,128]{3,2,1,0:T(8,128)(2,1)} %copy-done.4, f32[128,128]{1,0:T(8,128)} %rest_7_.1), custom_call_target="tpu_custom_call" | custom-call | flops 3000000000 | bytes 3000000 | tf_op jit(solution)/shard_map/own_plane/pallas_call | solution.py:240
  65.0 0.7 copy-done.5
  65.7 0.2 copy-done.6
  65.9 0.2 copy-done.7
  66.1 6.9 %finish.1 = (bf16[256,128]{1,0:T(8,128)(2,1)}, f32[64,8,128]{2,1,0:T(8,128)}) custom-call(bf16[256,128]{1,0:T(8,128)(2,1)} %bitcast.18, bf16[8,2,128,128]{3,2,1,0:T(8,128)(2,1)} %copy-done, bf16[8,2,128,128]{3,2,1,0:T(8,128)(2,1)} %copy-done.4, bf16[8,2,128,128]{3,2,1,0:T(8,128)(2,1)} %copy-done.3, bf16[8,2,128,128]{3,2,1,0:T(8,128)(2,1)} %copy-done.7, ...), custom_call_target="tpu_custom_call" | custom-call | flops 8999999488 | bytes 6000000 | tf_op jit(solution)/shard_map/finish/pallas_call | solution.py:252
  73.0 30.5 %all_to_all.21 = f32[64,8,128]{2,1,0:T(8,128)S(1)} all-to-all(f32[64,8,128]{2,1,0:T(8,128)} %get-tuple-element.15), channel_id=1, replica_groups=mesh['ctx'=64,'kvh'=8] {'ctx'}, dimensions={0} | all-to-all | bytes 524288 | tf_op jit(solution)/shard_map/all_to_all | solution.py:270
  103.5 0.1 reduce_sum.18
  103.6 16.7 %all_to_all.22 = f32[8,8,128]{2,1,0:T(8,128)S(1)} all-to-all(f32[8,8,128]{2,1,0:T(8,128)S(1)} %broadcast_in_dim.7), channel_id=1, replica_groups=mesh['ctx'=64,'kvh'=8] {'kvh'}, dimensions={0} | all-to-all | bytes 65536 | tf_op jit(solution)/shard_map/all_to_all | solution.py:213
  120.3 19.3 %all_to_all.23 = f32[64,8,128]{2,1,0:T(8,128)S(1)} all-to-all(f32[64,8,128]{2,1,0:T(8,128)S(1)} %broadcast_in_dim.8), channel_id=1, replica_groups=mesh['ctx'=64,'kvh'=8] {'ctx'}, dimensions={0} | all-to-all | bytes 524288 | tf_op jit(solution)/shard_map/all_to_all | solution.py:213
  139.6 0.7 fusion
  140.3 0.5 slice.21
  (22 shorter events, 0.1 us)
Async XLA Ops:
  23.7 35.3 %copy-start = (bf16[8,2,128,128]{3,2,1,0:T(8,128)(2,1)}, bf16[8,2,128,128]{3,2,1,0:T(8,128)(2,1)S(1)}, u32[]{:S(2)}) copy-start(bf16[8,2,128,128]{3,2,1,0:T(8,128)(2,1)S(1)} %all_to_all.20.same_ref) | copy-start | bytes 1572868
  23.7 26.8 %collective-permute-start.5 = (bf16[8,2,128,128]{3,2,1,0:T(8,128)(2,1)S(1)}, bf16[8,2,128,128]{3,2,1,0:T(8,128)(2,1)S(1)}, u32[]{:S(2)}, u32[]{:S(2)}) collective-permute-start(bf16[8,2,128,128]{3,2,1,0:T(8,128)(2,1)S(1)} %all_to_all.20.same_ref), channel_id=1, source_target_pairs={{0,384},{8,392},{16,400},{24,408},{32,416},{40,424},{48,432},{56,4... | collective-permute-start | bytes 1572872 | tf_op jit(solution)/shard_map/ppermute | solution.py:229
  29.4 25.2 %collective-permute-start.3 = (bf16[8,2,128,128]{3,2,1,0:T(8,128)(2,1)S(1)}, bf16[8,2,128,128]{3,2,1,0:T(8,128)(2,1)S(1)}, u32[]{:S(2)}, u32[]{:S(2)}) collective-permute-start(bf16[8,2,128,128]{3,2,1,0:T(8,128)(2,1)S(1)} %all_to_all.20.same_ref), channel_id=1, source_target_pairs={{0,256},{8,264},{16,272},{24,280},{32,288},{40,296},{48,304},{56,3... | collective-permute-start | bytes 1572872 | tf_op jit(solution)/shard_map/ppermute | solution.py:229
  30.7 25.9 %collective-permute-start.1 = (bf16[8,2,128,128]{3,2,1,0:T(8,128)(2,1)S(1)}, bf16[8,2,128,128]{3,2,1,0:T(8,128)(2,1)S(1)}, u32[]{:S(2)}, u32[]{:S(2)}) collective-permute-start(bf16[8,2,128,128]{3,2,1,0:T(8,128)(2,1)S(1)} %all_to_all.20.same_ref), channel_id=1, source_target_pairs={{0,128},{8,136},{16,144},{24,152},{32,160},{40,168},{48,176},{56,1... | collective-permute-start | bytes 1572872 | tf_op jit(solution)/shard_map/ppermute | solution.py:229
  33.2 25.8 %collective-permute-start = (bf16[8,2,128,128]{3,2,1,0:T(8,128)(2,1)S(1)}, bf16[8,2,128,128]{3,2,1,0:T(8,128)(2,1)S(1)}, u32[]{:S(2)}, u32[]{:S(2)}) collective-permute-start(bf16[8,2,128,128]{3,2,1,0:T(8,128)(2,1)S(1)} %all_to_all.20.same_ref), channel_id=1, source_target_pairs={{0,8},{8,0},{16,24},{24,16},{32,40},{40,32},{48,56},{56,48},{64,72... | collective-permute-start | bytes 1572872 | tf_op jit(solution)/shard_map/ppermute | solution.py:232
  50.5 14.4 %copy-start.1 = (bf16[8,2,128,128]{3,2,1,0:T(8,128)(2,1)}, bf16[8,2,128,128]{3,2,1,0:T(8,128)(2,1)S(1)}, u32[]{:S(2)}) copy-start(bf16[8,2,128,128]{3,2,1,0:T(8,128)(2,1)S(1)} %collective-permute-done.5.rest_4_) | copy-start | bytes 1572868
  50.5 14.4 %collective-permute-start.6 = (bf16[8,2,128,128]{3,2,1,0:T(8,128)(2,1)S(1)}, bf16[8,2,128,128]{3,2,1,0:T(8,128)(2,1)S(1)}, u32[]{:S(2)}, u32[]{:S(2)}) collective-permute-start(bf16[8,2,128,128]{3,2,1,0:T(8,128)(2,1)S(1)} %collective-permute-done.5.rest_4_), channel_id=1, source_target_pairs={{0,8},{8,0},{16,24},{24,16},{32,40},{40,32},{48,56},{56,48},{64,72... | collective-permute-start | bytes 1572872 | tf_op jit(solution)/shard_map/ppermute | solution.py:251
  54.6 10.3 %copy-start.2 = (bf16[8,2,128,128]{3,2,1,0:T(8,128)(2,1)}, bf16[8,2,128,128]{3,2,1,0:T(8,128)(2,1)S(1)}, u32[]{:S(2)}) copy-start(bf16[8,2,128,128]{3,2,1,0:T(8,128)(2,1)S(1)} %collective-permute-done.3.rest_2_) | copy-start | bytes 1572868
  54.6 10.3 %collective-permute-start.4 = (bf16[8,2,128,128]{3,2,1,0:T(8,128)(2,1)S(1)}, bf16[8,2,128,128]{3,2,1,0:T(8,128)(2,1)S(1)}, u32[]{:S(2)}, u32[]{:S(2)}) collective-permute-start(bf16[8,2,128,128]{3,2,1,0:T(8,128)(2,1)S(1)} %collective-permute-done.3.rest_2_), channel_id=1, source_target_pairs={{0,8},{8,0},{16,24},{24,16},{32,40},{40,32},{48,56},{56,48},{64,72... | collective-permute-start | bytes 1572872 | tf_op jit(solution)/shard_map/ppermute | solution.py:251
  56.6 8.3 %copy-start.3 = (bf16[8,2,128,128]{3,2,1,0:T(8,128)(2,1)}, bf16[8,2,128,128]{3,2,1,0:T(8,128)(2,1)S(1)}, u32[]{:S(2)}) copy-start(bf16[8,2,128,128]{3,2,1,0:T(8,128)(2,1)S(1)} %collective-permute-done.1.rest_0_) | copy-start | bytes 1572868
  56.6 8.4 %collective-permute-start.2 = (bf16[8,2,128,128]{3,2,1,0:T(8,128)(2,1)S(1)}, bf16[8,2,128,128]{3,2,1,0:T(8,128)(2,1)S(1)}, u32[]{:S(2)}, u32[]{:S(2)}) collective-permute-start(bf16[8,2,128,128]{3,2,1,0:T(8,128)(2,1)S(1)} %collective-permute-done.1.rest_0_), channel_id=1, source_target_pairs={{0,8},{8,0},{16,24},{24,16},{32,40},{40,32},{48,56},{56,48},{64,72... | collective-permute-start | bytes 1572872 | tf_op jit(solution)/shard_map/ppermute | solution.py:251
  59.0 0.8 copy-start.4
  64.9 0.8 copy-start.5
  64.9 1.0 copy-start.6
  65.0 1.1 copy-start.7

commit v2 on v1

--- a/solution.py
+++ b/solution.py
@@ -82,7 +82,11 @@
     return me // (ny * CORES), (me // CORES) % ny, me % CORES
 
 
-def own_plane(ny, scale, q_ref, same_ref, other_ref, wk_ref, m_ref, accl_ref, state_ref, sig_ref):
+def own_plane(
+    ny, scale,
+    q_ref, same_ref, other_ref, wq_ref, wk_ref,
+    m_ref, accl_ref, state_ref, sig_ref, fq_ref, fqt_ref, sigq_ref, fkd_ref, sigd_ref, near_ref,
+):
     _, y, core = place(ny)
     rows = same_ref.shape[2]
     keys_n = ny * rows
@@ -103,19 +107,37 @@
         q, flat(other_ref, 0), flat(other_ref, 1), w2, m_ref, accl_ref, state_ref, sig_ref.at[1], scale,
         col < (y + core) * rows, key < (y + core) * rows,
     )
-
-
-def finish(
-    ny, shifts, scale, count,
-    q_ref, same_ref, other_ref, *rest,
-):
+    wq = wq_ref[...]
+    wqt = jnp.concatenate(halves(wq.T), 1)
+    sp, sm, sigq_ref[...] = feature_parts(dot(wqt, pair(q), NT))
+    fq_t = jnp.concatenate([sp, sm], 0)
+    fqt_ref[...] = fq_t
+    fq = fq_t.T
+    fq_ref[...] = fq
+    kd, vd = same_ref[y, 0], same_ref[y, 1]
+    sp, sm, sigd_ref[...] = feature_parts(dot(w2, pair(kd), NT))
+    fk_t = jnp.concatenate([sp, sm], 0)
+    fkd_ref[...] = fk_t
+    attn = jnp.where(diagonal(q.shape[0], rows), dot3(fq, fk_t), 0.0)
+    near_ref[...] = dot2(attn, with_ones(vd))
+
+
+def diagonal(n, rows):
+    return lax.broadcasted_iota(jnp.int32, (n, rows), 1) <= (
+        lax.broadcasted_iota(jnp.int32, (n, rows), 0) // (n // rows)
+    )
+
+
+def finish(ny, shifts, scale, count, q_ref, same_ref, other_ref, *rest):
     got = rest[: 2 * shifts]
-    (wq_ref, wk_ref, m_in, accl_in, state_in, sig_own, out_ref, grad_ref, m_ref, accl_ref, state_ref, sig_ref) = rest[2 * shifts :]
+    (
+        wk_ref, m_in, accl_in, state_in, sig_own, fq_ref, fqt_ref, sigq_ref, fkd_ref, sigd_ref, near_ref,
+        out_ref, grad_ref, m_ref, accl_ref, state_ref, sig_ref, grads_ref,
+    ) = rest[2 * shifts :]
     x, y, core = place(ny)
     rows, head = same_ref.shape[2], same_ref.shape[3]
     keys_n = ny * rows
     q = q_ref[...]
-    per = q.shape[0] // rows
     w2 = jnp.concatenate(halves(wk_ref[...].T), 1)
     m_ref[...] = m_in[...]
     accl_ref[...] = accl_in[...]
@@ -133,22 +155,10 @@
 
     accl = accl_ref[...]
     targets = (accl[:, :head] / accl[:, head:]).astype(BF16).astype(F32)
-    wq = wq_ref[...]
-    wqh, wql = halves(wq)
-    sp, sm, _ = feature_parts(dot(q, wqh) + dot(q, wql))
-    fq = jnp.concatenate([sp, sm], 1)
-    wqt = jnp.concatenate(halves(wq.T), 1)
-    sp, sm, sig_q = feature_parts(dot(wqt, pair(q), NT))
-    fq_t = jnp.concatenate([sp, sm], 0)
     kd, vd = same_ref[y, 0], same_ref[y, 1]
-    sp, sm, sig_d = feature_parts(dot(w2, pair(kd), NT))
-    fk_t = jnp.concatenate([sp, sm], 0)
-    causal = lax.broadcasted_iota(jnp.int32, (q.shape[0], rows), 1) <= (
-        lax.broadcasted_iota(jnp.int32, (q.shape[0], rows), 0) // per
-    )
-    attn = jnp.where(causal, dot3(fq, fk_t), 0.0)
+    fq_t, fk_t, sig_q, sig_d = fqt_ref[...], fkd_ref[...], sigq_ref[...], sigd_ref[...]
     state = state_ref[...]
-    numden = dot3(fq, state) + dot2(attn, with_ones(vd))
+    numden = dot3(fq_ref[...], state) + near_ref[...]
     den = numden[:, head:]
     outs = numden[:, :head] / den
     out_ref[...] = outs.astype(BF16)
@@ -158,7 +168,7 @@
     d_num = grad_out / den
     d_den = -jnp.sum(grad_out * outs, -1, keepdims=True) / den
     back = dot3(fq_t, jnp.concatenate([d_num, d_den], 1))
-    d_attn = jnp.where(causal, dot2(d_num, vd, NT) + d_den[:, :rows], 0.0)
+    d_attn = jnp.where(diagonal(q.shape[0], rows), dot2(d_num, vd, NT) + d_den[:, :rows], 0.0)
     lane = lax.broadcasted_iota(jnp.int32, d_den.shape, 1)
     d_aug = jnp.concatenate([d_num, jnp.where(lane == 0, d_den, 0.0)], 1)
     d_fq = dot3(state, d_aug, NT) + dot3(fk_t, d_attn, NT)
@@ -182,7 +192,7 @@
     key = lax.broadcasted_iota(jnp.int32, (1, keys_n), 1)
     grad_k += key_grad(flat(same_ref, 0), flat(same_ref, 1), sig_own[0], key < y * rows)
     grad_k += key_grad(flat(other_ref, 0), flat(other_ref, 1), sig_own[1], key < (y + core) * rows)
-    state_ref[:, :head] = jnp.concatenate([grad_q, grad_k], 0)
+    state_ref[head:, :head] = grad_k
     for s in range(1, shifts + 1):
 
         @pl.when(x >= s)
@@ -193,14 +203,13 @@
                     flat(ref, 0), flat(ref, 1), sig_ref[2 * (s - 1) + half], None
                 )
 
-    n = grad_ref.shape[0]
-    grads = jnp.concatenate([state_ref[:head, :head].T, state_ref[head:, :head].T], 0)
-    parts = 2 * head // n
+    grads_ref[:head] = grad_q.T
+    grads_ref[head:] = state_ref[head:, :head].T
+    chunks = grad_ref.shape[0] - 2 * head
+    parts = 2 * head // chunks
     for r in range(parts):
-        grad_ref[:, r, :] = grads[r * n : (r + 1) * n]
-    grad_ref[:, parts, :] = jnp.full((n, head), loss, F32)
-    for r in range(parts + 1, grad_ref.shape[1]):
-        grad_ref[:, r, :] = jnp.zeros((n, head), F32)
+        grad_ref[pl.ds(r, chunks, stride=parts + 1), :] = grads_ref[pl.ds(r, chunks, stride=parts), :]
+    grad_ref[pl.ds(parts, chunks, stride=parts + 1), :] = jnp.full((chunks, head), loss, F32)
 
 
 VMEM = pl.BlockSpec(memory_space=pltpu.VMEM)
@@ -230,49 +239,45 @@
         for s in range(1, nx)
     ]
     other = lax.ppermute(same, "ctx", swap)
-    keys_n = ny * rows
-    carry = (
-        jax.ShapeDtypeStruct((rows * per, 1), F32),
-        jax.ShapeDtypeStruct((rows * per, 2 * head), F32),
-        jax.ShapeDtypeStruct((2 * head, 2 * head), F32),
-        jax.ShapeDtypeStruct((2, head, keys_n), F32),
-    )
+    n, feats, keys_n = rows * per, 2 * head, ny * rows
+    f32 = lambda *shape: jax.ShapeDtypeStruct(shape, F32)
     carried = pl.pallas_call(
         functools.partial(own_plane, ny, scale),
-        out_shape=carry,
-        in_specs=[VMEM] * 4,
-        out_specs=[VMEM] * 4,
+        out_shape=(
+            f32(n, 1), f32(n, feats), f32(feats, feats), f32(2, head, keys_n),
+            f32(n, feats), f32(feats, n), f32(head, n), f32(feats, rows), f32(head, rows), f32(n, feats),
+        ),
+        in_specs=[VMEM] * 5,
+        out_specs=[VMEM] * 10,
         compiler_params=PARAMS,
         cost_estimate=pl.CostEstimate(flops=3_000_000_000, bytes_accessed=3_000_000, transcendentals=1_000_000),
         name="own_plane",
-    )(q, same, other, w_key)
+    )(q, same, other, w_query, w_key)
+    got, carried = lax.optimization_barrier((got, carried))
     both = []
     for a in got:
         both += [a, lax.ppermute(a, "ctx", swap)]
+    parts = feats // n_ctx
     out, grads = pl.pallas_call(
         functools.partial(finish, ny, nx - 1, scale, count),
-        out_shape=(
-            jax.ShapeDtypeStruct((rows * per, head), BF16),
-            jax.ShapeDtypeStruct((n_ctx, 8, head), F32),
-        ),
-        in_specs=[VMEM] * (9 + len(both)),
+        out_shape=(jax.ShapeDtypeStruct((n, head), BF16), f32(n_ctx * (parts + 1), head)),
+        in_specs=[VMEM] * (14 + len(both)),
         out_specs=[VMEM] * 2,
         scratch_shapes=[
-            pltpu.VMEM((rows * per, 1), F32),
-            pltpu.VMEM((rows * per, 2 * head), F32),
-            pltpu.VMEM((2 * head, 2 * head), F32),
+            pltpu.VMEM((n, 1), F32),
+            pltpu.VMEM((n, feats), F32),
+            pltpu.VMEM((feats, feats), F32),
             pltpu.VMEM((2 * (nx - 1), head, keys_n), F32),
+            pltpu.VMEM((feats, head), F32),
         ],
         compiler_params=PARAMS,
         cost_estimate=pl.CostEstimate(flops=9_000_000_000, bytes_accessed=6_000_000, transcendentals=3_000_000),
         name="finish",
-    )(q, same, other, *both, w_query, w_key, *carried)
-    mine = lax.all_to_all(grads, "ctx", 0, 0, tiled=True).sum(0)
+    )(q, same, other, *both, w_key, *carried)
+    mine = lax.all_to_all(grads.reshape(n_ctx, 1, -1), "ctx", 0, 0, tiled=True).sum(0)
     mine = spread(mine, "kvh").sum(0)
-    summed = spread(mine, "ctx")
-    parts = 2 * head // n_ctx
-    g = summed[:, :parts].transpose(1, 0, 2).reshape(2, head, head)
-    return out.reshape(queries.shape), g[0], g[1], summed[0, parts, 0]
+    g = spread(mine[:, : parts * head], "ctx").reshape(2, head, head)
+    return out.reshape(queries.shape), g[0], g[1], mine[0, parts * head]
 
 
 def solution(mesh):

time: 141 us -> 136 us (0.965)
  blocking collectives: 88.6 us -> 65.6 us
  waiting for transfers between devices: 12.4 us -> 25.5 us
  starting transfers between devices: 22.8 us -> 27.6 us
    all_to_all x3 -> x2, blocking collectives: 58.2 us -> 38.7 us  [spread(): lax.all_to_all(copies, axis, 0, 0, tiled=True, axis_index_groups=groups)]
    all_to_all x0 -> x1, waiting for transfers between devices: none -> 9.85 us  [spread(): lax.all_to_all(copies, axis, 0, 0, tiled=True, axis_index_groups=groups)]
    all_to_all x0 -> x1, starting transfers between devices: none -> 6.78 us  [spread(): lax.all_to_all(copies, axis, 0, 0, tiled=True, axis_index_groups=groups)]
    all_to_all x1, blocking collectives: 30.5 us -> 26.9 us  [shards(): lax.all_to_all(grads.reshape(n_ctx, 1, -1), 'ctx', 0, 0, tiled=True).sum(0)]
    ppermute x3, waiting for transfers between devices: 12.4 us -> 14.2 us  [shards(): lax.ppermute(same, 'ctx', [(at(x, y, c), at(x + s, y, c)) for x, y, c in...]
    ppermute x3, waiting for transfers between devices: 0.01 us -> 1.48 us  [shards(): both += [a, lax.ppermute(a, 'ctx', swap)]]
  transfers between devices with their start and end apart: 7 -> 8, of which waited for: 1 -> 4; matrix products, arithmetic and copies ran while one was open for 0% -> 0% of each run, Pallas kernels for 4% -> 4%
where the time goes in v2:
time: 136 us
  blocking collectives  65.6 us (48%)
  starting transfers between devices  27.6 us (20%)
  waiting for transfers between devices  25.5 us (19%)
  Pallas kernels  11.6 us (9%)
  local copies, waits for them, and re-layouts  3.6 us (3%)
    all_to_all x2, blocking collectives, spread(): lax.all_to_all(copies, axis, 0, 0, tiled=True, axis_index_groups=groups)  38.7 us
    all_to_all x1, blocking collectives, shards(): lax.all_to_all(grads.reshape(n_ctx, 1, -1), 'ctx', 0, 0, tiled=True).sum(0)  26.9 us
    ppermute x3, waiting for transfers between devices, shards(): lax.ppermute(same, 'ctx', [(at(x, y, c), at(x + s, y, c)) for x, y, c in...  14.2 us
    all_to_all x1, waiting for transfers between devices, spread(): lax.all_to_all(copies, axis, 0, 0, tiled=True, axis_index_groups=groups)  9.85 us
    ppermute x3, starting transfers between devices, shards(): lax.ppermute(same, 'ctx', [(at(x, y, c), at(x + s, y, c)) for x, y, c in...  8.22 us
    ppermute x3, starting transfers between devices, shards(): both += [a, lax.ppermute(a, 'ctx', swap)]  7.02 us
    all_to_all x1, starting transfers between devices, spread(): lax.all_to_all(copies, axis, 0, 0, tiled=True, axis_index_groups=groups)  6.78 us
    pallas_call x1, Pallas kernels, shards(): pl.pallas_call(functools.partial(finish, ny, nx - 1, scale, count), out_s...  6.56 us
  transfers between devices with their start and end apart: 8, of which 4 were waited for; matrix products, arithmetic and copies ran while one was open for 0% of the time, Pallas kernels for 4%

profile of v2, /device:TPU:1, one launch (start us, length us, event | category | flops | bytes accessed | tf_op | source)
XLA Modules:
  0.0 135.7 jit_solution(2178938271537256556)
XLA Ops:
  0.6 0.8 pad_maximum_fusion
  1.5 22.2 %all_to_all.20.same_ref = bf16[8,2,128,128]{3,2,1,0:T(8,128)(2,1)S(1)} all-to-all(bf16[8,2,128,128]{3,2,1,0:T(8,128)(2,1)S(1)} %broadcast_in_dim.8), channel_id=1, replica_groups={{0,16,32,48,64,80,96,112},{8,24,40,56,72,88,104,120},{128,144,160,176,1..., dimensions={0} | all-to-all | bytes 1048576 | tf_op jit(solution)/shard_map/all_to_all | solution.py:222
  23.7 5.6 %collective-permute-start = (bf16[8,2,128,128]{3,2,1,0:T(8,128)(2,1)S(1)}, bf16[8,2,128,128]{3,2,1,0:T(8,128)(2,1)S(1)}, u32[]{:S(2)}, u32[]{:S(2)}) collective-permute-start(bf16[8,2,128,128]{3,2,1,0:T(8,128)(2,1)S(1)} %all_to_all.20.same_ref), channel_id=1, source_target_pairs={{0,8},{8,0},{16,24},{24,16},{32,40},{40,32},{48,56},{56,48},{64,72... | collective-permute-start | bytes 1572872 | tf_op jit(solution)/shard_map/ppermute | solution.py:241
  29.3 4.4 %collective-permute-start.3 = (bf16[8,2,128,128]{3,2,1,0:T(8,128)(2,1)S(1)}, bf16[8,2,128,128]{3,2,1,0:T(8,128)(2,1)S(1)}, u32[]{:S(2)}, u32[]{:S(2)}) collective-permute-start(bf16[8,2,128,128]{3,2,1,0:T(8,128)(2,1)S(1)} %all_to_all.20.same_ref), channel_id=1, source_target_pairs={{0,384},{8,392},{16,400},{24,408},{32,416},{40,424},{48,432},{56,4... | collective-permute-start | bytes 1572872 | tf_op jit(solution)/shard_map/ppermute | solution.py:238
  33.7 1.3 collective-permute-start.2
  35.1 2.5 %collective-permute-start.1 = (bf16[8,2,128,128]{3,2,1,0:T(8,128)(2,1)S(1)}, bf16[8,2,128,128]{3,2,1,0:T(8,128)(2,1)S(1)}, u32[]{:S(2)}, u32[]{:S(2)}) collective-permute-start(bf16[8,2,128,128]{3,2,1,0:T(8,128)(2,1)S(1)} %all_to_all.20.same_ref), channel_id=1, source_target_pairs={{0,128},{8,136},{16,144},{24,152},{32,160},{40,168},{48,176},{56,1... | collective-permute-start | bytes 1572872 | tf_op jit(solution)/shard_map/ppermute | solution.py:238
  37.6 0.8 copy-done.1
  38.4 5.1 %own_plane.1 = (f32[256,1]{1,0:T(8,128)}, f32[256,256]{1,0:T(8,128)}, f32[256,256]{1,0:T(8,128)}, f32[2,128,1024]{2,1,0:T(8,128)}, f32[256,256]{1,0:T(8,128)}, /...) custom-call(bf16[256,128]{1,0:T(8,128)(2,1)} %bitcast.17, ...), custom_call_target="tpu_custom_call" | custom-call | flops 3000000000 | bytes 3000000 | tf_op jit(solution)/shard_map/own_plane/pallas_call | solution.py:244
  43.4 12.8 %collective-permute-done.3.rest_4_ = bf16[8,2,128,128]{3,2,1,0:T(8,128)(2,1)S(1)} collective-permute-done((bf16[8,2,128,128]{3,2,1,0:T(8,128)(2,1)S(1)}, bf16[8,2,128,128]{3,2,1,0:T(8,128)(2,1)S(1)}, u32[]{:S(2)}, u32[]{:S(2)}) %collective-permute-start.3) | collective-permute-done | bytes 524320 | tf_op jit(solution)/shard_map/ppermute | solution.py:238
  56.3 1.4 %collective-permute-done.1.rest_0_ = bf16[8,2,128,128]{3,2,1,0:T(8,128)(2,1)S(1)} collective-permute-done((bf16[8,2,128,128]{3,2,1,0:T(8,128)(2,1)S(1)}, bf16[8,2,128,128]{3,2,1,0:T(8,128)(2,1)S(1)}, u32[]{:S(2)}, u32[]{:S(2)}) %collective-permute-start.1) | collective-permute-done | bytes 524320 | tf_op jit(solution)/shard_map/ppermute | solution.py:238
  57.6 2.7 %collective-permute-start.4 = (bf16[8,2,128,128]{3,2,1,0:T(8,128)(2,1)S(1)}, bf16[8,2,128,128]{3,2,1,0:T(8,128)(2,1)S(1)}, u32[]{:S(2)}, u32[]{:S(2)}) collective-permute-start(bf16[8,2,128,128]{3,2,1,0:T(8,128)(2,1)S(1)} %collective-permute-done.1.rest_0_), channel_id=1, source_target_pairs={{0,8},{8,0},{16,24},{24,16},{32,40},{40,32},{48,56},{56,48},{64,72... | collective-permute-start | bytes 1572872 | tf_op jit(solution)/shard_map/ppermute | solution.py:259
  60.3 1.9 %collective-permute-start.5 = (bf16[8,2,128,128]{3,2,1,0:T(8,128)(2,1)S(1)}, bf16[8,2,128,128]{3,2,1,0:T(8,128)(2,1)S(1)}, u32[]{:S(2)}, u32[]{:S(2)}) collective-permute-start(bf16[8,2,128,128]{3,2,1,0:T(8,128)(2,1)S(1)} %collective-permute-done.2.rest_2_), channel_id=1, source_target_pairs={{0,8},{8,0},{16,24},{24,16},{32,40},{40,32},{48,56},{56,48},{64,72... | collective-permute-start | bytes 1572872 | tf_op jit(solution)/shard_map/ppermute | solution.py:259
  62.3 2.4 %collective-permute-start.6 = (bf16[8,2,128,128]{3,2,1,0:T(8,128)(2,1)S(1)}, bf16[8,2,128,128]{3,2,1,0:T(8,128)(2,1)S(1)}, u32[]{:S(2)}, u32[]{:S(2)}) collective-permute-start(bf16[8,2,128,128]{3,2,1,0:T(8,128)(2,1)S(1)} %collective-permute-done.3.rest_4_), channel_id=1, source_target_pairs={{0,8},{8,0},{16,24},{24,16},{32,40},{40,32},{48,56},{56,48},{64,72... | collective-permute-start | bytes 1572872 | tf_op jit(solution)/shard_map/ppermute | solution.py:259
  64.7 1.5 %collective-permute-done.6.rest_5_ = bf16[8,2,128,128]{3,2,1,0:T(8,128)(2,1)S(1)} collective-permute-done((bf16[8,2,128,128]{3,2,1,0:T(8,128)(2,1)S(1)}, bf16[8,2,128,128]{3,2,1,0:T(8,128)(2,1)S(1)}, u32[]{:S(2)}, u32[]{:S(2)}) %collective-permute-start.6) | collective-permute-done | bytes 524320 | tf_op jit(solution)/shard_map/ppermute | solution.py:259
  66.2 0.8 copy-done.7
  67.0 6.6 %finish.1 = (bf16[256,128]{1,0:T(8,128)(2,1)}, f32[320,128]{1,0:T(8,128)}) custom-call(bf16[256,128]{1,0:T(8,128)(2,1)} %bitcast.18, bf16[8,2,128,128]{3,2,1,0:T(8,128)(2,1)} %copy-done, bf16[8,2,128,128]{3,2,1,0:T(8,128)(2,1)} %copy-done.1, bf16[8,2,128,128]{3,2,1,0:T(8,128)(2,1)} %copy-done.4, bf16[8,2,128,128]{3,2,1,0:T(8,128)(2,1)} %copy-done.5, ...), custom_call_target="tpu_custom_call" | custom-call | flops 8999999488 | bytes 6000000 | tf_op jit(solution)/shard_map/finish/pallas_call | solution.py:261
  73.6 26.9 %all_to_all.21 = f32[64,1,640]{2,1,0:T(1,128)S(1)} all-to-all(f32[64,1,640]{2,1,0:T(1,128)} %bitcast.11), channel_id=1, replica_groups=mesh['ctx'=64,'kvh'=8] {'ctx'}, dimensions={0} | all-to-all | bytes 327680 | tf_op jit(solution)/shard_map/all_to_all | solution.py:277
  100.5 0.1 reduce_sum.20
  100.6 16.5 %all_to_all.22 = f32[8,1,640]{2,1,0:T(1,128)S(1)} all-to-all(f32[8,1,640]{2,1,0:T(1,128)S(1)} %broadcast_in_dim.9), channel_id=1, replica_groups=mesh['ctx'=64,'kvh'=8] {'kvh'}, dimensions={0} | all-to-all | bytes 40960 | tf_op jit(solution)/shard_map/all_to_all | solution.py:222
  117.2 0.7 broadcast_in_dim.11
  117.9 6.8 %all-to-all-start.3 = ((f32[64,1,512]{2,1,0:T(1,128)}), f32[64,1,512]{2,1,0:T(1,128)S(1)}, u32[]{:S(2)}, u32[]{:S(2)}) async-start(f32[64,1,512]{2,1,0:T(1,128)} %broadcast_in_dim.11), calls=%async_computation.3 | async-start | bytes 262144 | tf_op jit(solution)/shard_map/all_to_all | solution.py:222
  124.7 0.5 slice.21
  125.2 9.8 %all-to-all-done.3 = f32[64,1,512]{2,1,0:T(1,128)S(1)} async-done(((f32[64,1,512]{2,1,0:T(1,128)}), f32[64,1,512]{2,1,0:T(1,128)S(1)}, u32[]{:S(2)}, u32[]{:S(2)}) %all-to-all-start.3) | async-done | bytes 131104 | tf_op jit(solution)/shard_map/all_to_all | solution.py:222
  135.0 0.7 fusion
  (23 shorter events, 0.2 us)
Async XLA Ops:
  23.7 13.9 %copy-start = (bf16[8,2,128,128]{3,2,1,0:T(8,128)(2,1)}, bf16[8,2,128,128]{3,2,1,0:T(8,128)(2,1)S(1)}, u32[]{:S(2)}) copy-start(bf16[8,2,128,128]{3,2,1,0:T(8,128)(2,1)S(1)} %all_to_all.20.same_ref) | copy-start | bytes 1572868
  23.7 13.9 %collective-permute-start = (bf16[8,2,128,128]{3,2,1,0:T(8,128)(2,1)S(1)}, bf16[8,2,128,128]{3,2,1,0:T(8,128)(2,1)S(1)}, u32[]{:S(2)}, u32[]{:S(2)}) collective-permute-start(bf16[8,2,128,128]{3,2,1,0:T(8,128)(2,1)S(1)} %all_to_all.20.same_ref), channel_id=1, source_target_pairs={{0,8},{8,0},{16,24},{24,16},{32,40},{40,32},{48,56},{56,48},{64,72... | collective-permute-start | bytes 1572872 | tf_op jit(solution)/shard_map/ppermute | solution.py:241
  29.3 27.0 %collective-permute-start.3 = (bf16[8,2,128,128]{3,2,1,0:T(8,128)(2,1)S(1)}, bf16[8,2,128,128]{3,2,1,0:T(8,128)(2,1)S(1)}, u32[]{:S(2)}, u32[]{:S(2)}) collective-permute-start(bf16[8,2,128,128]{3,2,1,0:T(8,128)(2,1)S(1)} %all_to_all.20.same_ref), channel_id=1, source_target_pairs={{0,384},{8,392},{16,400},{24,408},{32,416},{40,424},{48,432},{56,4... | collective-permute-start | bytes 1572872 | tf_op jit(solution)/shard_map/ppermute | solution.py:238
  33.7 22.5 %collective-permute-start.2 = (bf16[8,2,128,128]{3,2,1,0:T(8,128)(2,1)S(1)}, bf16[8,2,128,128]{3,2,1,0:T(8,128)(2,1)S(1)}, u32[]{:S(2)}, u32[]{:S(2)}) collective-permute-start(bf16[8,2,128,128]{3,2,1,0:T(8,128)(2,1)S(1)} %all_to_all.20.same_ref), channel_id=1, source_target_pairs={{0,256},{8,264},{16,272},{24,280},{32,288},{40,296},{48,304},{56,3... | collective-permute-start | bytes 1572872 | tf_op jit(solution)/shard_map/ppermute | solution.py:238
  35.1 22.6 %collective-permute-start.1 = (bf16[8,2,128,128]{3,2,1,0:T(8,128)(2,1)S(1)}, bf16[8,2,128,128]{3,2,1,0:T(8,128)(2,1)S(1)}, u32[]{:S(2)}, u32[]{:S(2)}) collective-permute-start(bf16[8,2,128,128]{3,2,1,0:T(8,128)(2,1)S(1)} %all_to_all.20.same_ref), channel_id=1, source_target_pairs={{0,128},{8,136},{16,144},{24,152},{32,160},{40,168},{48,176},{56,1... | collective-permute-start | bytes 1572872 | tf_op jit(solution)/shard_map/ppermute | solution.py:238
  37.6 0.8 copy-start.1
  56.3 9.9 %copy-start.2 = (bf16[8,2,128,128]{3,2,1,0:T(8,128)(2,1)}, bf16[8,2,128,128]{3,2,1,0:T(8,128)(2,1)S(1)}, u32[]{:S(2)}) copy-start(bf16[8,2,128,128]{3,2,1,0:T(8,128)(2,1)S(1)} %collective-permute-done.3.rest_4_) | copy-start | bytes 1572868
  56.3 9.9 %copy-start.3 = (bf16[8,2,128,128]{3,2,1,0:T(8,128)(2,1)}, bf16[8,2,128,128]{3,2,1,0:T(8,128)(2,1)S(1)}, u32[]{:S(2)}) copy-start(bf16[8,2,128,128]{3,2,1,0:T(8,128)(2,1)S(1)} %collective-permute-done.2.rest_2_) | copy-start | bytes 1572868
  57.6 8.6 %copy-start.4 = (bf16[8,2,128,128]{3,2,1,0:T(8,128)(2,1)}, bf16[8,2,128,128]{3,2,1,0:T(8,128)(2,1)S(1)}, u32[]{:S(2)}) copy-start(bf16[8,2,128,128]{3,2,1,0:T(8,128)(2,1)S(1)} %collective-permute-done.1.rest_0_) | copy-start | bytes 1572868
  57.6 7.0 %collective-permute-start.4 = (bf16[8,2,128,128]{3,2,1,0:T(8,128)(2,1)S(1)}, bf16[8,2,128,128]{3,2,1,0:T(8,128)(2,1)S(1)}, u32[]{:S(2)}, u32[]{:S(2)}) collective-permute-start(bf16[8,2,128,128]{3,2,1,0:T(8,128)(2,1)S(1)} %collective-permute-done.1.rest_0_), channel_id=1, source_target_pairs={{0,8},{8,0},{16,24},{24,16},{32,40},{40,32},{48,56},{56,48},{64,72... | collective-permute-start | bytes 1572872 | tf_op jit(solution)/shard_map/ppermute | solution.py:259
  60.3 4.4 %collective-permute-start.5 = (bf16[8,2,128,128]{3,2,1,0:T(8,128)(2,1)S(1)}, bf16[8,2,128,128]{3,2,1,0:T(8,128)(2,1)S(1)}, u32[]{:S(2)}, u32[]{:S(2)}) collective-permute-start(bf16[8,2,128,128]{3,2,1,0:T(8,128)(2,1)S(1)} %collective-permute-done.2.rest_2_), channel_id=1, source_target_pairs={{0,8},{8,0},{16,24},{24,16},{32,40},{40,32},{48,56},{56,48},{64,72... | collective-permute-start | bytes 1572872 | tf_op jit(solution)/shard_map/ppermute | solution.py:259
  62.3 3.9 %collective-permute-start.6 = (bf16[8,2,128,128]{3,2,1,0:T(8,128)(2,1)S(1)}, bf16[8,2,128,128]{3,2,1,0:T(8,128)(2,1)S(1)}, u32[]{:S(2)}, u32[]{:S(2)}) collective-permute-start(bf16[8,2,128,128]{3,2,1,0:T(8,128)(2,1)S(1)} %collective-permute-done.3.rest_4_), channel_id=1, source_target_pairs={{0,8},{8,0},{16,24},{24,16},{32,40},{40,32},{48,56},{56,48},{64,72... | collective-permute-start | bytes 1572872 | tf_op jit(solution)/shard_map/ppermute | solution.py:259
  64.7 1.5 %copy-start.5 = (bf16[8,2,128,128]{3,2,1,0:T(8,128)(2,1)}, bf16[8,2,128,128]{3,2,1,0:T(8,128)(2,1)S(1)}, u32[]{:S(2)}) copy-start(bf16[8,2,128,128]{3,2,1,0:T(8,128)(2,1)S(1)} %collective-permute-done.4.rest_1_) | copy-start | bytes 1572868
  64.7 1.5 %copy-start.6 = (bf16[8,2,128,128]{3,2,1,0:T(8,128)(2,1)}, bf16[8,2,128,128]{3,2,1,0:T(8,128)(2,1)S(1)}, u32[]{:S(2)}) copy-start(bf16[8,2,128,128]{3,2,1,0:T(8,128)(2,1)S(1)} %collective-permute-done.5.rest_3_) | copy-start | bytes 1572868
  66.2 0.8 copy-start.7
  117.9 17.1 %all-to-all-start.3 = ((f32[64,1,512]{2,1,0:T(1,128)}), f32[64,1,512]{2,1,0:T(1,128)S(1)}, u32[]{:S(2)}, u32[]{:S(2)}) async-start(f32[64,1,512]{2,1,0:T(1,128)} %broadcast_in_dim.11), calls=%async_computation.3 | async-start | bytes 262144 | tf_op jit(solution)/shard_map/all_to_all | solution.py:222

commit v3 on v2

v3 whole, which is shorter than its diff:
```python
import functools

import jax
import jax.numpy as jnp
from jax import lax
from jax.experimental import pallas as pl
from jax.experimental.pallas import tpu as pltpu
from jax.sharding import PartitionSpec as P

F32, BF16 = jnp.float32, jnp.bfloat16
NN = (((1,), (0,)), ((), ()))
NT = (((1,), (1,)), ((), ()))
LOG2E = 1.4426950408889634
CORES = 2


def dot(a, b, dims=NN):
    return lax.dot_general(a, b, dims, preferred_element_type=F32)


def halves(a):
    high = a.astype(BF16)
    return high, (a - high.astype(F32)).astype(BF16)


def dot3(a, b, dims=NN):
    ah, al = halves(a)
    bh, bl = halves(b)
    return dot(ah, bh, dims) + (dot(ah, bl, dims) + dot(al, bh, dims))


def dot2(a, b, dims=NN):
    ah, al = halves(a)
    return dot(ah, b, dims) + dot(al, b, dims)


def log1p(e):
    return jnp.where(e < 1e-3, e * (1.0 - e * (0.5 - e * (1.0 / 3.0))), jnp.log(1.0 + e))


def feature_parts(pre):
    e = jnp.exp(-jnp.abs(pre))
    t = log1p(e)
    r = 1.0 / (1.0 + e)
    return jnp.maximum(pre, 0.0) + t, jnp.maximum(-pre, 0.0) + t, jnp.where(pre >= 0.0, r, e * r)


def pair(a):
    return jnp.concatenate([a, a], 1)


def with_ones(v):
    return jnp.concatenate([v, jnp.ones_like(v)], 1)


def flat(ref, which):
    blocks, rows, head = ref.shape[0], ref.shape[2], ref.shape[3]
    return ref[:, which].reshape(blocks * rows, head)


def place(ny):
    me = lax.axis_index("ctx")
    return me // (ny * CORES), (me // CORES) % ny, me % CORES


def diagonal(n, rows):
    return lax.broadcasted_iota(jnp.int32, (n, rows), 1) <= (
        lax.broadcasted_iota(jnp.int32, (n, rows), 0) // (n // rows)
    )


def to_rows(columns, head):
    n = columns[0].shape[0]
    lane = lax.broadcasted_iota(jnp.int32, (n, head), 1)
    wide = jnp.zeros((n, head), F32)
    for i, c in enumerate(columns):
        wide = jnp.where(lane == i, c, wide)
    rows = wide.T[:8]
    return jnp.concatenate([rows[:, k : k + head] for k in range(0, n, head)], 0)


def to_columns(rows, head):
    top = jnp.concatenate([rows[k : k + 8] for k in range(0, rows.shape[0], 8)], 1)
    return jnp.concatenate([top] * (head // 8), 0).T


def prepare(q_ref, kv_ref, wq_ref, wk_ref, fq_ref, fqt_ref, sigq_ref, fkd_ref, sigd_ref, near_ref):
    q, kd, vd = q_ref[...], kv_ref[0], kv_ref[1]
    wqt = jnp.concatenate(halves(wq_ref[...].T), 1)
    w2 = jnp.concatenate(halves(wk_ref[...].T), 1)
    sp, sm, sigq_ref[...] = feature_parts(dot(wqt, pair(q), NT))
    fq_t = jnp.concatenate([sp, sm], 0)
    fqt_ref[...] = fq_t
    fq = fq_t.T
    fq_ref[...] = fq
    sp, sm, sigd_ref[...] = feature_parts(dot(w2, pair(kd), NT))
    fk_t = jnp.concatenate([sp, sm], 0)
    fkd_ref[...] = fk_t
    attn = jnp.where(diagonal(q.shape[0], kd.shape[0]), dot3(fq, fk_t), 0.0)
    near_ref[...] = dot2(attn, with_ones(vd))


def forward(
    nx, ny, scale,
    q_ref, *rest,
):
    later = rest[: nx - 1]
    same_ref, other_ref, wk_ref, m_ref, accl_ref, state_ref, sig_ref, pay_ref, m_s, accl_s, full_s = rest[nx - 1 :]
    x, y, core = place(ny)
    rows, head = same_ref.shape[2], same_ref.shape[3]
    n, keys_n = q_ref.shape[0], ny * rows
    c = scale * LOG2E
    w2 = jnp.concatenate(halves(wk_ref[...].T), 1)
    key = lax.broadcasted_iota(jnp.int32, (1, keys_n), 1)
    kvs = [(flat(same_ref, 0), with_ones(flat(same_ref, 1))), (flat(other_ref, 0), with_ones(flat(other_ref, 1)))]

    def rounded_max(scores):
        return scores.max(-1, keepdims=True).astype(BF16).astype(F32)

    for half, (keys, values1) in enumerate(kvs):
        sp, sm, sig_ref[half] = feature_parts(dot(w2, pair(keys), NT))
        feats = jnp.concatenate([sp, sm], 0)
        seen = jnp.where(key < (y + half * core) * rows, feats, 0.0)
        part, whole = dot2(seen, values1), dot2(feats, values1)
        if half == 0:
            state_ref[...], full_s[...] = part, whole
        else:
            state_ref[...] += part
            full_s[...] += whole

    feats_n = full_s.shape[0]

    def send(s):
        to = x + s
        total = accl_s[:, head : head + 1]
        norm = full_s[:, head : head + 1]
        th, nh = total.astype(BF16).astype(F32), norm.astype(BF16).astype(F32)
        pay_ref[to, :n] = accl_s[:, :head].astype(BF16)
        pay_ref[to, n : n + feats_n] = full_s[:, :head].astype(BF16)
        pay_ref[to, n + feats_n :] = to_rows([m_s[...], th, total - th, nh, norm - nh], head).astype(BF16)

    col = lax.broadcasted_iota(jnp.int32, (n, keys_n), 1)
    row = lax.broadcasted_iota(jnp.int32, (n, keys_n), 0) // (n // rows)
    q = q_ref[...]
    scores = jnp.where(col <= row + y * rows, dot(q, kvs[0][0], NT), -1e30)
    old = rounded_max(scores)
    first = dot(jnp.exp2((scores - old) * c).astype(BF16), kvs[0][1])
    scores = jnp.where(col < (y + core) * rows, dot(q, kvs[1][0], NT), -1e30)
    new = jnp.maximum(old, rounded_max(scores))
    m_ref[...] = new
    accl_ref[...] = first * jnp.exp2((old - new) * c) + dot(jnp.exp2((scores - new) * c).astype(BF16), kvs[1][1])
    for s in range(1, nx):

        @pl.when(x + s < nx)
        def _(s=s):
            q = later[s - 1][...]
            scores = dot(q, kvs[0][0], NT)
            old = rounded_max(scores)
            first = dot(jnp.exp2((scores - old) * c).astype(BF16), kvs[0][1])
            scores = dot(q, kvs[1][0], NT)
            new = jnp.maximum(old, rounded_max(scores))
            m_s[...] = new
            accl_s[...] = first * jnp.exp2((old - new) * c) + dot(
                jnp.exp2((scores - new) * c).astype(BF16), kvs[1][1]
            )
            send(s)

    for d in range(nx):

        @pl.when(d <= x)
        def _(d=d):
            pay_ref[d] = jnp.zeros(pay_ref.shape[1:], BF16)


def merge(
    nx, ny, scale, count,
    m_in, accl_in, state_in, got_ref, fq_ref, fqt_ref, near_ref,
    out_ref, dnum_ref, dden_ref, state_ref, back_ref, pay_ref, loss_ref, m_ref, accl_ref,
):
    x, _, _ = place(ny)
    n, feats_n = fq_ref.shape
    head = out_ref.shape[1]
    c = scale * LOG2E
    m_ref[...] = m_in[...]
    accl_ref[...] = accl_in[...]
    state_ref[...] = state_in[...]
    for s in range(1, nx):

        @pl.when(x >= s)
        def _(s=s):
            columns = to_columns(got_ref[x - s, n + feats_n :].astype(F32), head)
            theirs = columns[:, 0:1]
            total = columns[:, 1:2] + columns[:, 2:3]
            norm = columns[:, 3:4] + columns[:, 4:5]
            old = m_ref[...]
            new = jnp.maximum(old, theirs)
            m_ref[...] = new
            mine, other = jnp.exp2((old - new) * c), jnp.exp2((theirs - new) * c)
            accl_ref[:, :head] = accl_ref[:, :head] * mine + got_ref[x - s, :n].astype(F32) * other
            accl_ref[:, head:] = accl_ref[:, head:] * mine + total * other
            state_ref[:, :head] += got_ref[x - s, n : n + feats_n].astype(F32)
            state_ref[:, head:] += norm

    accl = accl_ref[...]
    targets = (accl[:, :head] / accl[:, head:]).astype(BF16).astype(F32)
    numden = dot3(fq_ref[...], state_ref[...]) + near_ref[...]
    den = numden[:, head:]
    outs = numden[:, :head] / den
    out_ref[...] = outs.astype(BF16)
    diff = outs - targets
    loss_ref[...] = jnp.full(loss_ref.shape, jnp.sum(diff * diff) / count, F32)
    grad_out = diff * (2.0 / count)
    d_num = grad_out / den
    d_den = -jnp.sum(grad_out * outs, -1, keepdims=True) / den
    dnum_ref[...] = d_num
    dden_ref[...] = d_den
    back = dot3(fqt_ref[...], jnp.concatenate([d_num, d_den], 1))
    back_ref[...] = back
    norm = back[:, head : head + 1]
    nh = norm.astype(BF16).astype(F32)
    rows = to_rows([nh, norm - nh], head).astype(BF16)
    for d in range(nx):
        pay_ref[d, :feats_n] = back[:, :head].astype(BF16)
        pay_ref[d, feats_n:] = rows


def near_grads(
    q_ref, kv_ref, dnum_ref, dden_ref, state_ref, fqt_ref, sigq_ref, fkd_ref, sigd_ref, grads_ref
):
    q, kd, vd = q_ref[...], kv_ref[0], kv_ref[1]
    head, rows = kd.shape[1], kd.shape[0]
    d_num, d_den, fq_t, fk_t = dnum_ref[...], dden_ref[...], fqt_ref[...], fkd_ref[...]
    d_attn = jnp.where(diagonal(q.shape[0], rows), dot2(d_num, vd, NT) + d_den[:, :rows], 0.0)
    lane = lax.broadcasted_iota(jnp.int32, d_den.shape, 1)
    d_aug = jnp.concatenate([d_num, jnp.where(lane == 0, d_den, 0.0)], 1)
    d_fq = dot3(state_ref[...], d_aug, NT) + dot3(fk_t, d_attn, NT)
    sig_q, sig_d = sigq_ref[...], sigd_ref[...]
    d_pre = d_fq[:head] * sig_q - d_fq[head:] * (1.0 - sig_q)
    grads_ref[:head] = dot2(d_pre, q)
    d_fk = dot3(fq_t, d_attn)
    d_pre = d_fk[:head] * sig_d - d_fk[head:] * (1.0 - sig_d)
    grads_ref[head:] = dot2(d_pre, kd)


def backward(
    nx, ny,
    same_ref, other_ref, sig_ref, back_in, got_ref, near_ref, loss_ref,
    grad_ref, after_ref, sum_ref,
):
    x, y, core = place(ny)
    rows, head = same_ref.shape[2], same_ref.shape[3]
    keys_n = ny * rows
    feats_n = back_in.shape[0]
    after_ref[...] = jnp.zeros_like(after_ref)
    for s in range(1, nx):

        @pl.when(x + s < nx)
        def _(s=s):
            columns = to_columns(got_ref[x + s, feats_n:].astype(F32), head)
            after_ref[:, :head] += got_ref[x + s, :feats_n].astype(F32)
            after_ref[:, head:] += columns[:, 0:1] + columns[:, 1:2]

    def both(state):
        joint = state[:head] + state[head:]
        mats = jnp.concatenate([joint[:, :head], state[head:, :head]], 0)
        norms = jnp.concatenate([joint[:, head : head + 1], state[head:, head : head + 1]], 0)
        return jnp.concatenate(halves(mats), 1), norms

    own2, own_n = both(back_in[...])
    after2, after_n = both(after_ref[...])
    two = jnp.concatenate([own2, after2], 0)
    key = lax.broadcasted_iota(jnp.int32, (1, keys_n), 1)
    total = near_ref[head:]
    for half, ref in enumerate((same_ref, other_ref)):
        z = dot(two, pair(flat(ref, 1)), NT)
        d = jnp.where(key < (y + half * core) * rows, z[: 2 * head] + own_n, 0.0) + (z[2 * head :] + after_n)
        total += dot2(sig_ref[half] * d[:head] - d[head:], flat(ref, 0))
    sum_ref[:head] = near_ref[:head].T
    sum_ref[head:] = total.T
    chunks = grad_ref.shape[0] - 2 * head
    parts = 2 * head // chunks
    for r in range(parts):
        grad_ref[pl.ds(r, chunks, stride=parts + 1), :] = sum_ref[pl.ds(r, chunks, stride=parts), :]
    grad_ref[pl.ds(parts, chunks, stride=parts + 1), :] = jnp.broadcast_to(loss_ref[0:1], (chunks, head))


VMEM = pl.BlockSpec(memory_space=pltpu.VMEM)
PARAMS = pltpu.CompilerParams(vmem_limit_bytes=56 * 1024 * 1024)


def spread(a, axis, groups=None, ways=None):
    ways = ways or lax.axis_size(axis)
    copies = jnp.broadcast_to(a[None], (ways, *a.shape))
    return lax.all_to_all(copies, axis, 0, 0, tiled=True, axis_index_groups=groups)


def shards(nx, ny, queries, keys, values, w_query, w_key):
    rows, groups, per, head = queries.shape
    n_ctx, n_kvh = lax.axis_size("ctx"), lax.axis_size("kvh")
    scale = head**-0.5
    count = float(rows * n_ctx * groups * n_kvh * per)
    at = lambda x, y, c: (x * ny + y) * CORES + c
    every = [(x, y, c) for x in range(nx) for y in range(ny) for c in range(CORES)]
    y_groups = [[at(x, y, c) for y in range(ny)] for x in range(nx) for c in range(CORES)]
    x_groups = [[at(x, y, c) for x in range(nx)] for y in range(ny) for c in range(CORES)]
    swap = [(at(x, y, c), at(x, y, 1 - c)) for x, y, c in every]
    n, feats, keys_n = rows * per, 2 * head, ny * rows
    f32 = lambda *shape: jax.ShapeDtypeStruct(shape, F32)
    bf16 = lambda *shape: jax.ShapeDtypeStruct(shape, BF16)

    def call(body, outs, args, scratch=(), flops=1, name=None):
        return pl.pallas_call(
            body,
            out_shape=outs,
            in_specs=[VMEM] * len(args),
            out_specs=jax.tree.map(lambda _: VMEM, outs),
            scratch_shapes=[pltpu.VMEM(shape, F32) for shape in scratch],
            compiler_params=PARAMS,
            cost_estimate=pl.CostEstimate(
                flops=flops * 1_000_000_000, bytes_accessed=2_000_000, transcendentals=flops * 300_000
            ),
            name=name,
        )(*args)

    q = queries.reshape(n, head)
    kv = jnp.stack([keys.reshape(rows, head), values.reshape(rows, head)])
    same = spread(kv, "ctx", y_groups, ny)
    later = [
        lax.ppermute(q, "ctx", [(at(x, y, c), at(x - s, y, c)) for x, y, c in every if x >= s])
        for s in range(1, nx)
    ]
    own = call(
        prepare,
        (f32(n, feats), f32(feats, n), f32(head, n), f32(feats, rows), f32(head, rows), f32(n, feats)),
        (q, kv, w_query, w_key), flops=2, name="prepare",
    )
    same, later, (fq, fqt, sigq, fkd, sigd, near) = lax.optimization_barrier((same, later, own))
    other = lax.ppermute(same, "ctx", swap)
    m, accl, state, sig, pay = call(
        functools.partial(forward, nx, ny, scale),
        (f32(n, 1), f32(n, feats), f32(feats, feats), f32(2, head, keys_n), bf16(nx, n + feats + 16, head)),
        (q, *later, same, other, w_key),
        scratch=((n, 1), (n, feats), (feats, feats)), flops=6, name="forward",
    )
    got = lax.all_to_all(pay, "ctx", 0, 0, tiled=True, axis_index_groups=x_groups)
    out, dnum, dden, state, back, pay, loss = call(
        functools.partial(merge, nx, ny, scale, count),
        (bf16(n, head), f32(n, head), f32(n, head), f32(feats, feats), f32(feats, feats), bf16(nx, feats + 16, head), f32(8, head)),
        (m, accl, state, got, fq, fqt, near),
        scratch=((n, 1), (n, feats)), flops=2, name="merge",
    )
    got = lax.all_to_all(pay, "ctx", 0, 0, tiled=True, axis_index_groups=x_groups)
    grads = call(
        near_grads, f32(feats, head), (q, kv, dnum, dden, state, fqt, sigq, fkd, sigd), flops=2, name="near_grads",
    )
    parts = feats // n_ctx
    grads = call(
        functools.partial(backward, nx, ny),
        f32(n_ctx * (parts + 1), head),
        (same, other, sig, back, got, grads, loss),
        scratch=((feats, feats), (feats, head)), flops=4, name="backward",
    )
    mine = lax.all_to_all(grads.reshape(n_ctx, 1, -1), "ctx", 0, 0, tiled=True).sum(0)
    mine = spread(mine, "kvh").sum(0)
    g = spread(mine[:, : parts * head], "ctx").reshape(2, head, head)
    return out.reshape(queries.shape), g[0], g[1], mine[0, parts * head]


def solution(mesh):
    n_ctx = mesh.shape["ctx"]
    ny = min(8, n_ctx // CORES)
    nx = n_ctx // (CORES * ny)
    placed = (P("ctx", "kvh", None, None), P("ctx", "kvh", None), P("ctx", "kvh", None), P(), P())
    return jax.shard_map(
        functools.partial(shards, nx, ny),
        mesh=mesh,
        in_specs=placed,
        out_specs=(P("ctx", "kvh", None, None), P(), P(), P()),
        check_vma=False,
    )
```

time: 136 us -> 127 us (0.934)
  blocking collectives: 65.6 us -> 47.5 us
  Pallas kernels: 11.6 us -> 23 us
  waiting for transfers between devices: 25.5 us -> 22.2 us
    all_to_all x2 -> x1, blocking collectives: 38.7 us -> 16.5 us  [spread(): lax.all_to_all(copies, axis, 0, 0, tiled=True, axis_index_groups=groups)]
    ppermute x6 -> x3, waiting for transfers between devices: 15.7 us -> 1.46 us  [shards(): lax.ppermute(q, 'ctx', [(at(x, y, c), at(x - s, y, c)) for x, y, c in eve...]
    all_to_all x0 -> x1, blocking collectives: none -> 13.6 us  [shards(): lax.all_to_all(pay, 'ctx', 0, 0, tiled=True, axis_index_groups=x_groups)]
    ppermute x6 -> x3, starting transfers between devices: 15.2 us -> 3.88 us  [shards(): lax.ppermute(q, 'ctx', [(at(x, y, c), at(x - s, y, c)) for x, y, c in eve...]
    pallas_call x2 -> x5, Pallas kernels: 11.6 us -> 23 us  [call(): pl.pallas_call(body, out_shape=outs, in_specs=[VMEM] * len(args), out_spe...]
    all_to_all x1, blocking collectives: 26.9 us -> 17.4 us  [shards(): lax.all_to_all(grads.reshape(n_ctx, 1, -1), 'ctx', 0, 0, tiled=True).sum(0)]
    all_to_all x1 -> x2, starting transfers between devices: 6.78 us -> 14.6 us  [spread(): lax.all_to_all(copies, axis, 0, 0, tiled=True, axis_index_groups=groups)]
    all_to_all x1 -> x2, waiting for transfers between devices: 9.85 us -> 16.7 us  [spread(): lax.all_to_all(copies, axis, 0, 0, tiled=True, axis_index_groups=groups)]
  transfers between devices with their start and end apart: 8 -> 7, of which waited for: 4 -> 6; matrix products, arithmetic and copies ran while one was open for 0% -> 0% of each run, Pallas kernels for 4% -> 4%
where the time goes in v3:
time: 127 us; the launch traced here: 126 us
  blocking collectives  47.5 us (37%)
  starting transfers between devices  27.5 us (22%)
  Pallas kernels  23 us (18%)
  waiting for transfers between devices  22.2 us (17%)
  local copies, waits for them, and re-layouts  4.36 us (3%)
    pallas_call x5, Pallas kernels, call(): pl.pallas_call(body, out_shape=outs, in_specs=[VMEM] * len(args), out_spe...  23 us
    all_to_all x1, blocking collectives, shards(): lax.all_to_all(grads.reshape(n_ctx, 1, -1), 'ctx', 0, 0, tiled=True).sum(0)  17.4 us
    all_to_all x2, waiting for transfers between devices, spread(): lax.all_to_all(copies, axis, 0, 0, tiled=True, axis_index_groups=groups)  16.7 us
    all_to_all x1, blocking collectives, spread(): lax.all_to_all(copies, axis, 0, 0, tiled=True, axis_index_groups=groups)  16.5 us
    all_to_all x2, starting transfers between devices, spread(): lax.all_to_all(copies, axis, 0, 0, tiled=True, axis_index_groups=groups)  14.6 us
    all_to_all x1, blocking collectives, shards(): lax.all_to_all(pay, 'ctx', 0, 0, tiled=True, axis_index_groups=x_groups)  13.6 us
    ppermute x1, starting transfers between devices, shards(): other = lax.ppermute(same, 'ctx', swap)  5.59 us
    ppermute x3, starting transfers between devices, shards(): lax.ppermute(q, 'ctx', [(at(x, y, c), at(x - s, y, c)) for x, y, c in eve...  3.88 us
  transfers between devices with their start and end apart: 7, of which 6 were waited for; matrix products, arithmetic and copies ran while one was open for 0% of the time, Pallas kernels for 4%

profile of v3, /device:TPU:1, one launch (start us, length us, event | category | flops | bytes accessed | tf_op | source)
XLA Modules:
  0.0 126.2 jit_solution(3785119792938026048)
XLA Ops:
  0.6 0.8 pad_maximum_fusion.kv_ref
  1.4 0.9 broadcast_in_dim.8
  2.3 7.8 %all-to-all-start = ((bf16[8,2,128,128]{3,2,1,0:T(8,128)(2,1)}), bf16[8,2,128,128]{3,2,1,0:T(8,128)(2,1)S(1)}, u32[]{:S(2)}, u32[]{:S(2)}) async-start(bf16[8,2,128,128]{3,2,1,0:T(8,128)(2,1)} %broadcast_in_dim.8), calls=%async_computation | async-start | bytes 1048576 | tf_op jit(solution)/shard_map/all_to_all | solution.py:294
  10.1 1.3 %collective-permute-start.2 = (bf16[256,128]{1,0:T(8,128)(2,1)S(1)}, bf16[256,128]{1,0:T(8,128)(2,1)S(1)}, u32[]{:S(2)}, u32[]{:S(2)}) collective-permute-start(bf16[256,128]{1,0:T(8,128)(2,1)S(1)} %bitcast.20), channel_id=1, source_target_pairs={{384,0},{392,8},{400,16},{408,24},{416,32},{424,40},{432,48},{440,... | collective-permute-start | bytes 196616 | tf_op jit(solution)/shard_map/ppermute | solution.py:329
  11.4 1.3 %collective-permute-start.1 = (bf16[256,128]{1,0:T(8,128)(2,1)S(1)}, bf16[256,128]{1,0:T(8,128)(2,1)S(1)}, u32[]{:S(2)}, u32[]{:S(2)}) collective-permute-start(bf16[256,128]{1,0:T(8,128)(2,1)S(1)} %bitcast.21), channel_id=1, source_target_pairs={{256,0},{264,8},{272,16},{280,24},{288,32},{296,40},{304,48},{312,... | collective-permute-start | bytes 196616 | tf_op jit(solution)/shard_map/ppermute | solution.py:329
  12.7 1.3 %collective-permute-start = (bf16[256,128]{1,0:T(8,128)(2,1)S(1)}, bf16[256,128]{1,0:T(8,128)(2,1)S(1)}, u32[]{:S(2)}, u32[]{:S(2)}) collective-permute-start(bf16[256,128]{1,0:T(8,128)(2,1)S(1)} %bitcast.22), channel_id=1, source_target_pairs={{128,0},{136,8},{144,16},{152,24},{160,32},{168,40},{176,48},{184,... | collective-permute-start | bytes 196616 | tf_op jit(solution)/shard_map/ppermute | solution.py:329
  14.0 2.5 %prepare.1 = (f32[256,256]{1,0:T(8,128)}, f32[256,256]{1,0:T(8,128)}, f32[128,256]{1,0:T(8,128)}, f32[256,128]{1,0:T(8,128)}, f32[128,128]{1,0:T(8,128)}, /*index=5*/f32[256,256]{1,0:T(8,128)}) custom-call(bf16[256,128]{1,0:T(8,128)(2,1)} %bitcast.17, bf16[2,128,128]{2,1,0:T(8,128)(2,1)} %copy-done.2, f32[128,128]{1,0:T(8,128)} %wq_ref.1, f32[128,128]{1,0:T(8,128)} %rest_5_.1), custom_call_target="tpu_custom_call" | custom-call | flops 2000000000 | bytes 2000000 | tf_op jit(solution)/shard_map/prepare/pallas_call | solution.py:312
  16.6 1.4 %collective-permute-done.1.rest_1_ = bf16[256,128]{1,0:T(8,128)(2,1)S(1)} collective-permute-done((bf16[256,128]{1,0:T(8,128)(2,1)S(1)}, bf16[256,128]{1,0:T(8,128)(2,1)S(1)}, u32[]{:S(2)}, u32[]{:S(2)}) %collective-permute-start.1) | collective-permute-done | bytes 65568 | tf_op jit(solution)/shard_map/ppermute | solution.py:329
  18.0 6.8 %all-to-all-done.rest_3_.same_ref = bf16[8,2,128,128]{3,2,1,0:T(8,128)(2,1)S(1)} async-done(((bf16[8,2,128,128]{3,2,1,0:T(8,128)(2,1)}), bf16[8,2,128,128]{3,2,1,0:T(8,128)(2,1)S(1)}, u32[]{:S(2)}, u32[]{:S(2)}) %all-to-all-start) | async-done | bytes 524320 | tf_op jit(solution)/shard_map/all_to_all | solution.py:294
  24.9 5.6 %collective-permute-start.3 = (bf16[8,2,128,128]{3,2,1,0:T(8,128)(2,1)S(1)}, bf16[8,2,128,128]{3,2,1,0:T(8,128)(2,1)S(1)}, u32[]{:S(2)}, u32[]{:S(2)}) collective-permute-start(bf16[8,2,128,128]{3,2,1,0:T(8,128)(2,1)S(1)} %all-to-all-done.rest_3_.same_ref), channel_id=1, source_target_pairs={{0,8},{8,0},{16,24},{24,16},{32,40},{40,32},{48,56},{56,48},{64,72... | collective-permute-start | bytes 1572872 | tf_op jit(solution)/shard_map/ppermute | solution.py:338
  30.5 1.5 %collective-permute-done.3.rest_4_.other_ref = bf16[8,2,128,128]{3,2,1,0:T(8,128)(2,1)S(1)} collective-permute-done((bf16[8,2,128,128]{3,2,1,0:T(8,128)(2,1)S(1)}, bf16[8,2,128,128]{3,2,1,0:T(8,128)(2,1)S(1)}, u32[]{:S(2)}, u32[]{:S(2)}) %collective-permute-start.3) | collective-permute-done | bytes 524320 | tf_op jit(solution)/shard_map/ppermute | solution.py:338
  32.0 0.8 copy-done.3
  32.8 9.8 %forward.1 = (f32[256,1]{1,0:T(8,128)}, f32[256,256]{1,0:T(8,128)}, f32[256,256]{1,0:T(8,128)}, f32[2,128,1024]{2,1,0:T(8,128)}, bf16[4,528,128]{2,1,0:T(8,128)(2,1)}) custom-call(bf16[256,128]{1,0:T(8,128)(2,1)} %bitcast.18, bf16[256,128]{1,0:T(8,128)(2,1)} %copy-done.7, bf16[256,128]{1,0:T(8,128)(2,1)} %copy-done.6, bf16[256,128]{1,0:T(8,128)(2,1)} %copy-done.5, ...), custom_call_target="tpu_custom_call" | custom-call | flops 6000000000 | bytes 2000000 | tf_op jit(solution)/shard_map/forward/pallas_call | solution.py:312
  42.5 13.6 %all_to_all.30.got_ref = bf16[4,528,128]{2,1,0:T(8,128)(2,1)} all-to-all(bf16[4,528,128]{2,1,0:T(8,128)(2,1)} %get-tuple-element.45), channel_id=1, replica_groups={{0,128,256,384},{8,136,264,392},{16,144,272,400},{24,152,280,408},{32,1..., dimensions={0} | all-to-all | bytes 1081344 | tf_op jit(solution)/shard_map/all_to_all | solution.py:345
  56.1 3.1 %merge.1 = (bf16[256,128]{1,0:T(8,128)(2,1)}, f32[256,128]{1,0:T(8,128)}, f32[256,128]{1,0:T(8,128)}, f32[256,256]{1,0:T(8,128)}, f32[256,256]{1,0:T(8,128)}, /*...) custom-call(f32[256,1]{1,0:T(8,128)} %get-tuple-element.42.m_in, f32[256,256]{1,0:T(8,128)} %get-tuple-element.43.accl_in, ...), custom_call_target="tpu_custom_call" | custom-call | flops 2000000000 | bytes 2000000 | tf_op jit(solution)/shard_map/merge/pallas_call | solution.py:312
  59.2 3.4 %all-to-all-start.2 = ((bf16[4,272,128]{2,1,0:T(8,128)(2,1)}), bf16[4,272,128]{2,1,0:T(8,128)(2,1)S(1)}, u32[]{:S(2)}, u32[]{:S(2)}) async-start(bf16[4,272,128]{2,1,0:T(8,128)(2,1)} %get-tuple-element.52), calls=%async_computation.2 | async-start | bytes 557056 | tf_op jit(solution)/shard_map/all_to_all | solution.py:352
  62.7 3.0 %near_grads.1.near_ref = f32[256,128]{1,0:T(8,128)} custom-call(bf16[256,128]{1,0:T(8,128)(2,1)} %bitcast.19, bf16[2,128,128]{2,1,0:T(8,128)(2,1)} %copy-done.2, f32[256,128]{1,0:T(8,128)} %get-tuple-element.53.dnum_ref, f32[256,128]{1,0:T(8,128)} %get-tuple-element.54.dden_ref, f32[256,256]{1,0:T(8,128)} %get-tuple-element.55.state_ref, ...), custom_call_target="tpu_custom_call" | custom-call | flops 2000000000 | bytes 2000000 | tf_op jit(solution)/shard_map/near_grads/pallas_call | solution.py:312
  65.7 2.6 %all-to-all-done.2.got_ref = bf16[4,272,128]{2,1,0:T(8,128)(2,1)S(1)} async-done(((bf16[4,272,128]{2,1,0:T(8,128)(2,1)}), bf16[4,272,128]{2,1,0:T(8,128)(2,1)S(1)}, u32[]{:S(2)}, u32[]{:S(2)}) %all-to-all-start.2) | async-done | bytes 278560 | tf_op jit(solution)/shard_map/all_to_all | solution.py:352
  69.0 4.5 %backward.1 = f32[320,128]{1,0:T(8,128)} custom-call(bf16[8,2,128,128]{3,2,1,0:T(8,128)(2,1)} %copy-done, bf16[8,2,128,128]{3,2,1,0:T(8,128)(2,1)} %copy-done.3, f32[2,128,1024]{2,1,0:T(8,128)} %get-tuple-element.50.sig_ref, f32[256,256]{1,0:T(8,128)} %get-tuple-element.51.back_in, bf16[4,272,128]{2,1,0:T(8,128)(2,1)} %copy-done.1, ...), custom_call_target="tpu_custom_call" | custom-call | flops 4000000000 | bytes 2000000 | tf_op jit(solution)/shard_map/backward/pallas_call | solution.py:312
  73.6 17.4 %all_to_all.31 = f32[64,1,640]{2,1,0:T(1,128)S(1)} all-to-all(f32[64,1,640]{2,1,0:T(1,128)} %bitcast.11), channel_id=1, replica_groups=mesh['ctx'=64,'kvh'=8] {'ctx'}, dimensions={0} | all-to-all | bytes 327680 | tf_op jit(solution)/shard_map/all_to_all | solution.py:363
  91.1 16.5 %all_to_all.32 = f32[8,1,640]{2,1,0:T(1,128)S(1)} all-to-all(f32[8,1,640]{2,1,0:T(1,128)S(1)} %broadcast_in_dim.9), channel_id=1, replica_groups=mesh['ctx'=64,'kvh'=8] {'kvh'}, dimensions={0} | all-to-all | bytes 40960 | tf_op jit(solution)/shard_map/all_to_all | solution.py:294
  107.6 0.7 broadcast_in_dim.11
  108.4 6.8 %all-to-all-start.5 = ((f32[64,1,512]{2,1,0:T(1,128)}), f32[64,1,512]{2,1,0:T(1,128)S(1)}, u32[]{:S(2)}, u32[]{:S(2)}) async-start(f32[64,1,512]{2,1,0:T(1,128)} %broadcast_in_dim.11), calls=%async_computation.5 | async-start | bytes 262144 | tf_op jit(solution)/shard_map/all_to_all | solution.py:294
  115.7 9.8 %all-to-all-done.5 = f32[64,1,512]{2,1,0:T(1,128)S(1)} async-done(((f32[64,1,512]{2,1,0:T(1,128)}), f32[64,1,512]{2,1,0:T(1,128)S(1)}, u32[]{:S(2)}, u32[]{:S(2)}) %all-to-all-start.5) | async-done | bytes 131104 | tf_op jit(solution)/shard_map/all_to_all | solution.py:294
  (24 shorter events, 2.2 us)
Async XLA Ops:
  1.4 0.9 copy-start.2
  2.3 7.8 %copy-start.4 = (bf16[128,1,2,128]{3,2,1,0:T(2,128)(2,1)S(1)}, bf16[128,1,2,128]{3,2,1,0:T(2,128)(2,1)}, u32[]{:S(2)}) copy-start(bf16[128,1,2,128]{3,2,1,0:T(2,128)(2,1)} %param.5) | copy-start | bytes 196612
  2.3 22.5 %all-to-all-start = ((bf16[8,2,128,128]{3,2,1,0:T(8,128)(2,1)}), bf16[8,2,128,128]{3,2,1,0:T(8,128)(2,1)S(1)}, u32[]{:S(2)}, u32[]{:S(2)}) async-start(bf16[8,2,128,128]{3,2,1,0:T(8,128)(2,1)} %broadcast_in_dim.8), calls=%async_computation | async-start | bytes 1048576 | tf_op jit(solution)/shard_map/all_to_all | solution.py:294
  10.1 6.4 %collective-permute-start.2 = (bf16[256,128]{1,0:T(8,128)(2,1)S(1)}, bf16[256,128]{1,0:T(8,128)(2,1)S(1)}, u32[]{:S(2)}, u32[]{:S(2)}) collective-permute-start(bf16[256,128]{1,0:T(8,128)(2,1)S(1)} %bitcast.20), channel_id=1, source_target_pairs={{384,0},{392,8},{400,16},{408,24},{416,32},{424,40},{432,48},{440,... | collective-permute-start | bytes 196616 | tf_op jit(solution)/shard_map/ppermute | solution.py:329
  11.4 6.5 %collective-permute-start.1 = (bf16[256,128]{1,0:T(8,128)(2,1)S(1)}, bf16[256,128]{1,0:T(8,128)(2,1)S(1)}, u32[]{:S(2)}, u32[]{:S(2)}) collective-permute-start(bf16[256,128]{1,0:T(8,128)(2,1)S(1)} %bitcast.21), channel_id=1, source_target_pairs={{256,0},{264,8},{272,16},{280,24},{288,32},{296,40},{304,48},{312,... | collective-permute-start | bytes 196616 | tf_op jit(solution)/shard_map/ppermute | solution.py:329
  12.7 5.3 %collective-permute-start = (bf16[256,128]{1,0:T(8,128)(2,1)S(1)}, bf16[256,128]{1,0:T(8,128)(2,1)S(1)}, u32[]{:S(2)}, u32[]{:S(2)}) collective-permute-start(bf16[256,128]{1,0:T(8,128)(2,1)S(1)} %bitcast.22), channel_id=1, source_target_pairs={{128,0},{136,8},{144,16},{152,24},{160,32},{168,40},{176,48},{184,... | collective-permute-start | bytes 196616 | tf_op jit(solution)/shard_map/ppermute | solution.py:329
  16.6 15.4 %copy-start.5 = (bf16[256,128]{1,0:T(8,128)(2,1)}, bf16[256,128]{1,0:T(8,128)(2,1)S(1)}, u32[]{:S(2)}) copy-start(bf16[256,128]{1,0:T(8,128)(2,1)S(1)} %collective-permute-done.2.rest_2_) | copy-start | bytes 196612
  17.9 14.1 %copy-start.6 = (bf16[256,128]{1,0:T(8,128)(2,1)}, bf16[256,128]{1,0:T(8,128)(2,1)S(1)}, u32[]{:S(2)}) copy-start(bf16[256,128]{1,0:T(8,128)(2,1)S(1)} %collective-permute-done.1.rest_1_) | copy-start | bytes 196612
  18.0 14.0 %copy-start.7 = (bf16[256,128]{1,0:T(8,128)(2,1)}, bf16[256,128]{1,0:T(8,128)(2,1)S(1)}, u32[]{:S(2)}) copy-start(bf16[256,128]{1,0:T(8,128)(2,1)S(1)} %collective-permute-done.rest_0_) | copy-start | bytes 196612
  24.9 7.1 %copy-start = (bf16[8,2,128,128]{3,2,1,0:T(8,128)(2,1)}, bf16[8,2,128,128]{3,2,1,0:T(8,128)(2,1)S(1)}, u32[]{:S(2)}) copy-start(bf16[8,2,128,128]{3,2,1,0:T(8,128)(2,1)S(1)} %all-to-all-done.rest_3_.same_ref) | copy-start | bytes 1572868
  24.9 7.1 %collective-permute-start.3 = (bf16[8,2,128,128]{3,2,1,0:T(8,128)(2,1)S(1)}, bf16[8,2,128,128]{3,2,1,0:T(8,128)(2,1)S(1)}, u32[]{:S(2)}, u32[]{:S(2)}) collective-permute-start(bf16[8,2,128,128]{3,2,1,0:T(8,128)(2,1)S(1)} %all-to-all-done.rest_3_.same_ref), channel_id=1, source_target_pairs={{0,8},{8,0},{16,24},{24,16},{32,40},{40,32},{48,56},{56,48},{64,72... | collective-permute-start | bytes 1572872 | tf_op jit(solution)/shard_map/ppermute | solution.py:338
  32.0 0.8 copy-start.3
  59.2 9.0 %all-to-all-start.2 = ((bf16[4,272,128]{2,1,0:T(8,128)(2,1)}), bf16[4,272,128]{2,1,0:T(8,128)(2,1)S(1)}, u32[]{:S(2)}, u32[]{:S(2)}) async-start(bf16[4,272,128]{2,1,0:T(8,128)(2,1)} %get-tuple-element.52), calls=%async_computation.2 | async-start | bytes 557056 | tf_op jit(solution)/shard_map/all_to_all | solution.py:352
  68.3 0.7 copy-start.1
  108.4 17.1 %all-to-all-start.5 = ((f32[64,1,512]{2,1,0:T(1,128)}), f32[64,1,512]{2,1,0:T(1,128)S(1)}, u32[]{:S(2)}, u32[]{:S(2)}) async-start(f32[64,1,512]{2,1,0:T(1,128)} %broadcast_in_dim.11), calls=%async_computation.5 | async-start | bytes 262144 | tf_op jit(solution)/shard_map/all_to_all | solution.py:294

commit v4 on v3

--- a/solution.py
+++ b/solution.py
@@ -84,8 +84,8 @@
     return jnp.concatenate([top] * (head // 8), 0).T
 
 
-def prepare(q_ref, kv_ref, wq_ref, wk_ref, fq_ref, fqt_ref, sigq_ref, fkd_ref, sigd_ref, near_ref):
-    q, kd, vd = q_ref[...], kv_ref[0], kv_ref[1]
+def prepare(q_ref, k_ref, v_ref, wq_ref, wk_ref, fq_ref, fqt_ref, sigq_ref, fkd_ref, sigd_ref, near_ref):
+    q, kd, vd = q_ref[...], k_ref[...], v_ref[...]
     wqt = jnp.concatenate(halves(wq_ref[...].T), 1)
     w2 = jnp.concatenate(halves(wk_ref[...].T), 1)
     sp, sm, sigq_ref[...] = feature_parts(dot(wqt, pair(q), NT))
@@ -100,70 +100,77 @@
     near_ref[...] = dot2(attn, with_ones(vd))
 
 
-def forward(
-    nx, ny, scale,
-    q_ref, *rest,
-):
+def add_states(keys, vals, w2, seen, sig_ref, part, whole):
+    rows = part.shape[0] // 2
+    sp, sm, sig_ref[...] = feature_parts(dot(w2, pair(keys), NT))
+    both = jnp.concatenate([sp, sm], 0)
+    for b in range(keys.shape[0] // rows):
+        high, low = halves(both[:, b * rows : (b + 1) * rows])
+        values1 = with_ones(vals[b * rows : (b + 1) * rows])
+        state = dot(jnp.concatenate([high, low], 1), jnp.concatenate([values1, values1], 0))
+        whole += state
+        part += state * (b < seen).astype(F32)
+    return part, whole
+
+
+def same_core(ny, same_ref, wk_ref, state_ref, full_ref, sig_ref):
+    _, y, _ = place(ny)
+    w2 = jnp.concatenate(halves(wk_ref[...].T), 1)
+    zero = jnp.zeros(state_ref.shape, F32)
+    state_ref[...], full_ref[...] = add_states(
+        flat(same_ref, 0), flat(same_ref, 1), w2, y, sig_ref, zero, zero
+    )
+
+
+def forward(nx, ny, scale, q_ref, *rest):
     later = rest[: nx - 1]
-    same_ref, other_ref, wk_ref, m_ref, accl_ref, state_ref, sig_ref, pay_ref, m_s, accl_s, full_s = rest[nx - 1 :]
+    (
+        same_ref, other_ref, wk_ref, state_in, full_in,
+        m_ref, accl_ref, state_ref, sig_ref, pay_ref, m_s, accl_s,
+    ) = rest[nx - 1 :]
     x, y, core = place(ny)
     rows, head = same_ref.shape[2], same_ref.shape[3]
     n, keys_n = q_ref.shape[0], ny * rows
     c = scale * LOG2E
     w2 = jnp.concatenate(halves(wk_ref[...].T), 1)
-    key = lax.broadcasted_iota(jnp.int32, (1, keys_n), 1)
-    kvs = [(flat(same_ref, 0), with_ones(flat(same_ref, 1))), (flat(other_ref, 0), with_ones(flat(other_ref, 1)))]
-
-    def rounded_max(scores):
-        return scores.max(-1, keepdims=True).astype(BF16).astype(F32)
-
-    for half, (keys, values1) in enumerate(kvs):
-        sp, sm, sig_ref[half] = feature_parts(dot(w2, pair(keys), NT))
-        feats = jnp.concatenate([sp, sm], 0)
-        seen = jnp.where(key < (y + half * core) * rows, feats, 0.0)
-        part, whole = dot2(seen, values1), dot2(feats, values1)
-        if half == 0:
-            state_ref[...], full_s[...] = part, whole
-        else:
-            state_ref[...] += part
-            full_s[...] += whole
-
-    feats_n = full_s.shape[0]
-
-    def send(s):
-        to = x + s
-        total = accl_s[:, head : head + 1]
-        norm = full_s[:, head : head + 1]
-        th, nh = total.astype(BF16).astype(F32), norm.astype(BF16).astype(F32)
-        pay_ref[to, :n] = accl_s[:, :head].astype(BF16)
-        pay_ref[to, n : n + feats_n] = full_s[:, :head].astype(BF16)
-        pay_ref[to, n + feats_n :] = to_rows([m_s[...], th, total - th, nh, norm - nh], head).astype(BF16)
+    keys0, values0 = flat(same_ref, 0), with_ones(flat(same_ref, 1))
+    keys1, values1 = flat(other_ref, 0), with_ones(flat(other_ref, 1))
+    state_ref[...], full = add_states(
+        keys1, flat(other_ref, 1), w2, y + core, sig_ref, state_in[...], full_in[...]
+    )
+    feats_n = full.shape[0]
+    full_high = full[:, :head].astype(BF16)
+    norm = full[:, head : head + 1]
+    norm_high = norm.astype(BF16).astype(F32)
+
+    def teach(q, m_out, accl_out, masks):
+        scores0, scores1 = dot(q, keys0, NT), dot(q, keys1, NT)
+        if masks is not None:
+            scores0 = jnp.where(masks[0], scores0, -1e30)
+            scores1 = jnp.where(masks[1], scores1, -1e30)
+        best = jnp.maximum(scores0.max(-1, keepdims=True), scores1.max(-1, keepdims=True))
+        best = best.astype(BF16).astype(F32)
+        m_out[...] = best
+        accl_out[...] = dot(jnp.exp2((scores0 - best) * c).astype(BF16), values0) + dot(
+            jnp.exp2((scores1 - best) * c).astype(BF16), values1
+        )
 
     col = lax.broadcasted_iota(jnp.int32, (n, keys_n), 1)
     row = lax.broadcasted_iota(jnp.int32, (n, keys_n), 0) // (n // rows)
-    q = q_ref[...]
-    scores = jnp.where(col <= row + y * rows, dot(q, kvs[0][0], NT), -1e30)
-    old = rounded_max(scores)
-    first = dot(jnp.exp2((scores - old) * c).astype(BF16), kvs[0][1])
-    scores = jnp.where(col < (y + core) * rows, dot(q, kvs[1][0], NT), -1e30)
-    new = jnp.maximum(old, rounded_max(scores))
-    m_ref[...] = new
-    accl_ref[...] = first * jnp.exp2((old - new) * c) + dot(jnp.exp2((scores - new) * c).astype(BF16), kvs[1][1])
+    teach(q_ref[...], m_ref, accl_ref, (col <= row + y * rows, col < (y + core) * rows))
     for s in range(1, nx):
 
         @pl.when(x + s < nx)
         def _(s=s):
-            q = later[s - 1][...]
-            scores = dot(q, kvs[0][0], NT)
-            old = rounded_max(scores)
-            first = dot(jnp.exp2((scores - old) * c).astype(BF16), kvs[0][1])
-            scores = dot(q, kvs[1][0], NT)
-            new = jnp.maximum(old, rounded_max(scores))
-            m_s[...] = new
-            accl_s[...] = first * jnp.exp2((old - new) * c) + dot(
-                jnp.exp2((scores - new) * c).astype(BF16), kvs[1][1]
-            )
-            send(s)
+            teach(later[s - 1][...], m_s, accl_s, None)
+            to = x + s
+            total = accl_s[:, head : head + 1]
+            high = total.astype(BF16).astype(F32)
+            pay_ref[to, :n] = accl_s[:, :head].astype(BF16)
+            pay_ref[to, n : n + feats_n] = full_high
+            pay_ref[to, n + feats_n :] = to_rows(
+                [m_s[...], high, total - high, norm_high, norm - norm_high], head
+            ).astype(BF16)
 
     for d in range(nx):
 
@@ -225,9 +232,9 @@
 
 
 def near_grads(
-    q_ref, kv_ref, dnum_ref, dden_ref, state_ref, fqt_ref, sigq_ref, fkd_ref, sigd_ref, grads_ref
+    q_ref, k_ref, v_ref, dnum_ref, dden_ref, state_ref, fqt_ref, sigq_ref, fkd_ref, sigd_ref, grads_ref
 ):
-    q, kd, vd = q_ref[...], kv_ref[0], kv_ref[1]
+    q, kd, vd = q_ref[...], k_ref[...], v_ref[...]
     head, rows = kd.shape[1], kd.shape[0]
     d_num, d_den, fq_t, fk_t = dnum_ref[...], dden_ref[...], fqt_ref[...], fkd_ref[...]
     d_attn = jnp.where(diagonal(q.shape[0], rows), dot2(d_num, vd, NT) + d_den[:, :rows], 0.0)
@@ -244,7 +251,7 @@
 
 def backward(
     nx, ny,
-    same_ref, other_ref, sig_ref, back_in, got_ref, near_ref, loss_ref,
+    same_ref, other_ref, sig0_ref, sig1_ref, back_in, got_ref, near_ref, loss_ref,
     grad_ref, after_ref, sum_ref,
 ):
     x, y, core = place(ny)
@@ -271,10 +278,10 @@
     two = jnp.concatenate([own2, after2], 0)
     key = lax.broadcasted_iota(jnp.int32, (1, keys_n), 1)
     total = near_ref[head:]
-    for half, ref in enumerate((same_ref, other_ref)):
+    for half, ref, sig_ref in ((0, same_ref, sig0_ref), (1, other_ref, sig1_ref)):
         z = dot(two, pair(flat(ref, 1)), NT)
         d = jnp.where(key < (y + half * core) * rows, z[: 2 * head] + own_n, 0.0) + (z[2 * head :] + after_n)
-        total += dot2(sig_ref[half] * d[:head] - d[head:], flat(ref, 0))
+        total += dot2(sig_ref[...] * d[:head] - d[head:], flat(ref, 0))
     sum_ref[:head] = near_ref[:head].T
     sum_ref[head:] = total.T
     chunks = grad_ref.shape[0] - 2 * head
@@ -285,7 +292,7 @@
 
 
 VMEM = pl.BlockSpec(memory_space=pltpu.VMEM)
-PARAMS = pltpu.CompilerParams(vmem_limit_bytes=56 * 1024 * 1024)
+PARAMS = pltpu.CompilerParams(vmem_limit_bytes=20 * 1024 * 1024)
 
 
 def spread(a, axis, groups=None, ways=None):
@@ -323,8 +330,8 @@
         )(*args)
 
     q = queries.reshape(n, head)
-    kv = jnp.stack([keys.reshape(rows, head), values.reshape(rows, head)])
-    same = spread(kv, "ctx", y_groups, ny)
+    k, v = keys.reshape(rows, head), values.reshape(rows, head)
+    same = spread(jnp.stack([k, v]), "ctx", y_groups, ny)
     later = [
         lax.ppermute(q, "ctx", [(at(x, y, c), at(x - s, y, c)) for x, y, c in every if x >= s])
         for s in range(1, nx)
@@ -332,15 +339,19 @@
     own = call(
         prepare,
         (f32(n, feats), f32(feats, n), f32(head, n), f32(feats, rows), f32(head, rows), f32(n, feats)),
-        (q, kv, w_query, w_key), flops=2, name="prepare",
+        (q, k, v, w_query, w_key), flops=2, name="prepare",
     )
     same, later, (fq, fqt, sigq, fkd, sigd, near) = lax.optimization_barrier((same, later, own))
     other = lax.ppermute(same, "ctx", swap)
-    m, accl, state, sig, pay = call(
+    state, full, sig0 = call(
+        functools.partial(same_core, ny),
+        (f32(feats, feats), f32(feats, feats), f32(head, keys_n)), (same, w_key), flops=2, name="same_core",
+    )
+    m, accl, state, sig1, pay = call(
         functools.partial(forward, nx, ny, scale),
-        (f32(n, 1), f32(n, feats), f32(feats, feats), f32(2, head, keys_n), bf16(nx, n + feats + 16, head)),
-        (q, *later, same, other, w_key),
-        scratch=((n, 1), (n, feats), (feats, feats)), flops=6, name="forward",
+        (f32(n, 1), f32(n, feats), f32(feats, feats), f32(head, keys_n), bf16(nx, n + feats + 16, head)),
+        (q, *later, same, other, w_key, state, full),
+        scratch=((n, 1), (n, feats)), flops=6, name="forward",
     )
     got = lax.all_to_all(pay, "ctx", 0, 0, tiled=True, axis_index_groups=x_groups)
     out, dnum, dden, state, back, pay, loss = call(
@@ -351,13 +362,13 @@
     )
     got = lax.all_to_all(pay, "ctx", 0, 0, tiled=True, axis_index_groups=x_groups)
     grads = call(
-        near_grads, f32(feats, head), (q, kv, dnum, dden, state, fqt, sigq, fkd, sigd), flops=2, name="near_grads",
+        near_grads, f32(feats, head), (q, k, v, dnum, dden, state, fqt, sigq, fkd, sigd), flops=2, name="near_grads",
     )
     parts = feats // n_ctx
     grads = call(
         functools.partial(backward, nx, ny),
         f32(n_ctx * (parts + 1), head),
-        (same, other, sig, back, got, grads, loss),
+        (same, other, sig0, sig1, back, got, grads, loss),
         scratch=((feats, feats), (feats, head)), flops=4, name="backward",
     )
     mine = lax.all_to_all(grads.reshape(n_ctx, 1, -1), "ctx", 0, 0, tiled=True).sum(0)

time: 127 us -> 118 us (0.929)
  Pallas kernels: 23 us -> 13.4 us
  blocking collectives: 47.5 us -> 44.8 us
  local copies, waits for them, and re-layouts: 4.36 us -> 5.84 us
  waiting for transfers between devices: 22.2 us -> 23.5 us
    pallas_call x5 -> x6, Pallas kernels: 23 us -> 13.4 us  [call(): pl.pallas_call(body, out_shape=outs, in_specs=[VMEM] * len(args), out_spe...]
    all_to_all x1, waiting for transfers between devices: 2.56 us -> 4.48 us  [shards(): lax.all_to_all(pay, 'ctx', 0, 0, tiled=True, axis_index_groups=x_groups)]
    all_to_all x1, blocking collectives: 13.6 us -> 11.8 us  [shards(): lax.all_to_all(pay, 'ctx', 0, 0, tiled=True, axis_index_groups=x_groups)]
    unnamed x16 -> x26, local copies, waits for them, and re-layouts: 1.54 us -> 3.02 us
  transfers between devices with their start and end apart: 7 -> 7, of which waited for: 6 -> 7; matrix products, arithmetic and copies ran while one was open for 0% -> 0% of each run, Pallas kernels for 4% -> 3%
where the time goes in v4:
time: 118 us; the launch traced here: 117 us
  blocking collectives  44.8 us (38%)
  starting transfers between devices  27.6 us (23%)
  waiting for transfers between devices  23.5 us (20%)
  Pallas kernels  13.4 us (11%)
  local copies, waits for them, and re-layouts  5.84 us (5%)
    all_to_all x2, waiting for transfers between devices, spread(): lax.all_to_all(copies, axis, 0, 0, tiled=True, axis_index_groups=groups)  16.7 us
    all_to_all x1, blocking collectives, shards(): lax.all_to_all(grads.reshape(n_ctx, 1, -1), 'ctx', 0, 0, tiled=True).sum(0)  16.5 us
    all_to_all x1, blocking collectives, spread(): lax.all_to_all(copies, axis, 0, 0, tiled=True, axis_index_groups=groups)  16.5 us
    all_to_all x2, starting transfers between devices, spread(): lax.all_to_all(copies, axis, 0, 0, tiled=True, axis_index_groups=groups)  14.6 us
    pallas_call x6, Pallas kernels, call(): pl.pallas_call(body, out_shape=outs, in_specs=[VMEM] * len(args), out_spe...  13.4 us
    all_to_all x1, blocking collectives, shards(): lax.all_to_all(pay, 'ctx', 0, 0, tiled=True, axis_index_groups=x_groups)  11.8 us
    ppermute x1, starting transfers between devices, shards(): other = lax.ppermute(same, 'ctx', swap)  5.59 us
    all_to_all x1, waiting for transfers between devices, shards(): lax.all_to_all(pay, 'ctx', 0, 0, tiled=True, axis_index_groups=x_groups)  4.48 us
  transfers between devices with their start and end apart: 7, of which 7 were waited for; matrix products, arithmetic and copies ran while one was open for 0% of the time, Pallas kernels for 3%

profile of v4, /device:TPU:1, one launch (start us, length us, event | category | flops | bytes accessed | tf_op | source)
XLA Modules:
  0.0 116.9 jit_solution(12691755533228863710)
XLA Ops:
  0.6 0.8 pad_maximum_fusion
  1.4 0.9 broadcast_in_dim.8
  2.3 7.8 %all-to-all-start = ((bf16[8,2,128,128]{3,2,1,0:T(8,128)(2,1)}), bf16[8,2,128,128]{3,2,1,0:T(8,128)(2,1)S(1)}, u32[]{:S(2)}, u32[]{:S(2)}) async-start(bf16[8,2,128,128]{3,2,1,0:T(8,128)(2,1)} %broadcast_in_dim.8), calls=%async_computation | async-start | bytes 1048576 | tf_op jit(solution)/shard_map/all_to_all | solution.py:301
  10.1 1.3 %collective-permute-start.2 = (bf16[256,128]{1,0:T(8,128)(2,1)S(1)}, bf16[256,128]{1,0:T(8,128)(2,1)S(1)}, u32[]{:S(2)}, u32[]{:S(2)}) collective-permute-start(bf16[256,128]{1,0:T(8,128)(2,1)S(1)} %bitcast.20), channel_id=1, source_target_pairs={{384,0},{392,8},{400,16},{408,24},{416,32},{424,40},{432,48},{440,... | collective-permute-start | bytes 196616 | tf_op jit(solution)/shard_map/ppermute | solution.py:336
  11.4 1.3 %collective-permute-start.1 = (bf16[256,128]{1,0:T(8,128)(2,1)S(1)}, bf16[256,128]{1,0:T(8,128)(2,1)S(1)}, u32[]{:S(2)}, u32[]{:S(2)}) collective-permute-start(bf16[256,128]{1,0:T(8,128)(2,1)S(1)} %bitcast.21), channel_id=1, source_target_pairs={{256,0},{264,8},{272,16},{280,24},{288,32},{296,40},{304,48},{312,... | collective-permute-start | bytes 196616 | tf_op jit(solution)/shard_map/ppermute | solution.py:336
  12.7 1.3 %collective-permute-start = (bf16[256,128]{1,0:T(8,128)(2,1)S(1)}, bf16[256,128]{1,0:T(8,128)(2,1)S(1)}, u32[]{:S(2)}, u32[]{:S(2)}) collective-permute-start(bf16[256,128]{1,0:T(8,128)(2,1)S(1)} %bitcast.22), channel_id=1, source_target_pairs={{128,0},{136,8},{144,16},{152,24},{160,32},{168,40},{176,48},{184,... | collective-permute-start | bytes 196616 | tf_op jit(solution)/shard_map/ppermute | solution.py:336
  14.1 0.9 prepare.1
  16.4 1.6 %collective-permute-done.1.rest_1_ = bf16[256,128]{1,0:T(8,128)(2,1)S(1)} collective-permute-done((bf16[256,128]{1,0:T(8,128)(2,1)S(1)}, bf16[256,128]{1,0:T(8,128)(2,1)S(1)}, u32[]{:S(2)}, u32[]{:S(2)}) %collective-permute-start.1) | collective-permute-done | bytes 65568 | tf_op jit(solution)/shard_map/ppermute | solution.py:336
  18.1 6.8 %all-to-all-done.same_ref.rest_3_ = bf16[8,2,128,128]{3,2,1,0:T(8,128)(2,1)S(1)} async-done(((bf16[8,2,128,128]{3,2,1,0:T(8,128)(2,1)}), bf16[8,2,128,128]{3,2,1,0:T(8,128)(2,1)S(1)}, u32[]{:S(2)}, u32[]{:S(2)}) %all-to-all-start) | async-done | bytes 524320 | tf_op jit(solution)/shard_map/all_to_all | solution.py:301
  24.9 5.6 %collective-permute-start.3 = (bf16[8,2,128,128]{3,2,1,0:T(8,128)(2,1)S(1)}, bf16[8,2,128,128]{3,2,1,0:T(8,128)(2,1)S(1)}, u32[]{:S(2)}, u32[]{:S(2)}) collective-permute-start(bf16[8,2,128,128]{3,2,1,0:T(8,128)(2,1)S(1)} %all-to-all-done.same_ref.rest_3_), channel_id=1, source_target_pairs={{0,8},{8,0},{16,24},{24,16},{32,40},{40,32},{48,56},{56,48},{64,72... | collective-permute-start | bytes 1572872 | tf_op jit(solution)/shard_map/ppermute | solution.py:345
  30.5 1.0 same_core.1
  32.0 6.7 %forward.1 = (f32[256,1]{1,0:T(8,128)S(1)}, f32[256,256]{1,0:T(8,128)S(1)}, f32[256,256]{1,0:T(8,128)S(1)}, f32[128,1024]{1,0:T(8,128)S(1)}, bf16[4,528,128]{2,1,0:T(8,128)(2,1)S(1)}) custom-call(bf16[256,128]{1,0:T(8,128)(2,1)S(1)} %bitcast.24, bf16[256,128]{1,0:T(8,128)(2,1)S(1)} %collective-permute-done.rest_0_, ...), custom_call_target="tpu_custom_call" | custom-call | flops 6000000000 | bytes 2000000 | tf_op jit(solution)/shard_map/forward/pallas_call | solution.py:319
  38.7 11.8 %all_to_all.30.got_ref = bf16[4,528,128]{2,1,0:T(8,128)(2,1)S(1)} all-to-all(bf16[4,528,128]{2,1,0:T(8,128)(2,1)S(1)} %get-tuple-element.50), channel_id=1, replica_groups={{0,128,256,384},{8,136,264,392},{16,144,272,400},{24,152,280,408},{32,1..., dimensions={0} | all-to-all | bytes 1081344 | tf_op jit(solution)/shard_map/all_to_all | solution.py:356
  50.5 1.6 %merge.1 = (bf16[256,128]{1,0:T(8,128)(2,1)}, f32[256,128]{1,0:T(8,128)S(1)}, f32[256,128]{1,0:T(8,128)S(1)}, f32[256,256]{1,0:T(8,128)S(1)}, f32[256,256]{1,0:T...) custom-call(f32[256,1]{1,0:T(8,128)S(1)} %get-tuple-element.47.m_in, ...), custom_call_target="tpu_custom_call" | custom-call | flops 2000000000 | bytes 2000000 | tf_op jit(solution)/shard_map/merge/pallas_call | solution.py:319
  52.8 3.6 %all-to-all-start.2 = ((bf16[4,272,128]{2,1,0:T(8,128)(2,1)}), bf16[4,272,128]{2,1,0:T(8,128)(2,1)S(1)}, u32[]{:S(2)}, u32[]{:S(2)}) async-start(bf16[4,272,128]{2,1,0:T(8,128)(2,1)} %get-tuple-element.58), calls=%async_computation.2 | async-start | bytes 557056 | tf_op jit(solution)/shard_map/all_to_all | solution.py:363
  56.4 1.1 near_grads.1.near_ref
  57.5 4.5 %all-to-all-done.2.got_ref = bf16[4,272,128]{2,1,0:T(8,128)(2,1)S(1)} async-done(((bf16[4,272,128]{2,1,0:T(8,128)(2,1)}), bf16[4,272,128]{2,1,0:T(8,128)(2,1)S(1)}, u32[]{:S(2)}, u32[]{:S(2)}) %all-to-all-start.2) | async-done | bytes 278560 | tf_op jit(solution)/shard_map/all_to_all | solution.py:363
  61.9 1.0 copy-done.8
  63.0 2.2 %backward.1 = f32[320,128]{1,0:T(8,128)S(1)} custom-call(bf16[8,2,128,128]{3,2,1,0:T(8,128)(2,1)S(1)} %all-to-all-done.same_ref.rest_3_, bf16[8,2,128,128]{3,2,1,0:T(8,128)(2,1)S(1)} %collective-permute-done.3.rest_4_.other_ref, f32[128,1024]{1,0:T(8,128)S(1)} %get-tuple-element.55.sig0_ref, f32[128,1024]{1,0:T(8,128)S(1)} %copy-done.8, ...), custom_call_target="tpu_custom_call" | custom-call | flops 4000000000 | bytes 2000000 | tf_op jit(solution)/shard_map/backward/pallas_call | solution.py:319
  65.2 16.5 %all_to_all.31 = f32[64,1,640]{2,1,0:T(1,128)S(1)} all-to-all(f32[64,1,640]{2,1,0:T(1,128)S(1)} %bitcast.13), channel_id=1, replica_groups=mesh['ctx'=64,'kvh'=8] {'ctx'}, dimensions={0} | all-to-all | bytes 327680 | tf_op jit(solution)/shard_map/all_to_all | solution.py:374
  81.8 16.5 %all_to_all.32 = f32[8,1,640]{2,1,0:T(1,128)S(1)} all-to-all(f32[8,1,640]{2,1,0:T(1,128)S(1)} %broadcast_in_dim.9), channel_id=1, replica_groups=mesh['ctx'=64,'kvh'=8] {'kvh'}, dimensions={0} | all-to-all | bytes 40960 | tf_op jit(solution)/shard_map/all_to_all | solution.py:301
  98.3 0.7 broadcast_in_dim.11
  99.1 6.8 %all-to-all-start.5 = ((f32[64,1,512]{2,1,0:T(1,128)}), f32[64,1,512]{2,1,0:T(1,128)S(1)}, u32[]{:S(2)}, u32[]{:S(2)}) async-start(f32[64,1,512]{2,1,0:T(1,128)} %broadcast_in_dim.11), calls=%async_computation.5 | async-start | bytes 262144 | tf_op jit(solution)/shard_map/all_to_all | solution.py:301
  106.4 9.8 %all-to-all-done.5 = f32[64,1,512]{2,1,0:T(1,128)S(1)} async-done(((f32[64,1,512]{2,1,0:T(1,128)}), f32[64,1,512]{2,1,0:T(1,128)S(1)}, u32[]{:S(2)}, u32[]{:S(2)}) %all-to-all-start.5) | async-done | bytes 131104 | tf_op jit(solution)/shard_map/all_to_all | solution.py:301
  (35 shorter events, 4.0 us)
Async XLA Ops:
  2.3 7.8 %copy-start.4 = (bf16[128,1,2,128]{3,2,1,0:T(2,128)(2,1)S(1)}, bf16[128,1,2,128]{3,2,1,0:T(2,128)(2,1)}, u32[]{:S(2)}) copy-start(bf16[128,1,2,128]{3,2,1,0:T(2,128)(2,1)} %param.5) | copy-start | bytes 196612
  2.3 11.7 %copy-start = (bf16[128,1,128]{2,0,1:T(8,128)(2,1)S(1)}, bf16[128,1,128]{2,0,1:T(8,128)(2,1)}, u32[]{:S(2)}) copy-start(bf16[128,1,128]{2,0,1:T(8,128)(2,1)} %param.7) | copy-start | bytes 98308
  2.3 11.7 %copy-start.1 = (bf16[128,1,128]{2,0,1:T(8,128)(2,1)S(1)}, bf16[128,1,128]{2,0,1:T(8,128)(2,1)}, u32[]{:S(2)}) copy-start(bf16[128,1,128]{2,0,1:T(8,128)(2,1)} %param.6) | copy-start | bytes 98308
  2.3 11.7 %copy-start.2 = (f32[128,128]{1,0:T(8,128)S(1)}, f32[128,128]{1,0:T(8,128)}, u32[]{:S(2)}) copy-start(f32[128,128]{1,0:T(8,128)} %wq_ref.1) | copy-start | bytes 196612
  2.3 11.7 %copy-start.3 = (f32[128,128]{1,0:T(8,128)S(1)}, f32[128,128]{1,0:T(8,128)}, u32[]{:S(2)}) copy-start(f32[128,128]{1,0:T(8,128)} %rest_5_.1) | copy-start | bytes 196612
  2.3 22.5 %all-to-all-start = ((bf16[8,2,128,128]{3,2,1,0:T(8,128)(2,1)}), bf16[8,2,128,128]{3,2,1,0:T(8,128)(2,1)S(1)}, u32[]{:S(2)}, u32[]{:S(2)}) async-start(bf16[8,2,128,128]{3,2,1,0:T(8,128)(2,1)} %broadcast_in_dim.8), calls=%async_computation | async-start | bytes 1048576 | tf_op jit(solution)/shard_map/all_to_all | solution.py:301
  10.1 6.2 %collective-permute-start.2 = (bf16[256,128]{1,0:T(8,128)(2,1)S(1)}, bf16[256,128]{1,0:T(8,128)(2,1)S(1)}, u32[]{:S(2)}, u32[]{:S(2)}) collective-permute-start(bf16[256,128]{1,0:T(8,128)(2,1)S(1)} %bitcast.20), channel_id=1, source_target_pairs={{384,0},{392,8},{400,16},{408,24},{416,32},{424,40},{432,48},{440,... | collective-permute-start | bytes 196616 | tf_op jit(solution)/shard_map/ppermute | solution.py:336
  11.4 6.5 %collective-permute-start.1 = (bf16[256,128]{1,0:T(8,128)(2,1)S(1)}, bf16[256,128]{1,0:T(8,128)(2,1)S(1)}, u32[]{:S(2)}, u32[]{:S(2)}) collective-permute-start(bf16[256,128]{1,0:T(8,128)(2,1)S(1)} %bitcast.21), channel_id=1, source_target_pairs={{256,0},{264,8},{272,16},{280,24},{288,32},{296,40},{304,48},{312,... | collective-permute-start | bytes 196616 | tf_op jit(solution)/shard_map/ppermute | solution.py:336
  12.7 5.3 %collective-permute-start = (bf16[256,128]{1,0:T(8,128)(2,1)S(1)}, bf16[256,128]{1,0:T(8,128)(2,1)S(1)}, u32[]{:S(2)}, u32[]{:S(2)}) collective-permute-start(bf16[256,128]{1,0:T(8,128)(2,1)S(1)} %bitcast.22), channel_id=1, source_target_pairs={{128,0},{136,8},{144,16},{152,24},{160,32},{168,40},{176,48},{184,... | collective-permute-start | bytes 196616 | tf_op jit(solution)/shard_map/ppermute | solution.py:336
  15.0 0.7 copy-start.9
  15.6 0.6 copy-start.11
  24.9 7.1 %collective-permute-start.3 = (bf16[8,2,128,128]{3,2,1,0:T(8,128)(2,1)S(1)}, bf16[8,2,128,128]{3,2,1,0:T(8,128)(2,1)S(1)}, u32[]{:S(2)}, u32[]{:S(2)}) collective-permute-start(bf16[8,2,128,128]{3,2,1,0:T(8,128)(2,1)S(1)} %all-to-all-done.same_ref.rest_3_), channel_id=1, source_target_pairs={{0,8},{8,0},{16,24},{24,16},{32,40},{40,32},{48,56},{56,48},{64,72... | collective-permute-start | bytes 1572872 | tf_op jit(solution)/shard_map/ppermute | solution.py:345
  38.7 11.8 %copy-start.7 = (f32[128,1024]{1,0:T(8,128)}, f32[128,1024]{1,0:T(8,128)S(1)}, u32[]{:S(2)}) copy-start(f32[128,1024]{1,0:T(8,128)S(1)} %get-tuple-element.56.sig1_ref) | copy-start | bytes 1572868
  52.1 0.7 copy-start.5
  52.8 3.6 %copy-start.6 = (f32[256,128]{1,0:T(8,128)S(1)}, f32[256,128]{1,0:T(8,128)}, u32[]{:S(2)}) copy-start(f32[256,128]{1,0:T(8,128)} %copy-done.5) | copy-start | bytes 393220
  52.8 3.6 %copy-start.10 = (f32[128,256]{1,0:T(8,128)S(1)}, f32[128,256]{1,0:T(8,128)}, u32[]{:S(2)}) copy-start(f32[128,256]{1,0:T(8,128)} %copy-done.9) | copy-start | bytes 393220
  52.8 3.6 %copy-start.12 = (f32[256,128]{1,0:T(8,128)S(1)}, f32[256,128]{1,0:T(8,128)}, u32[]{:S(2)}) copy-start(f32[256,128]{1,0:T(8,128)} %copy-done.11) | copy-start | bytes 393220
  52.8 9.2 %all-to-all-start.2 = ((bf16[4,272,128]{2,1,0:T(8,128)(2,1)}), bf16[4,272,128]{2,1,0:T(8,128)(2,1)S(1)}, u32[]{:S(2)}, u32[]{:S(2)}) async-start(bf16[4,272,128]{2,1,0:T(8,128)(2,1)} %get-tuple-element.58), calls=%async_computation.2 | async-start | bytes 557056 | tf_op jit(solution)/shard_map/all_to_all | solution.py:363
  61.9 1.0 copy-start.8
  99.1 17.1 %all-to-all-start.5 = ((f32[64,1,512]{2,1,0:T(1,128)}), f32[64,1,512]{2,1,0:T(1,128)S(1)}, u32[]{:S(2)}, u32[]{:S(2)}) async-start(f32[64,1,512]{2,1,0:T(1,128)} %broadcast_in_dim.11), calls=%async_computation.5 | async-start | bytes 262144 | tf_op jit(solution)/shard_map/all_to_all | solution.py:301

commit v5 on v4

v5 whole, which is shorter than its diff:
```python
import functools

import jax
import jax.numpy as jnp
from jax import lax
from jax.experimental import pallas as pl
from jax.experimental.pallas import tpu as pltpu
from jax.sharding import PartitionSpec as P

F32, BF16 = jnp.float32, jnp.bfloat16
NN = (((1,), (0,)), ((), ()))
NT = (((1,), (1,)), ((), ()))
LOG2E = 1.4426950408889634
CORES = 2


def dot(a, b, dims=NN):
    return lax.dot_general(a, b, dims, preferred_element_type=F32)


def halves(a):
    high = a.astype(BF16)
    return high, (a - high.astype(F32)).astype(BF16)


def dot3(a, b, dims=NN):
    ah, al = halves(a)
    bh, bl = halves(b)
    return dot(ah, bh, dims) + (dot(ah, bl, dims) + dot(al, bh, dims))


def dot2(a, b, dims=NN):
    ah, al = halves(a)
    return dot(ah, b, dims) + dot(al, b, dims)


def log1p(e):
    return jnp.where(e < 1e-3, e * (1.0 - e * (0.5 - e * (1.0 / 3.0))), jnp.log(1.0 + e))


def feature_parts(pre):
    e = jnp.exp(-jnp.abs(pre))
    t = log1p(e)
    r = 1.0 / (1.0 + e)
    return jnp.maximum(pre, 0.0) + t, jnp.maximum(-pre, 0.0) + t, jnp.where(pre >= 0.0, r, e * r)


def pair(a):
    return jnp.concatenate([a, a], 1)


def with_ones(v):
    return jnp.concatenate([v, jnp.ones_like(v)], 1)


def flat(ref, which):
    blocks, rows, head = ref.shape[0], ref.shape[2], ref.shape[3]
    return ref[:, which].reshape(blocks * rows, head)


def place(ny):
    me = lax.axis_index("ctx")
    return me // (ny * CORES), (me // CORES) % ny, me % CORES


def diagonal(n, rows):
    return lax.broadcasted_iota(jnp.int32, (n, rows), 1) <= (
        lax.broadcasted_iota(jnp.int32, (n, rows), 0) // (n // rows)
    )


def to_rows(columns, head):
    n = columns[0].shape[0]
    lane = lax.broadcasted_iota(jnp.int32, (n, head), 1)
    wide = jnp.zeros((n, head), F32)
    for i, c in enumerate(columns):
        wide = jnp.where(lane == i, c, wide)
    rows = wide.T[:8]
    return jnp.concatenate([rows[:, k : k + head] for k in range(0, n, head)], 0)


def to_columns(pages, head):
    rows = [
        jnp.concatenate([page[k : k + 8] for k in range(0, page.shape[0], 8)], 1) for page in pages
    ]
    rows += [rows[0]] * (head // 8 - len(rows))
    return jnp.concatenate(rows, 0).T


def own_features(q, k, wq, wk):
    wqt = jnp.concatenate(halves(wq.T), 1)
    w2 = jnp.concatenate(halves(wk.T), 1)
    sp, sm, sig_q = feature_parts(dot(wqt, pair(q), NT))
    fq_t = jnp.concatenate([sp, sm], 0)
    sp, sm, sig_k = feature_parts(dot(w2, pair(k), NT))
    return fq_t, sig_q, jnp.concatenate([sp, sm], 0), sig_k


def prepare(q_ref, k_ref, v_ref, wq_ref, wk_ref, fq_ref, near_ref):
    q, k, v = q_ref[...], k_ref[...], v_ref[...]
    fq_t, _, fk_t, _ = own_features(q, k, wq_ref[...], wk_ref[...])
    fq = fq_t.T
    fq_ref[...] = fq
    attn = jnp.where(diagonal(q.shape[0], k.shape[0]), dot3(fq, fk_t), 0.0)
    near_ref[...] = dot2(attn, with_ones(v))


def add_states(keys, vals, w2, seen, part, whole):
    rows = part.shape[0] // 2
    sp, sm, _ = feature_parts(dot(w2, pair(keys), NT))
    both = jnp.concatenate([sp, sm], 0)
    for b in range(keys.shape[0] // rows):
        high, low = halves(both[:, b * rows : (b + 1) * rows])
        values1 = with_ones(vals[b * rows : (b + 1) * rows])
        state = dot(jnp.concatenate([high, low], 1), jnp.concatenate([values1, values1], 0))
        whole += state
        part += state * (b < seen).astype(F32)
    return part, whole


def same_core(ny, same_ref, wk_ref, state_ref, full_ref):
    _, y, _ = place(ny)
    w2 = jnp.concatenate(halves(wk_ref[...].T), 1)
    zero = jnp.zeros(state_ref.shape, F32)
    state_ref[...], full_ref[...] = add_states(flat(same_ref, 0), flat(same_ref, 1), w2, y, zero, zero)


def teach(q, keys0, values0, keys1, values1, scale, masks=None):
    scores0, scores1 = dot(q, keys0, NT), dot(q, keys1, NT)
    if masks is not None:
        scores0 = jnp.where(masks[0], scores0, -1e30)
        scores1 = jnp.where(masks[1], scores1, -1e30)
    best = jnp.maximum(scores0.max(-1, keepdims=True), scores1.max(-1, keepdims=True))
    best = best.astype(BF16).astype(F32)
    c = scale * LOG2E
    return best, dot(jnp.exp2((scores0 - best) * c).astype(BF16), values0) + dot(
        jnp.exp2((scores1 - best) * c).astype(BF16), values1
    )


def own_teacher(ny, scale, q_ref, same_ref, other_ref, accl_ref):
    _, y, core = place(ny)
    n, rows = q_ref.shape[0], same_ref.shape[2]
    col = lax.broadcasted_iota(jnp.int32, (n, ny * rows), 1)
    row = lax.broadcasted_iota(jnp.int32, (n, ny * rows), 0) // (n // rows)
    best, accl = teach(
        q_ref[...],
        flat(same_ref, 0), with_ones(flat(same_ref, 1)),
        flat(other_ref, 0), with_ones(flat(other_ref, 1)),
        scale, (col <= row + y * rows, col < (y + core) * rows),
    )
    lane = lax.broadcasted_iota(jnp.int32, accl.shape, 1)
    accl_ref[...] = jnp.where(lane == accl.shape[1] - 1, best, accl)


def forward(nx, ny, scale, *refs):
    later = refs[: nx - 1]
    same_ref, other_ref, wk_ref, state_in, full_in, pay_ref = refs[nx - 1 :]
    x, y, core = place(ny)
    head = same_ref.shape[3]
    n = later[0].shape[0]
    w2 = jnp.concatenate(halves(wk_ref[...].T), 1)
    keys0, values0 = flat(same_ref, 0), with_ones(flat(same_ref, 1))
    keys1, values1 = flat(other_ref, 0), with_ones(flat(other_ref, 1))
    state, full = add_states(keys1, flat(other_ref, 1), w2, y + core, state_in[...], full_in[...])
    feats_n = full.shape[0]
    full_high = full[:, :head].astype(BF16)
    norm = full[:, head : head + 1]
    norm_high = norm.astype(BF16).astype(F32)
    for s in range(1, nx):

        @pl.when(x + s < nx)
        def _(s=s):
            best, accl = teach(later[s - 1][...], keys0, values0, keys1, values1, scale)
            to = x + s
            total = accl[:, head : head + 1]
            high = total.astype(BF16).astype(F32)
            pay_ref[to, :n] = accl[:, :head].astype(BF16)
            pay_ref[to, n : n + feats_n] = full_high
            pay_ref[to, n + feats_n :] = to_rows(
                [best, high, total - high, norm_high, norm - norm_high], head
            ).astype(BF16)

    for d in range(nx):

        @pl.when(d < x)
        def _(d=d):
            pay_ref[d] = jnp.zeros(pay_ref.shape[1:], BF16)

    high, low = halves(state[:, :head])
    norm = state[:, head : head + 1]
    norm_high = norm.astype(BF16).astype(F32)
    zero = jnp.zeros_like(norm)
    pay_ref[x, :feats_n] = low
    pay_ref[x, n : n + feats_n] = high
    pay_ref[x, n + feats_n :] = to_rows([zero, zero, zero, norm_high, norm - norm_high], head).astype(BF16)


def merge(
    nx, ny, scale, count,
    accl_in, got_ref, fq_ref, near_ref,
    out_ref, dnum_ref, dden_ref, state_ref, back_ref, pay_ref, loss_ref,
):
    x, _, _ = place(ny)
    n, feats_n = fq_ref.shape
    head = out_ref.shape[1]
    c = scale * LOG2E
    columns = to_columns([got_ref[d, n + feats_n :].astype(F32) for d in range(nx)], head)
    bests = [accl_in[:, 2 * head - 1 :]]
    for d in range(nx):
        bests.append(jnp.where(d < x, columns[:, 8 * d : 8 * d + 1], -1e30))
    best = functools.reduce(jnp.maximum, bests)
    factor = jnp.exp2((bests[0] - best) * c)
    accl = accl_in[...] * factor
    acc, total = accl[:, :head], accl[:, head : head + 1]
    state, norm = got_ref[x, :feats_n].astype(F32), jnp.zeros((feats_n, 1), F32)
    for d in range(nx):
        factor = jnp.where(d < x, jnp.exp2((bests[d + 1] - best) * c), 0.0)
        acc += got_ref[d, :n].astype(F32) * factor
        total += (columns[:, 8 * d + 1 : 8 * d + 2] + columns[:, 8 * d + 2 : 8 * d + 3]) * factor
        state += got_ref[d, n : n + feats_n].astype(F32)
        norm += columns[:, 8 * d + 3 : 8 * d + 4] + columns[:, 8 * d + 4 : 8 * d + 5]
    state = jnp.concatenate([state, jnp.broadcast_to(norm, state.shape)], 1)
    state_ref[...] = state
    targets = (acc / total).astype(BF16).astype(F32)
    fq = fq_ref[...]
    numden = dot3(fq, state) + near_ref[...]
    den = numden[:, head:]
    outs = numden[:, :head] / den
    out_ref[...] = outs.astype(BF16)
    diff = outs - targets
    loss_ref[...] = jnp.full(loss_ref.shape, jnp.sum(diff * diff) / count, F32)
    grad_out = diff * (2.0 / count)
    d_num = grad_out / den
    d_den = -jnp.sum(grad_out * outs, -1, keepdims=True) / den
    dnum_ref[...] = d_num
    dden_ref[...] = d_den
    back = dot3(fq.T, jnp.concatenate([d_num, d_den], 1))
    back_ref[...] = back
    norm = back[:, head : head + 1]
    nh = norm.astype(BF16).astype(F32)
    rows = to_rows([nh, norm - nh], head).astype(BF16)
    for d in range(nx):
        pay_ref[d, :feats_n] = back[:, :head].astype(BF16)
        pay_ref[d, feats_n:] = rows


def near_grads(q_ref, k_ref, v_ref, wq_ref, wk_ref, dnum_ref, dden_ref, state_ref, grads_ref):
    q, kd, vd = q_ref[...], k_ref[...], v_ref[...]
    head, rows = kd.shape[1], kd.shape[0]
    d_num, d_den = dnum_ref[...], dden_ref[...]
    fq_t, sig_q, fk_t, sig_d = own_features(q, kd, wq_ref[...], wk_ref[...])
    d_attn = jnp.where(diagonal(q.shape[0], rows), dot2(d_num, vd, NT) + d_den[:, :rows], 0.0)
    lane = lax.broadcasted_iota(jnp.int32, d_den.shape, 1)
    d_aug = jnp.concatenate([d_num, jnp.where(lane == 0, d_den, 0.0)], 1)
    d_fq = dot3(state_ref[...], d_aug, NT) + dot3(fk_t, d_attn, NT)
    d_pre = d_fq[:head] * sig_q - d_fq[head:] * (1.0 - sig_q)
    grads_ref[:head] = dot2(d_pre, q)
    d_fk = dot3(fq_t, d_attn)
    d_pre = d_fk[:head] * sig_d - d_fk[head:] * (1.0 - sig_d)
    grads_ref[head:] = dot2(d_pre, kd)


def backward(
    nx, ny,
    same_ref, other_ref, wk_ref, back_in, got_ref, near_ref, loss_ref,
    grad_ref, sum_ref,
):
    x, y, core = place(ny)
    rows, head = same_ref.shape[2], same_ref.shape[3]
    keys_n = ny * rows
    feats_n = back_in.shape[0]
    columns = to_columns([got_ref[d, feats_n:].astype(F32) for d in range(nx)], head)
    after, norm = jnp.zeros((feats_n, head), F32), jnp.zeros((feats_n, 1), F32)
    for d in range(nx):
        counts = (d > x).astype(F32)
        after += got_ref[d, :feats_n].astype(F32) * counts
        norm += (columns[:, 8 * d : 8 * d + 1] + columns[:, 8 * d + 1 : 8 * d + 2]) * counts

    def both(state, norm):
        mats = jnp.concatenate([state[:head] + state[head:], state[head:]], 0)
        norms = jnp.concatenate([norm[:head] + norm[head:], norm[head:]], 0)
        return jnp.concatenate(halves(mats), 1), norms

    own2, own_n = both(back_in[:, :head], back_in[:, head : head + 1])
    after2, after_n = both(after, norm)
    two = jnp.concatenate([own2, after2], 0)
    key = lax.broadcasted_iota(jnp.int32, (1, keys_n), 1)
    w2 = jnp.concatenate(halves(wk_ref[...].T), 1)
    total = near_ref[head:]
    for half, ref in enumerate((same_ref, other_ref)):
        z = dot(two, pair(flat(ref, 1)), NT)
        d = jnp.where(key < (y + half * core) * rows, z[: 2 * head] + own_n, 0.0) + (z[2 * head :] + after_n)
        _, _, sig = feature_parts(dot(w2, pair(flat(ref, 0)), NT))
        total += dot2(sig * d[:head] - d[head:], flat(ref, 0))
    sum_ref[:head] = near_ref[:head].T
    sum_ref[head:] = total.T
    chunks = grad_ref.shape[0] - 2 * head
    parts = 2 * head // chunks
    for r in range(parts):
        grad_ref[pl.ds(r, chunks, stride=parts + 1), :] = sum_ref[pl.ds(r, chunks, stride=parts), :]
    grad_ref[pl.ds(parts, chunks, stride=parts + 1), :] = jnp.broadcast_to(loss_ref[0:1], (chunks, head))


VMEM = pl.BlockSpec(memory_space=pltpu.VMEM)
PARAMS = pltpu.CompilerParams(vmem_limit_bytes=20 * 1024 * 1024)


def spread(a, axis):
    copies = jnp.broadcast_to(a[None], (lax.axis_size(axis), *a.shape))
    return lax.all_to_all(copies, axis, 0, 0, tiled=True)


def shards(nx, ny, queries, keys, values, w_query, w_key):
    rows, groups, per, head = queries.shape
    n_ctx, n_kvh = lax.axis_size("ctx"), lax.axis_size("kvh")
    scale = head**-0.5
    count = float(rows * n_ctx * groups * n_kvh * per)
    at = lambda x, y, c: (x * ny + y) * CORES + c
    every = [(x, y, c) for x in range(nx) for y in range(ny) for c in range(CORES)]
    y_groups = [[at(x, y, c) for y in range(ny)] for x in range(nx) for c in range(CORES)]
    x_groups = [[at(x, y, c) for x in range(nx)] for y in range(ny) for c in range(CORES)]
    swap = [(at(x, y, c), at(x, y, 1 - c)) for x, y, c in every]
    n, feats, keys_n = rows * per, 2 * head, ny * rows
    f32 = lambda *shape: jax.ShapeDtypeStruct(shape, F32)
    bf16 = lambda *shape: jax.ShapeDtypeStruct(shape, BF16)

    def call(body, outs, args, scratch=(), flops=1, name=None):
        return pl.pallas_call(
            body,
            out_shape=outs,
            in_specs=[VMEM] * len(args),
            out_specs=jax.tree.map(lambda _: VMEM, outs),
            scratch_shapes=list(scratch),
            compiler_params=PARAMS,
            cost_estimate=pl.CostEstimate(
                flops=flops * 1_000_000_000, bytes_accessed=20_000_000, transcendentals=flops * 300_000
            ),
            name=name,
        )(*args)

    q = queries.reshape(n, head)
    k, v = keys.reshape(rows, head), values.reshape(rows, head)
    kvs = jnp.broadcast_to(jnp.stack([k, v])[None], (ny, 2, rows, head))
    same = lax.all_to_all(kvs, "ctx", 0, 0, tiled=True, axis_index_groups=y_groups)
    later = [
        lax.ppermute(q, "ctx", [(at(x, y, c), at(x - s, y, c)) for x, y, c in every if x >= s])
        for s in range(1, nx)
    ]
    own = call(
        prepare,
        (f32(n, feats), f32(n, feats)), (q, k, v, w_query, w_key), flops=2, name="prepare",
    )
    same, later, (fq, near) = lax.optimization_barrier((same, later, own))
    other = lax.ppermute(same, "ctx", swap)
    state, full = call(
        functools.partial(same_core, ny),
        (f32(feats, feats), f32(feats, feats)), (same, w_key), flops=2, name="same_core",
    )
    pay = call(
        functools.partial(forward, nx, ny, scale),
        bf16(nx, n + feats + 16, head),
        (*later, same, other, w_key, state, full), flops=6, name="forward",
    )
    got = lax.all_to_all(pay, "ctx", 0, 0, tiled=True, axis_index_groups=x_groups)
    accl = call(
        functools.partial(own_teacher, ny, scale), f32(n, feats), (q, same, other), flops=2, name="own_teacher",
    )
    out, dnum, dden, state, back, pay, loss = call(
        functools.partial(merge, nx, ny, scale, count),
        (bf16(n, head), f32(n, head), f32(n, head), f32(feats, feats), f32(feats, feats), bf16(nx, feats + 16, head), f32(8, head)),
        (accl, got, fq, near), flops=2, name="merge",
    )
    got = lax.all_to_all(pay, "ctx", 0, 0, tiled=True, axis_index_groups=x_groups)
    grads = call(
        near_grads, f32(feats, head), (q, k, v, w_query, w_key, dnum, dden, state), flops=2, name="near_grads",
    )
    parts = feats // n_ctx
    grads = call(
        functools.partial(backward, nx, ny),
        f32(n_ctx * (parts + 1), head),
        (same, other, w_key, back, got, grads, loss),
        scratch=(pltpu.VMEM((feats, head), F32),), flops=4, name="backward",
    )
    mine = lax.all_to_all(grads.reshape(n_ctx, 1, -1), "ctx", 0, 0, tiled=True).sum(0)
    mine = spread(mine, "kvh").sum(0)
    g = spread(mine[:, : parts * head], "ctx").reshape(2, head, head)
    return out.reshape(queries.shape), g[0], g[1], mine[0, parts * head]


def solution(mesh):
    n_ctx = mesh.shape["ctx"]
    ny = min(8, n_ctx // CORES)
    nx = n_ctx // (CORES * ny)
    placed = (P("ctx", "kvh", None, None), P("ctx", "kvh", None), P("ctx", "kvh", None), P(), P())
    return jax.shard_map(
        functools.partial(shards, nx, ny),
        mesh=mesh,
        in_specs=placed,
        out_specs=(P("ctx", "kvh", None, None), P(), P(), P()),
        check_vma=False,
    )
```

time: 118 us -> 117 us (level)
  blocking collectives: 44.8 us -> 32.7 us
  waiting for transfers between devices: 23.5 us -> 32.5 us
  starting transfers between devices: 27.6 us -> 31.1 us
  local copies, waits for them, and re-layouts: 5.84 us -> 2.83 us
  Pallas kernels: 13.4 us -> 15.5 us
    all_to_all x2 -> x1, blocking collectives: 28.3 us -> 16.5 us  [spread(): return lax.all_to_all(copies, axis, 0, 0, tiled=True)]
    all_to_all x1 -> x2, waiting for transfers between devices: 4.48 us -> 12.1 us  [shards(): lax.all_to_all(pay, 'ctx', 0, 0, tiled=True, axis_index_groups=x_groups)]
    all_to_all x1 -> x2, starting transfers between devices: 3.58 us -> 7.1 us  [shards(): lax.all_to_all(pay, 'ctx', 0, 0, tiled=True, axis_index_groups=x_groups)]
    unnamed x26 -> x10, local copies, waits for them, and re-layouts: 3.02 us -> 0.02 us
    pallas_call x6 -> x7, Pallas kernels: 13.4 us -> 15.5 us  [call(): pl.pallas_call(body, out_shape=outs, in_specs=[VMEM] * len(args), out_spe...]
    ppermute x3, waiting for transfers between devices: 1.77 us -> 3.11 us  [shards(): lax.ppermute(q, 'ctx', [(at(x, y, c), at(x - s, y, c)) for x, y, c in eve...]
  transfers between devices with their start and end apart: 7 -> 8, of which waited for: 7 -> 8; matrix products, arithmetic and copies ran while one was open for 0% -> 0% of each run, Pallas kernels for 3% -> 4%
where the time goes in v5:
time: 117 us; the launch traced here: 116 us
  blocking collectives  32.7 us (28%)
  waiting for transfers between devices  32.5 us (28%)
  starting transfers between devices  31.1 us (27%)
  Pallas kernels  15.5 us (13%)
  local copies, waits for them, and re-layouts  2.83 us (2%)
    all_to_all x1, blocking collectives, spread(): return lax.all_to_all(copies, axis, 0, 0, tiled=True)  16.5 us
    all_to_all x1, blocking collectives, shards(): lax.all_to_all(grads.reshape(n_ctx, 1, -1), 'ctx', 0, 0, tiled=True).sum(0)  16.3 us
    pallas_call x7, Pallas kernels, call(): pl.pallas_call(body, out_shape=outs, in_specs=[VMEM] * len(args), out_spe...  15.5 us
    all_to_all x2, waiting for transfers between devices, shards(): lax.all_to_all(pay, 'ctx', 0, 0, tiled=True, axis_index_groups=x_groups)  12.1 us
    all_to_all x1, waiting for transfers between devices, spread(): return lax.all_to_all(copies, axis, 0, 0, tiled=True)  9.85 us
    all_to_all x1, starting transfers between devices, shards(): lax.all_to_all(kvs, 'ctx', 0, 0, tiled=True, axis_index_groups=y_groups)  7.79 us
    all_to_all x2, starting transfers between devices, shards(): lax.all_to_all(pay, 'ctx', 0, 0, tiled=True, axis_index_groups=x_groups)  7.1 us
    all_to_all x1, waiting for transfers between devices, shards(): lax.all_to_all(kvs, 'ctx', 0, 0, tiled=True, axis_index_groups=y_groups)  6.84 us
  transfers between devices with their start and end apart: 8, of which 8 were waited for; matrix products, arithmetic and copies ran while one was open for 0% of the time, Pallas kernels for 4%

profile of v5, /device:TPU:1, one launch (start us, length us, event | category | flops | bytes accessed | tf_op | source)
XLA Modules:
  0.0 116.4 jit_solution(3853269439778727376)
XLA Ops:
  1.4 0.9 broadcast_in_dim.8
  2.3 7.8 %all-to-all-start = ((bf16[8,2,128,128]{3,2,1,0:T(8,128)(2,1)}), bf16[8,2,128,128]{3,2,1,0:T(8,128)(2,1)S(1)}, u32[]{:S(2)}, u32[]{:S(2)}) async-start(bf16[8,2,128,128]{3,2,1,0:T(8,128)(2,1)} %broadcast_in_dim.8), calls=%async_computation | async-start | bytes 1048576 | tf_op jit(solution)/shard_map/all_to_all | solution.py:345
  10.1 1.3 %collective-permute-start.2 = (bf16[256,128]{1,0:T(8,128)(2,1)S(1)}, bf16[256,128]{1,0:T(8,128)(2,1)S(1)}, u32[]{:S(2)}, u32[]{:S(2)}) collective-permute-start(bf16[256,128]{1,0:T(8,128)(2,1)S(1)} %bitcast.20), channel_id=1, source_target_pairs={{384,0},{392,8},{400,16},{408,24},{416,32},{424,40},{432,48},{440,... | collective-permute-start | bytes 196616 | tf_op jit(solution)/shard_map/ppermute | solution.py:347
  11.4 1.3 %collective-permute-start.1 = (bf16[256,128]{1,0:T(8,128)(2,1)S(1)}, bf16[256,128]{1,0:T(8,128)(2,1)S(1)}, u32[]{:S(2)}, u32[]{:S(2)}) collective-permute-start(bf16[256,128]{1,0:T(8,128)(2,1)S(1)} %bitcast.21), channel_id=1, source_target_pairs={{256,0},{264,8},{272,16},{280,24},{288,32},{296,40},{304,48},{312,... | collective-permute-start | bytes 196616 | tf_op jit(solution)/shard_map/ppermute | solution.py:347
  12.7 1.3 %collective-permute-start = (bf16[256,128]{1,0:T(8,128)(2,1)S(1)}, bf16[256,128]{1,0:T(8,128)(2,1)S(1)}, u32[]{:S(2)}, u32[]{:S(2)}) collective-permute-start(bf16[256,128]{1,0:T(8,128)(2,1)S(1)} %bitcast.22), channel_id=1, source_target_pairs={{128,0},{136,8},{144,16},{152,24},{160,32},{168,40},{176,48},{184,... | collective-permute-start | bytes 196616 | tf_op jit(solution)/shard_map/ppermute | solution.py:347
  14.1 0.8 prepare.1
  14.9 1.4 %collective-permute-done.2.refs_2_ = bf16[256,128]{1,0:T(8,128)(2,1)S(1)} collective-permute-done((bf16[256,128]{1,0:T(8,128)(2,1)S(1)}, bf16[256,128]{1,0:T(8,128)(2,1)S(1)}, u32[]{:S(2)}, u32[]{:S(2)}) %collective-permute-start.2) | collective-permute-done | bytes 65568 | tf_op jit(solution)/shard_map/ppermute | solution.py:347
  16.3 1.6 %collective-permute-done.1.refs_1_ = bf16[256,128]{1,0:T(8,128)(2,1)S(1)} collective-permute-done((bf16[256,128]{1,0:T(8,128)(2,1)S(1)}, bf16[256,128]{1,0:T(8,128)(2,1)S(1)}, u32[]{:S(2)}, u32[]{:S(2)}) %collective-permute-start.1) | collective-permute-done | bytes 65568 | tf_op jit(solution)/shard_map/ppermute | solution.py:347
  18.0 6.8 %all-to-all-done.same_ref.refs_3_ = bf16[8,2,128,128]{3,2,1,0:T(8,128)(2,1)S(1)} async-done(((bf16[8,2,128,128]{3,2,1,0:T(8,128)(2,1)}), bf16[8,2,128,128]{3,2,1,0:T(8,128)(2,1)S(1)}, u32[]{:S(2)}, u32[]{:S(2)}) %all-to-all-start) | async-done | bytes 524320 | tf_op jit(solution)/shard_map/all_to_all | solution.py:345
  24.9 5.6 %collective-permute-start.3 = (bf16[8,2,128,128]{3,2,1,0:T(8,128)(2,1)S(1)}, bf16[8,2,128,128]{3,2,1,0:T(8,128)(2,1)S(1)}, u32[]{:S(2)}, u32[]{:S(2)}) collective-permute-start(bf16[8,2,128,128]{3,2,1,0:T(8,128)(2,1)S(1)} %all-to-all-done.same_ref.refs_3_), channel_id=1, source_target_pairs={{0,8},{8,0},{16,24},{24,16},{32,40},{40,32},{48,56},{56,48},{64,72... | collective-permute-start | bytes 1572872 | tf_op jit(solution)/shard_map/ppermute | solution.py:355
  30.5 0.9 same_core.1
  32.0 6.4 %forward.1 = bf16[4,528,128]{2,1,0:T(8,128)(2,1)} custom-call(bf16[256,128]{1,0:T(8,128)(2,1)S(1)} %collective-permute-done.refs_0_, bf16[256,128]{1,0:T(8,128)(2,1)S(1)} %collective-permute-done.1.refs_1_, bf16[256,128]{1,0:T(8,128)(2,1)S(1)} %collective-permute-done.2.refs_2_, bf16[8,2,128,128]{3,2,1,0:T(8,128)(2,1)S(1)} %all-to-all-done.same_ref.refs_3_, ...), custom_call_target="tpu_custom_call" | custom-call | flops 6000000000 | bytes 20000000 | tf_op jit(solution)/shard_map/forward/pallas_call | solution.py:329
  38.4 3.5 %all-to-all-start.1 = ((bf16[4,528,128]{2,1,0:T(8,128)(2,1)}), bf16[4,528,128]{2,1,0:T(8,128)(2,1)S(1)}, u32[]{:S(2)}, u32[]{:S(2)}) async-start(bf16[4,528,128]{2,1,0:T(8,128)(2,1)} %forward.1), calls=%async_computation.1 | async-start | bytes 1081344 | tf_op jit(solution)/shard_map/all_to_all | solution.py:365
  41.9 1.5 %own_teacher.1.accl_in = f32[256,256]{1,0:T(8,128)S(1)} custom-call(bf16[256,128]{1,0:T(8,128)(2,1)S(1)} %bitcast.24, bf16[8,2,128,128]{3,2,1,0:T(8,128)(2,1)S(1)} %all-to-all-done.same_ref.refs_3_, bf16[8,2,128,128]{3,2,1,0:T(8,128)(2,1)S(1)} %collective-permute-done.3.other_ref.refs_4_), custom_call_target="tpu_custom_call" | custom-call | flops 2000000000 | bytes 20000000 | tf_op jit(solution)/shard_map/own_teacher/pallas_call | solution.py:329
  43.4 7.9 %all-to-all-done.1.got_ref = bf16[4,528,128]{2,1,0:T(8,128)(2,1)S(1)} async-done(((bf16[4,528,128]{2,1,0:T(8,128)(2,1)}), bf16[4,528,128]{2,1,0:T(8,128)(2,1)S(1)}, u32[]{:S(2)}, u32[]{:S(2)}) %all-to-all-start.1) | async-done | bytes 540704 | tf_op jit(solution)/shard_map/all_to_all | solution.py:365
  51.3 2.7 %merge.1 = (bf16[256,128]{1,0:T(8,128)(2,1)}, f32[256,128]{1,0:T(8,128)S(1)}, f32[256,128]{1,0:T(8,128)S(1)}, f32[256,256]{1,0:T(8,128)S(1)}, f32[256,256]{1,0:T...) custom-call(f32[256,256]{1,0:T(8,128)S(1)} %own_teacher.1.accl_in, ...), custom_call_target="tpu_custom_call" | custom-call | flops 2000000000 | bytes 20000000 | tf_op jit(solution)/shard_map/merge/pallas_call | solution.py:329
  54.0 3.6 %all-to-all-start.2 = ((bf16[4,272,128]{2,1,0:T(8,128)(2,1)}), bf16[4,272,128]{2,1,0:T(8,128)(2,1)S(1)}, u32[]{:S(2)}, u32[]{:S(2)}) async-start(bf16[4,272,128]{2,1,0:T(8,128)(2,1)} %get-tuple-element.33), calls=%async_computation.2 | async-start | bytes 557056 | tf_op jit(solution)/shard_map/all_to_all | solution.py:374
  57.6 1.2 %near_grads.1.near_ref = f32[256,128]{1,0:T(8,128)S(1)} custom-call(bf16[256,128]{1,0:T(8,128)(2,1)S(1)} %bitcast.25, bf16[128,128]{1,0:T(8,128)(2,1)S(1)} %bitcast.19, bf16[128,128]{1,0:T(8,128)(2,1)S(1)} %bitcast.16, f32[128,128]{1,0:T(8,128)S(1)} %copy-done.3, f32[128,128]{1,0:T(8,128)S(1)} %copy-done.4, f32[256,128]{1,0:T(8,128)S(1)} %get-tuple-element.34.dnum_ref, ...), custom_call_target="tpu_custom_call" | custom-call | flops 2000000000 | bytes 20000000 | tf_op jit(solution)/shard_map/near_grads/pallas_call | solution.py:329
  58.8 4.2 %all-to-all-done.2.got_ref = bf16[4,272,128]{2,1,0:T(8,128)(2,1)S(1)} async-done(((bf16[4,272,128]{2,1,0:T(8,128)(2,1)}), bf16[4,272,128]{2,1,0:T(8,128)(2,1)S(1)}, u32[]{:S(2)}, u32[]{:S(2)}) %all-to-all-start.2) | async-done | bytes 278560 | tf_op jit(solution)/shard_map/all_to_all | solution.py:374
  63.0 1.9 %backward.1 = f32[320,128]{1,0:T(8,128)S(1)} custom-call(bf16[8,2,128,128]{3,2,1,0:T(8,128)(2,1)S(1)} %all-to-all-done.same_ref.refs_3_, bf16[8,2,128,128]{3,2,1,0:T(8,128)(2,1)S(1)} %collective-permute-done.3.other_ref.refs_4_, f32[128,128]{1,0:T(8,128)S(1)} %copy-done.4, f32[256,256]{1,0:T(8,128)S(1)} %get-tuple-element.32.back_in, ...), custom_call_target="tpu_custom_call" | custom-call | flops 4000000000 | bytes 20000000 | tf_op jit(solution)/shard_map/backward/pallas_call | solution.py:329
  65.0 16.3 %all_to_all.30 = f32[64,1,640]{2,1,0:T(1,128)S(1)} all-to-all(f32[64,1,640]{2,1,0:T(1,128)S(1)} %bitcast.13), channel_id=1, replica_groups=mesh['ctx'=64,'kvh'=8] {'ctx'}, dimensions={0} | all-to-all | bytes 327680 | tf_op jit(solution)/shard_map/all_to_all | solution.py:385
  81.4 16.5 %all_to_all.31 = f32[8,1,640]{2,1,0:T(1,128)S(1)} all-to-all(f32[8,1,640]{2,1,0:T(1,128)S(1)} %broadcast_in_dim.9), channel_id=1, replica_groups=mesh['ctx'=64,'kvh'=8] {'kvh'}, dimensions={0} | all-to-all | bytes 40960 | tf_op jit(solution)/shard_map/all_to_all | solution.py:311
  98.6 6.8 %all-to-all-start.5 = ((f32[64,1,512]{2,1,0:T(1,128)}), f32[64,1,512]{2,1,0:T(1,128)S(1)}, u32[]{:S(2)}, u32[]{:S(2)}) async-start(f32[64,1,512]{2,1,0:T(1,128)} %broadcast_in_dim.11), calls=%async_computation.5 | async-start | bytes 262144 | tf_op jit(solution)/shard_map/all_to_all | solution.py:311
  105.9 9.8 %all-to-all-done.5 = f32[64,1,512]{2,1,0:T(1,128)S(1)} async-done(((f32[64,1,512]{2,1,0:T(1,128)}), f32[64,1,512]{2,1,0:T(1,128)S(1)}, u32[]{:S(2)}, u32[]{:S(2)}) %all-to-all-start.5) | async-done | bytes 131104 | tf_op jit(solution)/shard_map/all_to_all | solution.py:311
  (21 shorter events, 3.6 us)
Async XLA Ops:
  2.3 7.8 %copy-start.2 = (bf16[128,1,2,128]{3,2,1,0:T(2,128)(2,1)S(1)}, bf16[128,1,2,128]{3,2,1,0:T(2,128)(2,1)}, u32[]{:S(2)}) copy-start(bf16[128,1,2,128]{3,2,1,0:T(2,128)(2,1)} %param.5) | copy-start | bytes 196612
  2.3 11.7 %copy-start = (bf16[128,1,128]{2,0,1:T(8,128)(2,1)S(1)}, bf16[128,1,128]{2,0,1:T(8,128)(2,1)}, u32[]{:S(2)}) copy-start(bf16[128,1,128]{2,0,1:T(8,128)(2,1)} %param.7) | copy-start | bytes 98308
  2.3 11.7 %copy-start.1 = (bf16[128,1,128]{2,0,1:T(8,128)(2,1)S(1)}, bf16[128,1,128]{2,0,1:T(8,128)(2,1)}, u32[]{:S(2)}) copy-start(bf16[128,1,128]{2,0,1:T(8,128)(2,1)} %param.6) | copy-start | bytes 98308
  2.3 11.7 %copy-start.3 = (f32[128,128]{1,0:T(8,128)S(1)}, f32[128,128]{1,0:T(8,128)}, u32[]{:S(2)}) copy-start(f32[128,128]{1,0:T(8,128)} %wq_ref.3) | copy-start | bytes 196612
  2.3 11.7 %copy-start.4 = (f32[128,128]{1,0:T(8,128)S(1)}, f32[128,128]{1,0:T(8,128)}, u32[]{:S(2)}) copy-start(f32[128,128]{1,0:T(8,128)} %wk_ref.7) | copy-start | bytes 196612
  2.3 22.5 %all-to-all-start = ((bf16[8,2,128,128]{3,2,1,0:T(8,128)(2,1)}), bf16[8,2,128,128]{3,2,1,0:T(8,128)(2,1)S(1)}, u32[]{:S(2)}, u32[]{:S(2)}) async-start(bf16[8,2,128,128]{3,2,1,0:T(8,128)(2,1)} %broadcast_in_dim.8), calls=%async_computation | async-start | bytes 1048576 | tf_op jit(solution)/shard_map/all_to_all | solution.py:345
  10.1 6.2 %collective-permute-start.2 = (bf16[256,128]{1,0:T(8,128)(2,1)S(1)}, bf16[256,128]{1,0:T(8,128)(2,1)S(1)}, u32[]{:S(2)}, u32[]{:S(2)}) collective-permute-start(bf16[256,128]{1,0:T(8,128)(2,1)S(1)} %bitcast.20), channel_id=1, source_target_pairs={{384,0},{392,8},{400,16},{408,24},{416,32},{424,40},{432,48},{440,... | collective-permute-start | bytes 196616 | tf_op jit(solution)/shard_map/ppermute | solution.py:347
  11.4 6.5 %collective-permute-start.1 = (bf16[256,128]{1,0:T(8,128)(2,1)S(1)}, bf16[256,128]{1,0:T(8,128)(2,1)S(1)}, u32[]{:S(2)}, u32[]{:S(2)}) collective-permute-start(bf16[256,128]{1,0:T(8,128)(2,1)S(1)} %bitcast.21), channel_id=1, source_target_pairs={{256,0},{264,8},{272,16},{280,24},{288,32},{296,40},{304,48},{312,... | collective-permute-start | bytes 196616 | tf_op jit(solution)/shard_map/ppermute | solution.py:347
  12.7 5.3 %collective-permute-start = (bf16[256,128]{1,0:T(8,128)(2,1)S(1)}, bf16[256,128]{1,0:T(8,128)(2,1)S(1)}, u32[]{:S(2)}, u32[]{:S(2)}) collective-permute-start(bf16[256,128]{1,0:T(8,128)(2,1)S(1)} %bitcast.22), channel_id=1, source_target_pairs={{128,0},{136,8},{144,16},{152,24},{160,32},{168,40},{176,48},{184,... | collective-permute-start | bytes 196616 | tf_op jit(solution)/shard_map/ppermute | solution.py:347
  24.9 7.1 %collective-permute-start.3 = (bf16[8,2,128,128]{3,2,1,0:T(8,128)(2,1)S(1)}, bf16[8,2,128,128]{3,2,1,0:T(8,128)(2,1)S(1)}, u32[]{:S(2)}, u32[]{:S(2)}) collective-permute-start(bf16[8,2,128,128]{3,2,1,0:T(8,128)(2,1)S(1)} %all-to-all-done.same_ref.refs_3_), channel_id=1, source_target_pairs={{0,8},{8,0},{16,24},{24,16},{32,40},{40,32},{48,56},{56,48},{64,72... | collective-permute-start | bytes 1572872 | tf_op jit(solution)/shard_map/ppermute | solution.py:355
  38.4 12.8 %all-to-all-start.1 = ((bf16[4,528,128]{2,1,0:T(8,128)(2,1)}), bf16[4,528,128]{2,1,0:T(8,128)(2,1)S(1)}, u32[]{:S(2)}, u32[]{:S(2)}) async-start(bf16[4,528,128]{2,1,0:T(8,128)(2,1)} %forward.1), calls=%async_computation.1 | async-start | bytes 1081344 | tf_op jit(solution)/shard_map/all_to_all | solution.py:365
  54.0 9.0 %all-to-all-start.2 = ((bf16[4,272,128]{2,1,0:T(8,128)(2,1)}), bf16[4,272,128]{2,1,0:T(8,128)(2,1)S(1)}, u32[]{:S(2)}, u32[]{:S(2)}) async-start(bf16[4,272,128]{2,1,0:T(8,128)(2,1)} %get-tuple-element.33), calls=%async_computation.2 | async-start | bytes 557056 | tf_op jit(solution)/shard_map/all_to_all | solution.py:374
  98.6 17.1 %all-to-all-start.5 = ((f32[64,1,512]{2,1,0:T(1,128)}), f32[64,1,512]{2,1,0:T(1,128)S(1)}, u32[]{:S(2)}, u32[]{:S(2)}) async-start(f32[64,1,512]{2,1,0:T(1,128)} %broadcast_in_dim.11), calls=%async_computation.5 | async-start | bytes 262144 | tf_op jit(solution)/shard_map/all_to_all | solution.py:311

commit v6 on v5

--- a/solution.py
+++ b/solution.py
@@ -69,14 +69,18 @@
     )
 
 
-def to_rows(columns, head):
-    n = columns[0].shape[0]
+def to_rows(pages, head):
+    n = pages[0][0].shape[0]
     lane = lax.broadcasted_iota(jnp.int32, (n, head), 1)
     wide = jnp.zeros((n, head), F32)
-    for i, c in enumerate(columns):
-        wide = jnp.where(lane == i, c, wide)
-    rows = wide.T[:8]
-    return jnp.concatenate([rows[:, k : k + head] for k in range(0, n, head)], 0)
+    for p, columns in enumerate(pages):
+        for i, c in enumerate(columns):
+            wide = jnp.where(lane == 8 * p + i, c, wide)
+    rows = wide.T
+    return [
+        jnp.concatenate([rows[8 * p : 8 * p + 8, k : k + head] for k in range(0, n, head)], 0).astype(BF16)
+        for p in range(len(pages))
+    ]
 
 
 def to_columns(pages, head):
@@ -85,6 +89,18 @@
     ]
     rows += [rows[0]] * (head // 8 - len(rows))
     return jnp.concatenate(rows, 0).T
+
+
+def copies(k_ref, v_ref, out_ref, sems):
+    moves = [
+        pltpu.make_async_copy(ref, out_ref.at[d, i], sems.at[d, i])
+        for d in range(out_ref.shape[0])
+        for i, ref in enumerate((k_ref, v_ref))
+    ]
+    for move in moves:
+        move.start()
+    for move in moves:
+        move.wait()
 
 
 def own_features(q, k, wq, wk):
@@ -118,13 +134,6 @@
     return part, whole
 
 
-def same_core(ny, same_ref, wk_ref, state_ref, full_ref):
-    _, y, _ = place(ny)
-    w2 = jnp.concatenate(halves(wk_ref[...].T), 1)
-    zero = jnp.zeros(state_ref.shape, F32)
-    state_ref[...], full_ref[...] = add_states(flat(same_ref, 0), flat(same_ref, 1), w2, y, zero, zero)
-
-
 def teach(q, keys0, values0, keys1, values1, scale, masks=None):
     scores0, scores1 = dot(q, keys0, NT), dot(q, keys1, NT)
     if masks is not None:
@@ -153,47 +162,74 @@
     accl_ref[...] = jnp.where(lane == accl.shape[1] - 1, best, accl)
 
 
+def partial_softmax(q, keys, values1, c):
+    scores = dot(q, keys, NT)
+    best = scores.max(-1, keepdims=True).astype(BF16).astype(F32)
+    return best, dot(jnp.exp2((scores - best) * c).astype(BF16), values1)
+
+
+def same_core(nx, ny, scale, *refs):
+    later = refs[: nx - 1]
+    same_ref, wk_ref, state_ref, full_ref, accl_ref = refs[nx - 1 :]
+    _, y, _ = place(ny)
+    w2 = jnp.concatenate(halves(wk_ref[...].T), 1)
+    zero = jnp.zeros(state_ref.shape, F32)
+    keys, vals = flat(same_ref, 0), flat(same_ref, 1)
+    state_ref[...], full_ref[...] = add_states(keys, vals, w2, y, zero, zero)
+    lane = lax.broadcasted_iota(jnp.int32, accl_ref.shape[1:], 1)
+    for s in range(nx - 1):
+        best, accl = partial_softmax(later[s][...], keys, with_ones(vals), scale * LOG2E)
+        accl_ref[s] = jnp.where(lane == accl.shape[1] - 1, best, accl)
+
+
 def forward(nx, ny, scale, *refs):
     later = refs[: nx - 1]
-    same_ref, other_ref, wk_ref, state_in, full_in, pay_ref = refs[nx - 1 :]
+    other_ref, wk_ref, state_in, full_in, accl_in, pay_ref = refs[nx - 1 :]
     x, y, core = place(ny)
-    head = same_ref.shape[3]
+    head = other_ref.shape[3]
     n = later[0].shape[0]
+    c = scale * LOG2E
     w2 = jnp.concatenate(halves(wk_ref[...].T), 1)
-    keys0, values0 = flat(same_ref, 0), with_ones(flat(same_ref, 1))
-    keys1, values1 = flat(other_ref, 0), with_ones(flat(other_ref, 1))
-    state, full = add_states(keys1, flat(other_ref, 1), w2, y + core, state_in[...], full_in[...])
+    keys, vals = flat(other_ref, 0), flat(other_ref, 1)
+    values1 = with_ones(vals)
+    state, full = add_states(keys, vals, w2, y + core, state_in[...], full_in[...])
     feats_n = full.shape[0]
     full_high = full[:, :head].astype(BF16)
-    norm = full[:, head : head + 1]
-    norm_high = norm.astype(BF16).astype(F32)
+
+    def two(column):
+        high = column.astype(BF16).astype(F32)
+        return [high, column - high]
+
+    high, low = halves(state[:, :head])
+    pay_ref[x, :feats_n] = low
+    pay_ref[x, n : n + feats_n] = high
+    zero = jnp.zeros((n, 1), F32)
+    columns = [[zero, zero, zero, *two(state[:, head : head + 1])]]
+    sums = []
+    for s in range(nx - 1):
+        best, accl = partial_softmax(later[s][...], keys, values1, c)
+        before = accl_in[s]
+        old = before[:, 2 * head - 1 :]
+        new = jnp.maximum(old, best)
+        mine, other = jnp.exp2((old - new) * c), jnp.exp2((best - new) * c)
+        sums.append((before[:, :head] * mine + accl[:, :head] * other).astype(BF16))
+        total = before[:, head : head + 1] * mine + accl[:, head : head + 1] * other
+        columns.append([new, *two(total), *two(full[:, head : head + 1])])
+    rows = to_rows(columns, head)
+    pay_ref[x, n + feats_n :] = rows[0]
     for s in range(1, nx):
 
         @pl.when(x + s < nx)
         def _(s=s):
-            best, accl = teach(later[s - 1][...], keys0, values0, keys1, values1, scale)
-            to = x + s
-            total = accl[:, head : head + 1]
-            high = total.astype(BF16).astype(F32)
-            pay_ref[to, :n] = accl[:, :head].astype(BF16)
-            pay_ref[to, n : n + feats_n] = full_high
-            pay_ref[to, n + feats_n :] = to_rows(
-                [best, high, total - high, norm_high, norm - norm_high], head
-            ).astype(BF16)
+            pay_ref[x + s, :n] = sums[s - 1]
+            pay_ref[x + s, n : n + feats_n] = full_high
+            pay_ref[x + s, n + feats_n :] = rows[s]
 
     for d in range(nx):
 
         @pl.when(d < x)
         def _(d=d):
             pay_ref[d] = jnp.zeros(pay_ref.shape[1:], BF16)
-
-    high, low = halves(state[:, :head])
-    norm = state[:, head : head + 1]
-    norm_high = norm.astype(BF16).astype(F32)
-    zero = jnp.zeros_like(norm)
-    pay_ref[x, :feats_n] = low
-    pay_ref[x, n : n + feats_n] = high
-    pay_ref[x, n + feats_n :] = to_rows([zero, zero, zero, norm_high, norm - norm_high], head).astype(BF16)
 
 
 def merge(
@@ -239,7 +275,7 @@
     back_ref[...] = back
     norm = back[:, head : head + 1]
     nh = norm.astype(BF16).astype(F32)
-    rows = to_rows([nh, norm - nh], head).astype(BF16)
+    (rows,) = to_rows([[nh, norm - nh]], head)
     for d in range(nx):
         pay_ref[d, :feats_n] = back[:, :head].astype(BF16)
         pay_ref[d, feats_n:] = rows
@@ -341,7 +377,15 @@
 
     q = queries.reshape(n, head)
     k, v = keys.reshape(rows, head), values.reshape(rows, head)
-    kvs = jnp.broadcast_to(jnp.stack([k, v])[None], (ny, 2, rows, head))
+    kvs = pl.pallas_call(
+        copies,
+        out_shape=bf16(ny, 2, rows, head),
+        in_specs=[pl.BlockSpec(memory_space=pl.ANY)] * 2,
+        out_specs=pl.BlockSpec(memory_space=pl.ANY),
+        scratch_shapes=[pltpu.SemaphoreType.DMA((ny, 2))],
+        compiler_params=pltpu.CompilerParams(vmem_limit_bytes=60 * 1024 * 1024),
+        name="copies",
+    )(k, v)
     same = lax.all_to_all(kvs, "ctx", 0, 0, tiled=True, axis_index_groups=y_groups)
     later = [
         lax.ppermute(q, "ctx", [(at(x, y, c), at(x - s, y, c)) for x, y, c in every if x >= s])
@@ -353,14 +397,14 @@
     )
     same, later, (fq, near) = lax.optimization_barrier((same, later, own))
     other = lax.ppermute(same, "ctx", swap)
-    state, full = call(
-        functools.partial(same_core, ny),
-        (f32(feats, feats), f32(feats, feats)), (same, w_key), flops=2, name="same_core",
+    state, full, sums = call(
+        functools.partial(same_core, nx, ny, scale),
+        (f32(feats, feats), f32(feats, feats), f32(nx - 1, n, feats)), (*later, same, w_key), flops=3, name="same_core",
     )
     pay = call(
         functools.partial(forward, nx, ny, scale),
         bf16(nx, n + feats + 16, head),
-        (*later, same, other, w_key, state, full), flops=6, name="forward",
+        (*later, other, w_key, state, full, sums), flops=4, name="forward",
     )
     got = lax.all_to_all(pay, "ctx", 0, 0, tiled=True, axis_index_groups=x_groups)
     accl = call(

time: 117 us -> 130 us (1.11)
  Pallas kernels: 15.5 us -> 30.6 us
    pallas_call x0 -> x1, Pallas kernels: none -> 17.1 us  [shards(): pl.pallas_call(copies, out_shape=bf16(ny, 2, rows, head), in_specs=[pl.Bl...]
    ppermute x3, waiting for transfers between devices: 3.11 us -> 6.82 us  [shards(): lax.ppermute(q, 'ctx', [(at(x, y, c), at(x - s, y, c)) for x, y, c in eve...]
    all_to_all x1, waiting for transfers between devices: 6.84 us -> 3.13 us  [shards(): lax.all_to_all(kvs, 'ctx', 0, 0, tiled=True, axis_index_groups=y_groups)]
    pallas_call x7, Pallas kernels: 15.5 us -> 13.4 us  [call(): pl.pallas_call(body, out_shape=outs, in_specs=[VMEM] * len(args), out_spe...]
  transfers between devices with their start and end apart: 8 -> 8, of which waited for: 8 -> 7; matrix products, arithmetic and copies ran while one was open for 0% -> 0% of each run, Pallas kernels for 4% -> 4%
where the time goes in v6:
time: 130 us
  blocking collectives  32.7 us (25%)
  waiting for transfers between devices  32.2 us (25%)
  starting transfers between devices  31.5 us (24%)
  Pallas kernels  30.6 us (24%)
  local copies, waits for them, and re-layouts  1.95 us (2%)
    pallas_call x1, Pallas kernels, shards(): pl.pallas_call(copies, out_shape=bf16(ny, 2, rows, head), in_specs=[pl.Bl...  17.1 us
    all_to_all x1, blocking collectives, shards(): lax.all_to_all(grads.reshape(n_ctx, 1, -1), 'ctx', 0, 0, tiled=True).sum(0)  16.9 us
    all_to_all x1, blocking collectives, spread(): return lax.all_to_all(copies, axis, 0, 0, tiled=True)  15.7 us
    pallas_call x7, Pallas kernels, call(): pl.pallas_call(body, out_shape=outs, in_specs=[VMEM] * len(args), out_spe...  13.4 us
    all_to_all x2, waiting for transfers between devices, shards(): lax.all_to_all(pay, 'ctx', 0, 0, tiled=True, axis_index_groups=x_groups)  12.4 us
    all_to_all x1, waiting for transfers between devices, spread(): return lax.all_to_all(copies, axis, 0, 0, tiled=True)  9.85 us
    all_to_all x1, starting transfers between devices, shards(): lax.all_to_all(kvs, 'ctx', 0, 0, tiled=True, axis_index_groups=y_groups)  7.79 us
    all_to_all x2, starting transfers between devices, shards(): lax.all_to_all(pay, 'ctx', 0, 0, tiled=True, axis_index_groups=x_groups)  7.45 us
  transfers between devices with their start and end apart: 8, of which 7 were waited for; matrix products, arithmetic and copies ran while one was open for 0% of the time, Pallas kernels for 4%

profile of v6, /device:TPU:1, one launch (start us, length us, event | category | flops | bytes accessed | tf_op | source)
XLA Modules:
  0.0 129.8 jit_solution(1647328538588917669)
XLA Ops:
  0.6 17.1 %copies.1 = bf16[8,2,128,128]{3,2,1,0:T(8,128)(2,1)} custom-call(bf16[128,128]{1,0:T(8,128)(2,1)} %bitcast.12, bf16[128,128]{1,0:T(8,128)(2,1)} %bitcast.15), custom_call_target="tpu_custom_call" | custom-call | tf_op jit(solution)/shard_map/copies/pallas_call | solution.py:380
  17.8 7.8 %all-to-all-start = ((bf16[8,2,128,128]{3,2,1,0:T(8,128)(2,1)}), bf16[8,2,128,128]{3,2,1,0:T(8,128)(2,1)S(1)}, u32[]{:S(2)}, u32[]{:S(2)}) async-start(bf16[8,2,128,128]{3,2,1,0:T(8,128)(2,1)} %copies.1), calls=%async_computation | async-start | bytes 1048576 | tf_op jit(solution)/shard_map/all_to_all | solution.py:389
  25.6 1.3 collective-permute-start
  26.9 1.3 collective-permute-start.1
  28.2 1.3 collective-permute-start.2
  29.6 0.8 prepare.1
  30.6 2.8 %collective-permute-done.1.refs_1_ = bf16[256,128]{1,0:T(8,128)(2,1)S(1)} collective-permute-done((bf16[256,128]{1,0:T(8,128)(2,1)S(1)}, bf16[256,128]{1,0:T(8,128)(2,1)S(1)}, u32[]{:S(2)}, u32[]{:S(2)}) %collective-permute-start.1) | collective-permute-done | bytes 65568 | tf_op jit(solution)/shard_map/ppermute | solution.py:391
  33.5 3.8 %collective-permute-done.2.refs_2_ = bf16[256,128]{1,0:T(8,128)(2,1)S(1)} collective-permute-done((bf16[256,128]{1,0:T(8,128)(2,1)S(1)}, bf16[256,128]{1,0:T(8,128)(2,1)S(1)}, u32[]{:S(2)}, u32[]{:S(2)}) %collective-permute-start.2) | collective-permute-done | bytes 65568 | tf_op jit(solution)/shard_map/ppermute | solution.py:391
  37.2 3.1 %all-to-all-done.same_ref.refs_3_ = bf16[8,2,128,128]{3,2,1,0:T(8,128)(2,1)S(1)} async-done(((bf16[8,2,128,128]{3,2,1,0:T(8,128)(2,1)}), bf16[8,2,128,128]{3,2,1,0:T(8,128)(2,1)S(1)}, u32[]{:S(2)}, u32[]{:S(2)}) %all-to-all-start) | async-done | bytes 524320 | tf_op jit(solution)/shard_map/all_to_all | solution.py:389
  40.4 5.6 %collective-permute-start.3 = (bf16[8,2,128,128]{3,2,1,0:T(8,128)(2,1)S(1)}, bf16[8,2,128,128]{3,2,1,0:T(8,128)(2,1)S(1)}, u32[]{:S(2)}, u32[]{:S(2)}) collective-permute-start(bf16[8,2,128,128]{3,2,1,0:T(8,128)(2,1)S(1)} %all-to-all-done.same_ref.refs_3_), channel_id=1, source_target_pairs={{0,8},{8,0},{16,24},{24,16},{32,40},{40,32},{48,56},{56,48},{64,72... | collective-permute-start | bytes 1572872 | tf_op jit(solution)/shard_map/ppermute | solution.py:399
  46.0 2.0 %same_core.1 = (f32[256,256]{1,0:T(8,128)S(1)}, f32[256,256]{1,0:T(8,128)S(1)}, f32[3,256,256]{2,1,0:T(8,128)S(1)}) custom-call(bf16[256,128]{1,0:T(8,128)(2,1)S(1)} %collective-permute-done.refs_0_, bf16[256,128]{1,0:T(8,128)(2,1)S(1)} %collective-permute-done.1.refs_1_, bf16[256,128]{1,0:T(8,128)(2,1)S(1)} %collective-permute-done.2.refs_2_, ...), custom_call_target="tpu_custom_call" | custom-call | flops 3000000000 | bytes 20000000 | tf_op jit(solution)/shard_map/same_core/pallas_call | solution.py:365
  48.0 3.2 %forward.1 = bf16[4,528,128]{2,1,0:T(8,128)(2,1)} custom-call(bf16[256,128]{1,0:T(8,128)(2,1)S(1)} %collective-permute-done.refs_0_, bf16[256,128]{1,0:T(8,128)(2,1)S(1)} %collective-permute-done.1.refs_1_, bf16[256,128]{1,0:T(8,128)(2,1)S(1)} %collective-permute-done.2.refs_2_, bf16[8,2,128,128]{3,2,1,0:T(8,128)(2,1)S(1)} %collective-permute-done.3.other_ref.refs_3_, ...), custom_call_target="tpu_custom_call" | custom-call | flops 4000000000 | bytes 20000000 | tf_op jit(solution)/shard_map/forward/pallas_call | solution.py:365
  51.2 4.0 %all-to-all-start.1 = ((bf16[4,528,128]{2,1,0:T(8,128)(2,1)}), bf16[4,528,128]{2,1,0:T(8,128)(2,1)S(1)}, u32[]{:S(2)}, u32[]{:S(2)}) async-start(bf16[4,528,128]{2,1,0:T(8,128)(2,1)} %forward.1), calls=%async_computation.1 | async-start | bytes 1081344 | tf_op jit(solution)/shard_map/all_to_all | solution.py:409
  55.2 1.5 %own_teacher.1.accl_in = f32[256,256]{1,0:T(8,128)S(1)} custom-call(bf16[256,128]{1,0:T(8,128)(2,1)S(1)} %bitcast.22, bf16[8,2,128,128]{3,2,1,0:T(8,128)(2,1)S(1)} %all-to-all-done.same_ref.refs_3_, bf16[8,2,128,128]{3,2,1,0:T(8,128)(2,1)S(1)} %collective-permute-done.3.other_ref.refs_3_), custom_call_target="tpu_custom_call" | custom-call | flops 2000000000 | bytes 20000000 | tf_op jit(solution)/shard_map/own_teacher/pallas_call | solution.py:365
  56.7 8.0 %all-to-all-done.1.got_ref = bf16[4,528,128]{2,1,0:T(8,128)(2,1)S(1)} async-done(((bf16[4,528,128]{2,1,0:T(8,128)(2,1)}), bf16[4,528,128]{2,1,0:T(8,128)(2,1)S(1)}, u32[]{:S(2)}, u32[]{:S(2)}) %all-to-all-start.1) | async-done | bytes 540704 | tf_op jit(solution)/shard_map/all_to_all | solution.py:409
  64.7 2.8 %merge.1 = (bf16[256,128]{1,0:T(8,128)(2,1)}, f32[256,128]{1,0:T(8,128)S(1)}, f32[256,128]{1,0:T(8,128)S(1)}, f32[256,256]{1,0:T(8,128)S(1)}, f32[256,256]{1,0:T...) custom-call(f32[256,256]{1,0:T(8,128)S(1)} %own_teacher.1.accl_in, ...), custom_call_target="tpu_custom_call" | custom-call | flops 2000000000 | bytes 20000000 | tf_op jit(solution)/shard_map/merge/pallas_call | solution.py:365
  67.5 3.4 %all-to-all-start.2 = ((bf16[4,272,128]{2,1,0:T(8,128)(2,1)}), bf16[4,272,128]{2,1,0:T(8,128)(2,1)S(1)}, u32[]{:S(2)}, u32[]{:S(2)}) async-start(bf16[4,272,128]{2,1,0:T(8,128)(2,1)} %get-tuple-element.35), calls=%async_computation.2 | async-start | bytes 557056 | tf_op jit(solution)/shard_map/all_to_all | solution.py:418
  70.9 1.2 near_grads.1.near_ref
  72.1 4.4 %all-to-all-done.2.got_ref = bf16[4,272,128]{2,1,0:T(8,128)(2,1)S(1)} async-done(((bf16[4,272,128]{2,1,0:T(8,128)(2,1)}), bf16[4,272,128]{2,1,0:T(8,128)(2,1)S(1)}, u32[]{:S(2)}, u32[]{:S(2)}) %all-to-all-start.2) | async-done | bytes 278560 | tf_op jit(solution)/shard_map/all_to_all | solution.py:418
  76.5 1.9 %backward.1 = f32[320,128]{1,0:T(8,128)S(1)} custom-call(bf16[8,2,128,128]{3,2,1,0:T(8,128)(2,1)S(1)} %all-to-all-done.same_ref.refs_3_, bf16[8,2,128,128]{3,2,1,0:T(8,128)(2,1)S(1)} %collective-permute-done.3.other_ref.refs_3_, f32[128,128]{1,0:T(8,128)S(1)} %copy-done.4, f32[256,256]{1,0:T(8,128)S(1)} %get-tuple-element.34.back_in, ...), custom_call_target="tpu_custom_call" | custom-call | flops 4000000000 | bytes 20000000 | tf_op jit(solution)/shard_map/backward/pallas_call | solution.py:365
  78.5 16.9 %all_to_all.30 = f32[64,1,640]{2,1,0:T(1,128)S(1)} all-to-all(f32[64,1,640]{2,1,0:T(1,128)S(1)} %bitcast.11), channel_id=1, replica_groups=mesh['ctx'=64,'kvh'=8] {'ctx'}, dimensions={0} | all-to-all | bytes 327680 | tf_op jit(solution)/shard_map/all_to_all | solution.py:429
  95.5 15.7 %all_to_all.31 = f32[8,1,640]{2,1,0:T(1,128)S(1)} all-to-all(f32[8,1,640]{2,1,0:T(1,128)S(1)} %broadcast_in_dim.6), channel_id=1, replica_groups=mesh['ctx'=64,'kvh'=8] {'kvh'}, dimensions={0} | all-to-all | bytes 40960 | tf_op jit(solution)/shard_map/all_to_all | solution.py:347
  112.0 6.8 %all-to-all-start.5 = ((f32[64,1,512]{2,1,0:T(1,128)}), f32[64,1,512]{2,1,0:T(1,128)S(1)}, u32[]{:S(2)}, u32[]{:S(2)}) async-start(f32[64,1,512]{2,1,0:T(1,128)} %broadcast_in_dim.16), calls=%async_computation.5 | async-start | bytes 262144 | tf_op jit(solution)/shard_map/all_to_all | solution.py:347
  119.3 9.8 %all-to-all-done.5 = f32[64,1,512]{2,1,0:T(1,128)S(1)} async-done(((f32[64,1,512]{2,1,0:T(1,128)}), f32[64,1,512]{2,1,0:T(1,128)S(1)}, u32[]{:S(2)}, u32[]{:S(2)}) %all-to-all-start.5) | async-done | bytes 131104 | tf_op jit(solution)/shard_map/all_to_all | solution.py:347
  (20 shorter events, 2.3 us)
Async XLA Ops:
  17.8 7.9 %copy-start.2 = (bf16[128,1,2,128]{3,2,1,0:T(2,128)(2,1)S(1)}, bf16[128,1,2,128]{3,2,1,0:T(2,128)(2,1)}, u32[]{:S(2)}) copy-start(bf16[128,1,2,128]{3,2,1,0:T(2,128)(2,1)} %param.5) | copy-start | bytes 196612
  17.8 11.8 %copy-start = (bf16[128,1,128]{2,0,1:T(8,128)(2,1)S(1)}, bf16[128,1,128]{2,0,1:T(8,128)(2,1)}, u32[]{:S(2)}) copy-start(bf16[128,1,128]{2,0,1:T(8,128)(2,1)} %param.6) | copy-start | bytes 98308
  17.8 11.7 %copy-start.1 = (bf16[128,1,128]{2,0,1:T(8,128)(2,1)S(1)}, bf16[128,1,128]{2,0,1:T(8,128)(2,1)}, u32[]{:S(2)}) copy-start(bf16[128,1,128]{2,0,1:T(8,128)(2,1)} %param.7) | copy-start | bytes 98308
  17.8 11.7 %copy-start.3 = (f32[128,128]{1,0:T(8,128)S(1)}, f32[128,128]{1,0:T(8,128)}, u32[]{:S(2)}) copy-start(f32[128,128]{1,0:T(8,128)} %wq_ref.3) | copy-start | bytes 196612
  17.8 11.7 %copy-start.4 = (f32[128,128]{1,0:T(8,128)S(1)}, f32[128,128]{1,0:T(8,128)}, u32[]{:S(2)}) copy-start(f32[128,128]{1,0:T(8,128)} %wk_ref.5) | copy-start | bytes 196612
  17.8 22.5 %all-to-all-start = ((bf16[8,2,128,128]{3,2,1,0:T(8,128)(2,1)}), bf16[8,2,128,128]{3,2,1,0:T(8,128)(2,1)S(1)}, u32[]{:S(2)}, u32[]{:S(2)}) async-start(bf16[8,2,128,128]{3,2,1,0:T(8,128)(2,1)} %copies.1), calls=%async_computation | async-start | bytes 1048576 | tf_op jit(solution)/shard_map/all_to_all | solution.py:389
  25.6 5.0 %collective-permute-start = (bf16[256,128]{1,0:T(8,128)(2,1)S(1)}, bf16[256,128]{1,0:T(8,128)(2,1)S(1)}, u32[]{:S(2)}, u32[]{:S(2)}) collective-permute-start(bf16[256,128]{1,0:T(8,128)(2,1)S(1)} %bitcast.18), channel_id=1, source_target_pairs={{128,0},{136,8},{144,16},{152,24},{160,32},{168,40},{176,48},{184,... | collective-permute-start | bytes 196616 | tf_op jit(solution)/shard_map/ppermute | solution.py:391
  26.9 6.5 %collective-permute-start.1 = (bf16[256,128]{1,0:T(8,128)(2,1)S(1)}, bf16[256,128]{1,0:T(8,128)(2,1)S(1)}, u32[]{:S(2)}, u32[]{:S(2)}) collective-permute-start(bf16[256,128]{1,0:T(8,128)(2,1)S(1)} %bitcast.19), channel_id=1, source_target_pairs={{256,0},{264,8},{272,16},{280,24},{288,32},{296,40},{304,48},{312,... | collective-permute-start | bytes 196616 | tf_op jit(solution)/shard_map/ppermute | solution.py:391
  28.2 9.0 %collective-permute-start.2 = (bf16[256,128]{1,0:T(8,128)(2,1)S(1)}, bf16[256,128]{1,0:T(8,128)(2,1)S(1)}, u32[]{:S(2)}, u32[]{:S(2)}) collective-permute-start(bf16[256,128]{1,0:T(8,128)(2,1)S(1)} %bitcast.20), channel_id=1, source_target_pairs={{384,0},{392,8},{400,16},{408,24},{416,32},{424,40},{432,48},{440,... | collective-permute-start | bytes 196616 | tf_op jit(solution)/shard_map/ppermute | solution.py:391
  40.4 7.6 %collective-permute-start.3 = (bf16[8,2,128,128]{3,2,1,0:T(8,128)(2,1)S(1)}, bf16[8,2,128,128]{3,2,1,0:T(8,128)(2,1)S(1)}, u32[]{:S(2)}, u32[]{:S(2)}) collective-permute-start(bf16[8,2,128,128]{3,2,1,0:T(8,128)(2,1)S(1)} %all-to-all-done.same_ref.refs_3_), channel_id=1, source_target_pairs={{0,8},{8,0},{16,24},{24,16},{32,40},{40,32},{48,56},{56,48},{64,72... | collective-permute-start | bytes 1572872 | tf_op jit(solution)/shard_map/ppermute | solution.py:399
  51.2 13.5 %all-to-all-start.1 = ((bf16[4,528,128]{2,1,0:T(8,128)(2,1)}), bf16[4,528,128]{2,1,0:T(8,128)(2,1)S(1)}, u32[]{:S(2)}, u32[]{:S(2)}) async-start(bf16[4,528,128]{2,1,0:T(8,128)(2,1)} %forward.1), calls=%async_computation.1 | async-start | bytes 1081344 | tf_op jit(solution)/shard_map/all_to_all | solution.py:409
  67.5 9.1 %all-to-all-start.2 = ((bf16[4,272,128]{2,1,0:T(8,128)(2,1)}), bf16[4,272,128]{2,1,0:T(8,128)(2,1)S(1)}, u32[]{:S(2)}, u32[]{:S(2)}) async-start(bf16[4,272,128]{2,1,0:T(8,128)(2,1)} %get-tuple-element.35), calls=%async_computation.2 | async-start | bytes 557056 | tf_op jit(solution)/shard_map/all_to_all | solution.py:418
  112.0 17.1 %all-to-all-start.5 = ((f32[64,1,512]{2,1,0:T(1,128)}), f32[64,1,512]{2,1,0:T(1,128)S(1)}, u32[]{:S(2)}, u32[]{:S(2)}) async-start(f32[64,1,512]{2,1,0:T(1,128)} %broadcast_in_dim.16), calls=%async_computation.5 | async-start | bytes 262144 | tf_op jit(solution)/shard_map/all_to_all | solution.py:347

commit v7 on v6

--- a/solution.py
+++ b/solution.py
@@ -83,24 +83,18 @@
     ]
 
 
-def to_columns(pages, head):
-    rows = [
-        jnp.concatenate([page[k : k + 8] for k in range(0, page.shape[0], 8)], 1) for page in pages
-    ]
-    rows += [rows[0]] * (head // 8 - len(rows))
-    return jnp.concatenate(rows, 0).T
-
-
-def copies(k_ref, v_ref, out_ref, sems):
-    moves = [
-        pltpu.make_async_copy(ref, out_ref.at[d, i], sems.at[d, i])
-        for d in range(out_ref.shape[0])
-        for i, ref in enumerate((k_ref, v_ref))
-    ]
-    for move in moves:
-        move.start()
-    for move in moves:
-        move.wait()
+def row_numbers(page):
+    return jnp.concatenate([page[k : k + 8] for k in range(0, page.shape[0], 8)], 1).astype(F32)
+
+
+def to_columns(rows, head):
+    return jnp.concatenate(rows + [jnp.zeros((head - len(rows), rows[0].shape[1]), F32)], 0).T
+
+
+def copies(k_ref, v_ref, out_ref):
+    for d in range(out_ref.shape[0]):
+        out_ref[d, 0] = k_ref[...]
+        out_ref[d, 1] = v_ref[...]
 
 
 def own_features(q, k, wq, wk):
@@ -147,7 +141,7 @@
     )
 
 
-def own_teacher(ny, scale, q_ref, same_ref, other_ref, accl_ref):
+def own_teacher(ny, scale, q_ref, same_ref, other_ref, acc_ref, stats_ref):
     _, y, core = place(ny)
     n, rows = q_ref.shape[0], same_ref.shape[2]
     col = lax.broadcasted_iota(jnp.int32, (n, ny * rows), 1)
@@ -158,8 +152,10 @@
         flat(other_ref, 0), with_ones(flat(other_ref, 1)),
         scale, (col <= row + y * rows, col < (y + core) * rows),
     )
-    lane = lax.broadcasted_iota(jnp.int32, accl.shape, 1)
-    accl_ref[...] = jnp.where(lane == accl.shape[1] - 1, best, accl)
+    head = accl.shape[1] // 2
+    acc_ref[...] = accl[:, :head]
+    lane = lax.broadcasted_iota(jnp.int32, (n, head), 1)
+    stats_ref[...] = jnp.where(lane == 0, best, accl[:, head:]).T[:8]
 
 
 def partial_softmax(q, keys, values1, c):
@@ -234,31 +230,34 @@
 
 def merge(
     nx, ny, scale, count,
-    accl_in, got_ref, fq_ref, near_ref,
+    acc_in, stats_in, got_ref, fq_ref, near_ref,
     out_ref, dnum_ref, dden_ref, state_ref, back_ref, pay_ref, loss_ref,
 ):
     x, _, _ = place(ny)
     n, feats_n = fq_ref.shape
     head = out_ref.shape[1]
     c = scale * LOG2E
-    columns = to_columns([got_ref[d, n + feats_n :].astype(F32) for d in range(nx)], head)
-    bests = [accl_in[:, 2 * head - 1 :]]
+    pages = [row_numbers(got_ref[d, n + feats_n :]) for d in range(nx)]
+    own = stats_in[0:1]
+    bests = [jnp.where(d < x, pages[d][0:1], -1e30) for d in range(nx)]
+    best = functools.reduce(jnp.maximum, bests, own)
+    factors = [jnp.exp2((own - best) * c)]
+    total = stats_in[1:2] * factors[0]
+    norm = jnp.zeros_like(total)
     for d in range(nx):
-        bests.append(jnp.where(d < x, columns[:, 8 * d : 8 * d + 1], -1e30))
-    best = functools.reduce(jnp.maximum, bests)
-    factor = jnp.exp2((bests[0] - best) * c)
-    accl = accl_in[...] * factor
-    acc, total = accl[:, :head], accl[:, head : head + 1]
-    state, norm = got_ref[x, :feats_n].astype(F32), jnp.zeros((feats_n, 1), F32)
+        factors.append(jnp.where(d < x, jnp.exp2((bests[d] - best) * c), 0.0))
+        total += (pages[d][1:2] + pages[d][2:3]) * factors[d + 1]
+        norm += pages[d][3:4] + pages[d][4:5]
+    columns = to_columns([f / total for f in factors] + [norm], head)
+    targets = acc_in[...] * columns[:, 0:1]
+    state = got_ref[x, :feats_n].astype(F32)
     for d in range(nx):
-        factor = jnp.where(d < x, jnp.exp2((bests[d + 1] - best) * c), 0.0)
-        acc += got_ref[d, :n].astype(F32) * factor
-        total += (columns[:, 8 * d + 1 : 8 * d + 2] + columns[:, 8 * d + 2 : 8 * d + 3]) * factor
+        targets += got_ref[d, :n].astype(F32) * columns[:, d + 1 : d + 2]
         state += got_ref[d, n : n + feats_n].astype(F32)
-        norm += columns[:, 8 * d + 3 : 8 * d + 4] + columns[:, 8 * d + 4 : 8 * d + 5]
+    targets = targets.astype(BF16).astype(F32)
+    norm = columns[:, nx + 1 : nx + 2]
     state = jnp.concatenate([state, jnp.broadcast_to(norm, state.shape)], 1)
     state_ref[...] = state
-    targets = (acc / total).astype(BF16).astype(F32)
     fq = fq_ref[...]
     numden = dot3(fq, state) + near_ref[...]
     den = numden[:, head:]
@@ -306,12 +305,13 @@
     rows, head = same_ref.shape[2], same_ref.shape[3]
     keys_n = ny * rows
     feats_n = back_in.shape[0]
-    columns = to_columns([got_ref[d, feats_n:].astype(F32) for d in range(nx)], head)
-    after, norm = jnp.zeros((feats_n, head), F32), jnp.zeros((feats_n, 1), F32)
+    after, norm = jnp.zeros((feats_n, head), F32), jnp.zeros((1, feats_n), F32)
     for d in range(nx):
         counts = (d > x).astype(F32)
         after += got_ref[d, :feats_n].astype(F32) * counts
-        norm += (columns[:, 8 * d : 8 * d + 1] + columns[:, 8 * d + 1 : 8 * d + 2]) * counts
+        page = row_numbers(got_ref[d, feats_n:])
+        norm += (page[0:1] + page[1:2]) * counts
+    norm = to_columns([norm], head)[:, 0:1]
 
     def both(state, norm):
         mats = jnp.concatenate([state[:head] + state[head:], state[head:]], 0)
@@ -339,7 +339,6 @@
 
 
 VMEM = pl.BlockSpec(memory_space=pltpu.VMEM)
-PARAMS = pltpu.CompilerParams(vmem_limit_bytes=20 * 1024 * 1024)
 
 
 def spread(a, axis):
@@ -361,14 +360,14 @@
     f32 = lambda *shape: jax.ShapeDtypeStruct(shape, F32)
     bf16 = lambda *shape: jax.ShapeDtypeStruct(shape, BF16)
 
-    def call(body, outs, args, scratch=(), flops=1, name=None):
+    def call(body, outs, args, scratch=(), flops=1, name=None, vmem=20):
         return pl.pallas_call(
             body,
             out_shape=outs,
             in_specs=[VMEM] * len(args),
             out_specs=jax.tree.map(lambda _: VMEM, outs),
             scratch_shapes=list(scratch),
-            compiler_params=PARAMS,
+            compiler_params=pltpu.CompilerParams(vmem_limit_bytes=vmem * 1024 * 1024),
             cost_estimate=pl.CostEstimate(
                 flops=flops * 1_000_000_000, bytes_accessed=20_000_000, transcendentals=flops * 300_000
             ),
@@ -377,15 +376,7 @@
 
     q = queries.reshape(n, head)
     k, v = keys.reshape(rows, head), values.reshape(rows, head)
-    kvs = pl.pallas_call(
-        copies,
-        out_shape=bf16(ny, 2, rows, head),
-        in_specs=[pl.BlockSpec(memory_space=pl.ANY)] * 2,
-        out_specs=pl.BlockSpec(memory_space=pl.ANY),
-        scratch_shapes=[pltpu.SemaphoreType.DMA((ny, 2))],
-        compiler_params=pltpu.CompilerParams(vmem_limit_bytes=60 * 1024 * 1024),
-        name="copies",
-    )(k, v)
+    kvs = call(copies, bf16(ny, 2, rows, head), (k, v), name="copies", vmem=60)
     same = lax.all_to_all(kvs, "ctx", 0, 0, tiled=True, axis_index_groups=y_groups)
     later = [
         lax.ppermute(q, "ctx", [(at(x, y, c), at(x - s, y, c)) for x, y, c in every if x >= s])
@@ -407,13 +398,13 @@
         (*later, other, w_key, state, full, sums), flops=4, name="forward",
     )
     got = lax.all_to_all(pay, "ctx", 0, 0, tiled=True, axis_index_groups=x_groups)
-    accl = call(
-        functools.partial(own_teacher, ny, scale), f32(n, feats), (q, same, other), flops=2, name="own_teacher",
+    acc, stats = call(
+        functools.partial(own_teacher, ny, scale), (f32(n, head), f32(8, n)), (q, same, other), flops=2, name="own_teacher",
     )
     out, dnum, dden, state, back, pay, loss = call(
         functools.partial(merge, nx, ny, scale, count),
         (bf16(n, head), f32(n, head), f32(n, head), f32(feats, feats), f32(feats, feats), bf16(nx, feats + 16, head), f32(8, head)),
-        (accl, got, fq, near), flops=2, name="merge",
+        (acc, stats, got, fq, near), flops=2, name="merge",
     )
     got = lax.all_to_all(pay, "ctx", 0, 0, tiled=True, axis_index_groups=x_groups)
     grads = call(

time: 130 us -> 114 us (0.88)
  Pallas kernels: 30.6 us -> 14.2 us
    pallas_call x1 -> x0, Pallas kernels: 17.1 us -> none  [shards(): pl.pallas_call(copies, out_shape=bf16(ny, 2, rows, head), in_specs=[pl.Bl...]
    pallas_call x7 -> x8, Pallas kernels: 13.4 us -> 14.2 us  [call(): pl.pallas_call(body, out_shape=outs, in_specs=[VMEM] * len(args), out_spe...]
  transfers between devices with their start and end apart: 8 -> 8, of which waited for: 7 -> 7; matrix products, arithmetic and copies ran while one was open for 0% -> 0% of each run, Pallas kernels for 4% -> 5%
where the time goes in v7:
time: 114 us; the launch traced here: 113 us
  blocking collectives  32.6 us (29%)
  waiting for transfers between devices  32.2 us (28%)
  starting transfers between devices  31.5 us (28%)
  Pallas kernels  14.2 us (12%)
  local copies, waits for them, and re-layouts  1.94 us (2%)
    all_to_all x1, blocking collectives, shards(): lax.all_to_all(grads.reshape(n_ctx, 1, -1), 'ctx', 0, 0, tiled=True).sum(0)  16.9 us
    all_to_all x1, blocking collectives, spread(): return lax.all_to_all(copies, axis, 0, 0, tiled=True)  15.7 us
    pallas_call x8, Pallas kernels, call(): pl.pallas_call(body, out_shape=outs, in_specs=[VMEM] * len(args), out_spe...  14.2 us
    all_to_all x2, waiting for transfers between devices, shards(): lax.all_to_all(pay, 'ctx', 0, 0, tiled=True, axis_index_groups=x_groups)  12.4 us
    all_to_all x1, waiting for transfers between devices, spread(): return lax.all_to_all(copies, axis, 0, 0, tiled=True)  9.85 us
    all_to_all x1, starting transfers between devices, shards(): lax.all_to_all(kvs, 'ctx', 0, 0, tiled=True, axis_index_groups=y_groups)  7.79 us
    all_to_all x2, starting transfers between devices, shards(): lax.all_to_all(pay, 'ctx', 0, 0, tiled=True, axis_index_groups=x_groups)  7.46 us
    ppermute x3, waiting for transfers between devices, shards(): lax.ppermute(q, 'ctx', [(at(x, y, c), at(x - s, y, c)) for x, y, c in eve...  6.82 us
  transfers between devices with their start and end apart: 8, of which 7 were waited for; matrix products, arithmetic and copies ran while one was open for 0% of the time, Pallas kernels for 5%

profile of v7, /device:TPU:1, one launch (start us, length us, event | category | flops | bytes accessed | tf_op | source)
XLA Modules:
  0.0 113.4 jit_solution(18209277402617228819)
XLA Ops:
  0.6 1.6 %copies.1 = bf16[8,2,128,128]{3,2,1,0:T(8,128)(2,1)} custom-call(bf16[128,128]{1,0:T(8,128)(2,1)} %bitcast.18, bf16[128,128]{1,0:T(8,128)(2,1)} %bitcast.21), custom_call_target="tpu_custom_call" | custom-call | flops 1000000000 | bytes 20000000 | tf_op jit(solution)/shard_map/copies/pallas_call | solution.py:364
  2.3 7.8 %all-to-all-start = ((bf16[8,2,128,128]{3,2,1,0:T(8,128)(2,1)}), bf16[8,2,128,128]{3,2,1,0:T(8,128)(2,1)S(1)}, u32[]{:S(2)}, u32[]{:S(2)}) async-start(bf16[8,2,128,128]{3,2,1,0:T(8,128)(2,1)} %copies.1), calls=%async_computation | async-start | bytes 1048576 | tf_op jit(solution)/shard_map/all_to_all | solution.py:380
  10.1 1.3 %collective-permute-start = (bf16[256,128]{1,0:T(8,128)(2,1)S(1)}, bf16[256,128]{1,0:T(8,128)(2,1)S(1)}, u32[]{:S(2)}, u32[]{:S(2)}) collective-permute-start(bf16[256,128]{1,0:T(8,128)(2,1)S(1)} %bitcast.12), channel_id=1, source_target_pairs={{128,0},{136,8},{144,16},{152,24},{160,32},{168,40},{176,48},{184,... | collective-permute-start | bytes 196616 | tf_op jit(solution)/shard_map/ppermute | solution.py:382
  11.4 1.3 %collective-permute-start.1 = (bf16[256,128]{1,0:T(8,128)(2,1)S(1)}, bf16[256,128]{1,0:T(8,128)(2,1)S(1)}, u32[]{:S(2)}, u32[]{:S(2)}) collective-permute-start(bf16[256,128]{1,0:T(8,128)(2,1)S(1)} %bitcast.13), channel_id=1, source_target_pairs={{256,0},{264,8},{272,16},{280,24},{288,32},{296,40},{304,48},{312,... | collective-permute-start | bytes 196616 | tf_op jit(solution)/shard_map/ppermute | solution.py:382
  12.7 1.3 %collective-permute-start.2 = (bf16[256,128]{1,0:T(8,128)(2,1)S(1)}, bf16[256,128]{1,0:T(8,128)(2,1)S(1)}, u32[]{:S(2)}, u32[]{:S(2)}) collective-permute-start(bf16[256,128]{1,0:T(8,128)(2,1)S(1)} %bitcast.14), channel_id=1, source_target_pairs={{384,0},{392,8},{400,16},{408,24},{416,32},{424,40},{432,48},{440,... | collective-permute-start | bytes 196616 | tf_op jit(solution)/shard_map/ppermute | solution.py:382
  14.0 0.8 prepare.1
  15.1 2.8 %collective-permute-done.1.refs_1_ = bf16[256,128]{1,0:T(8,128)(2,1)S(1)} collective-permute-done((bf16[256,128]{1,0:T(8,128)(2,1)S(1)}, bf16[256,128]{1,0:T(8,128)(2,1)S(1)}, u32[]{:S(2)}, u32[]{:S(2)}) %collective-permute-start.1) | collective-permute-done | bytes 65568 | tf_op jit(solution)/shard_map/ppermute | solution.py:382
  17.9 3.8 %collective-permute-done.2.refs_2_ = bf16[256,128]{1,0:T(8,128)(2,1)S(1)} collective-permute-done((bf16[256,128]{1,0:T(8,128)(2,1)S(1)}, bf16[256,128]{1,0:T(8,128)(2,1)S(1)}, u32[]{:S(2)}, u32[]{:S(2)}) %collective-permute-start.2) | collective-permute-done | bytes 65568 | tf_op jit(solution)/shard_map/ppermute | solution.py:382
  21.7 3.1 %all-to-all-done.same_ref.refs_3_ = bf16[8,2,128,128]{3,2,1,0:T(8,128)(2,1)S(1)} async-done(((bf16[8,2,128,128]{3,2,1,0:T(8,128)(2,1)}), bf16[8,2,128,128]{3,2,1,0:T(8,128)(2,1)S(1)}, u32[]{:S(2)}, u32[]{:S(2)}) %all-to-all-start) | async-done | bytes 524320 | tf_op jit(solution)/shard_map/all_to_all | solution.py:380
  24.8 5.6 %collective-permute-start.3 = (bf16[8,2,128,128]{3,2,1,0:T(8,128)(2,1)S(1)}, bf16[8,2,128,128]{3,2,1,0:T(8,128)(2,1)S(1)}, u32[]{:S(2)}, u32[]{:S(2)}) collective-permute-start(bf16[8,2,128,128]{3,2,1,0:T(8,128)(2,1)S(1)} %all-to-all-done.same_ref.refs_3_), channel_id=1, source_target_pairs={{0,8},{8,0},{16,24},{24,16},{32,40},{40,32},{48,56},{56,48},{64,72... | collective-permute-start | bytes 1572872 | tf_op jit(solution)/shard_map/ppermute | solution.py:390
  30.4 2.0 %same_core.1 = (f32[256,256]{1,0:T(8,128)S(1)}, f32[256,256]{1,0:T(8,128)S(1)}, f32[3,256,256]{2,1,0:T(8,128)S(1)}) custom-call(bf16[256,128]{1,0:T(8,128)(2,1)S(1)} %collective-permute-done.refs_0_, bf16[256,128]{1,0:T(8,128)(2,1)S(1)} %collective-permute-done.1.refs_1_, bf16[256,128]{1,0:T(8,128)(2,1)S(1)} %collective-permute-done.2.refs_2_, ...), custom_call_target="tpu_custom_call" | custom-call | flops 3000000000 | bytes 20000000 | tf_op jit(solution)/shard_map/same_core/pallas_call | solution.py:364
  32.5 3.2 %forward.1 = bf16[4,528,128]{2,1,0:T(8,128)(2,1)} custom-call(bf16[256,128]{1,0:T(8,128)(2,1)S(1)} %collective-permute-done.refs_0_, bf16[256,128]{1,0:T(8,128)(2,1)S(1)} %collective-permute-done.1.refs_1_, bf16[256,128]{1,0:T(8,128)(2,1)S(1)} %collective-permute-done.2.refs_2_, bf16[8,2,128,128]{3,2,1,0:T(8,128)(2,1)S(1)} %collective-permute-done.3.other_ref.refs_3_, ...), custom_call_target="tpu_custom_call" | custom-call | flops 4000000000 | bytes 20000000 | tf_op jit(solution)/shard_map/forward/pallas_call | solution.py:364
  35.7 4.0 %all-to-all-start.1 = ((bf16[4,528,128]{2,1,0:T(8,128)(2,1)}), bf16[4,528,128]{2,1,0:T(8,128)(2,1)S(1)}, u32[]{:S(2)}, u32[]{:S(2)}) async-start(bf16[4,528,128]{2,1,0:T(8,128)(2,1)} %forward.1), calls=%async_computation.1 | async-start | bytes 1081344 | tf_op jit(solution)/shard_map/all_to_all | solution.py:400
  39.7 1.5 %own_teacher.1 = (f32[256,128]{1,0:T(8,128)S(1)}, f32[8,256]{1,0:T(8,128)S(1)}) custom-call(bf16[256,128]{1,0:T(8,128)(2,1)S(1)} %bitcast.16, bf16[8,2,128,128]{3,2,1,0:T(8,128)(2,1)S(1)} %all-to-all-done.same_ref.refs_3_, bf16[8,2,128,128]{3,2,1,0:T(8,128)(2,1)S(1)} %collective-permute-done.3.other_ref.refs_3_), custom_call_target="tpu_custom_call" | custom-call | flops 2000000000 | bytes 20000000 | tf_op jit(solution)/shard_map/own_teacher/pallas_call | solution.py:364
  41.2 8.0 %all-to-all-done.1.got_ref = bf16[4,528,128]{2,1,0:T(8,128)(2,1)S(1)} async-done(((bf16[4,528,128]{2,1,0:T(8,128)(2,1)}), bf16[4,528,128]{2,1,0:T(8,128)(2,1)S(1)}, u32[]{:S(2)}, u32[]{:S(2)}) %all-to-all-start.1) | async-done | bytes 540704 | tf_op jit(solution)/shard_map/all_to_all | solution.py:400
  49.2 1.9 %merge.1 = (bf16[256,128]{1,0:T(8,128)(2,1)}, f32[256,128]{1,0:T(8,128)S(1)}, f32[256,128]{1,0:T(8,128)S(1)}, f32[256,256]{1,0:T(8,128)S(1)}, f32[256,256]{1,0:T...) custom-call(f32[256,128]{1,0:T(8,128)S(1)} %get-tuple-element.27.acc_in, ...), custom_call_target="tpu_custom_call" | custom-call | flops 2000000000 | bytes 20000000 | tf_op jit(solution)/shard_map/merge/pallas_call | solution.py:364
  51.1 3.4 %all-to-all-start.2 = ((bf16[4,272,128]{2,1,0:T(8,128)(2,1)}), bf16[4,272,128]{2,1,0:T(8,128)(2,1)S(1)}, u32[]{:S(2)}, u32[]{:S(2)}) async-start(bf16[4,272,128]{2,1,0:T(8,128)(2,1)} %get-tuple-element.39), calls=%async_computation.2 | async-start | bytes 557056 | tf_op jit(solution)/shard_map/all_to_all | solution.py:409
  54.5 1.2 %near_grads.1.near_ref = f32[256,128]{1,0:T(8,128)S(1)} custom-call(bf16[256,128]{1,0:T(8,128)(2,1)S(1)} %bitcast.17, bf16[128,128]{1,0:T(8,128)(2,1)S(1)} %bitcast.20, bf16[128,128]{1,0:T(8,128)(2,1)S(1)} %bitcast.23, f32[128,128]{1,0:T(8,128)S(1)} %copy-done.1, f32[128,128]{1,0:T(8,128)S(1)} %copy-done.2, f32[256,128]{1,0:T(8,128)S(1)} %get-tuple-element.40.dnum_ref, ...), custom_call_target="tpu_custom_call" | custom-call | flops 2000000000 | bytes 20000000 | tf_op jit(solution)/shard_map/near_grads/pallas_call | solution.py:364
  55.7 4.4 %all-to-all-done.2.got_ref = bf16[4,272,128]{2,1,0:T(8,128)(2,1)S(1)} async-done(((bf16[4,272,128]{2,1,0:T(8,128)(2,1)}), bf16[4,272,128]{2,1,0:T(8,128)(2,1)S(1)}, u32[]{:S(2)}, u32[]{:S(2)}) %all-to-all-start.2) | async-done | bytes 278560 | tf_op jit(solution)/shard_map/all_to_all | solution.py:409
  60.1 1.9 %backward.1 = f32[320,128]{1,0:T(8,128)S(1)} custom-call(bf16[8,2,128,128]{3,2,1,0:T(8,128)(2,1)S(1)} %all-to-all-done.same_ref.refs_3_, bf16[8,2,128,128]{3,2,1,0:T(8,128)(2,1)S(1)} %collective-permute-done.3.other_ref.refs_3_, f32[128,128]{1,0:T(8,128)S(1)} %copy-done.2, f32[256,256]{1,0:T(8,128)S(1)} %get-tuple-element.38.back_in, ...), custom_call_target="tpu_custom_call" | custom-call | flops 4000000000 | bytes 20000000 | tf_op jit(solution)/shard_map/backward/pallas_call | solution.py:364
  62.0 16.9 %all_to_all.30 = f32[64,1,640]{2,1,0:T(1,128)S(1)} all-to-all(f32[64,1,640]{2,1,0:T(1,128)S(1)} %bitcast.11), channel_id=1, replica_groups=mesh['ctx'=64,'kvh'=8] {'ctx'}, dimensions={0} | all-to-all | bytes 327680 | tf_op jit(solution)/shard_map/all_to_all | solution.py:420
  79.1 15.7 %all_to_all.31 = f32[8,1,640]{2,1,0:T(1,128)S(1)} all-to-all(f32[8,1,640]{2,1,0:T(1,128)S(1)} %broadcast_in_dim.6), channel_id=1, replica_groups=mesh['ctx'=64,'kvh'=8] {'kvh'}, dimensions={0} | all-to-all | bytes 40960 | tf_op jit(solution)/shard_map/all_to_all | solution.py:346
  95.6 6.8 %all-to-all-start.5 = ((f32[64,1,512]{2,1,0:T(1,128)}), f32[64,1,512]{2,1,0:T(1,128)S(1)}, u32[]{:S(2)}, u32[]{:S(2)}) async-start(f32[64,1,512]{2,1,0:T(1,128)} %broadcast_in_dim.16), calls=%async_computation.5 | async-start | bytes 262144 | tf_op jit(solution)/shard_map/all_to_all | solution.py:346
  102.9 9.8 %all-to-all-done.5 = f32[64,1,512]{2,1,0:T(1,128)S(1)} async-done(((f32[64,1,512]{2,1,0:T(1,128)}), f32[64,1,512]{2,1,0:T(1,128)S(1)}, u32[]{:S(2)}, u32[]{:S(2)}) %all-to-all-start.5) | async-done | bytes 131104 | tf_op jit(solution)/shard_map/all_to_all | solution.py:346
  (20 shorter events, 2.3 us)
Async XLA Ops:
  2.3 7.8 %copy-start = (bf16[128,1,2,128]{3,2,1,0:T(2,128)(2,1)S(1)}, bf16[128,1,2,128]{3,2,1,0:T(2,128)(2,1)}, u32[]{:S(2)}) copy-start(bf16[128,1,2,128]{3,2,1,0:T(2,128)(2,1)} %param.5) | copy-start | bytes 196612
  2.3 11.7 %copy-start.1 = (f32[128,128]{1,0:T(8,128)S(1)}, f32[128,128]{1,0:T(8,128)}, u32[]{:S(2)}) copy-start(f32[128,128]{1,0:T(8,128)} %wq_ref.3) | copy-start | bytes 196612
  2.3 11.7 %copy-start.2 = (f32[128,128]{1,0:T(8,128)S(1)}, f32[128,128]{1,0:T(8,128)}, u32[]{:S(2)}) copy-start(f32[128,128]{1,0:T(8,128)} %wk_ref.5) | copy-start | bytes 196612
  2.3 11.7 %copy-start.3 = (bf16[128,1,128]{2,0,1:T(8,128)(2,1)S(1)}, bf16[128,1,128]{2,0,1:T(8,128)(2,1)}, u32[]{:S(2)}) copy-start(bf16[128,1,128]{2,0,1:T(8,128)(2,1)} %param.6) | copy-start | bytes 98308
  2.3 11.7 %copy-start.4 = (bf16[128,1,128]{2,0,1:T(8,128)(2,1)S(1)}, bf16[128,1,128]{2,0,1:T(8,128)(2,1)}, u32[]{:S(2)}) copy-start(bf16[128,1,128]{2,0,1:T(8,128)(2,1)} %param.7) | copy-start | bytes 98308
  2.3 22.5 %all-to-all-start = ((bf16[8,2,128,128]{3,2,1,0:T(8,128)(2,1)}), bf16[8,2,128,128]{3,2,1,0:T(8,128)(2,1)S(1)}, u32[]{:S(2)}, u32[]{:S(2)}) async-start(bf16[8,2,128,128]{3,2,1,0:T(8,128)(2,1)} %copies.1), calls=%async_computation | async-start | bytes 1048576 | tf_op jit(solution)/shard_map/all_to_all | solution.py:380
  10.1 5.0 %collective-permute-start = (bf16[256,128]{1,0:T(8,128)(2,1)S(1)}, bf16[256,128]{1,0:T(8,128)(2,1)S(1)}, u32[]{:S(2)}, u32[]{:S(2)}) collective-permute-start(bf16[256,128]{1,0:T(8,128)(2,1)S(1)} %bitcast.12), channel_id=1, source_target_pairs={{128,0},{136,8},{144,16},{152,24},{160,32},{168,40},{176,48},{184,... | collective-permute-start | bytes 196616 | tf_op jit(solution)/shard_map/ppermute | solution.py:382
  11.4 6.5 %collective-permute-start.1 = (bf16[256,128]{1,0:T(8,128)(2,1)S(1)}, bf16[256,128]{1,0:T(8,128)(2,1)S(1)}, u32[]{:S(2)}, u32[]{:S(2)}) collective-permute-start(bf16[256,128]{1,0:T(8,128)(2,1)S(1)} %bitcast.13), channel_id=1, source_target_pairs={{256,0},{264,8},{272,16},{280,24},{288,32},{296,40},{304,48},{312,... | collective-permute-start | bytes 196616 | tf_op jit(solution)/shard_map/ppermute | solution.py:382
  12.7 9.0 %collective-permute-start.2 = (bf16[256,128]{1,0:T(8,128)(2,1)S(1)}, bf16[256,128]{1,0:T(8,128)(2,1)S(1)}, u32[]{:S(2)}, u32[]{:S(2)}) collective-permute-start(bf16[256,128]{1,0:T(8,128)(2,1)S(1)} %bitcast.14), channel_id=1, source_target_pairs={{384,0},{392,8},{400,16},{408,24},{416,32},{424,40},{432,48},{440,... | collective-permute-start | bytes 196616 | tf_op jit(solution)/shard_map/ppermute | solution.py:382
  24.8 7.6 %collective-permute-start.3 = (bf16[8,2,128,128]{3,2,1,0:T(8,128)(2,1)S(1)}, bf16[8,2,128,128]{3,2,1,0:T(8,128)(2,1)S(1)}, u32[]{:S(2)}, u32[]{:S(2)}) collective-permute-start(bf16[8,2,128,128]{3,2,1,0:T(8,128)(2,1)S(1)} %all-to-all-done.same_ref.refs_3_), channel_id=1, source_target_pairs={{0,8},{8,0},{16,24},{24,16},{32,40},{40,32},{48,56},{56,48},{64,72... | collective-permute-start | bytes 1572872 | tf_op jit(solution)/shard_map/ppermute | solution.py:390
  35.7 13.5 %all-to-all-start.1 = ((bf16[4,528,128]{2,1,0:T(8,128)(2,1)}), bf16[4,528,128]{2,1,0:T(8,128)(2,1)S(1)}, u32[]{:S(2)}, u32[]{:S(2)}) async-start(bf16[4,528,128]{2,1,0:T(8,128)(2,1)} %forward.1), calls=%async_computation.1 | async-start | bytes 1081344 | tf_op jit(solution)/shard_map/all_to_all | solution.py:400
  51.1 9.1 %all-to-all-start.2 = ((bf16[4,272,128]{2,1,0:T(8,128)(2,1)}), bf16[4,272,128]{2,1,0:T(8,128)(2,1)S(1)}, u32[]{:S(2)}, u32[]{:S(2)}) async-start(bf16[4,272,128]{2,1,0:T(8,128)(2,1)} %get-tuple-element.39), calls=%async_computation.2 | async-start | bytes 557056 | tf_op jit(solution)/shard_map/all_to_all | solution.py:409
  95.6 17.1 %all-to-all-start.5 = ((f32[64,1,512]{2,1,0:T(1,128)}), f32[64,1,512]{2,1,0:T(1,128)S(1)}, u32[]{:S(2)}, u32[]{:S(2)}) async-start(f32[64,1,512]{2,1,0:T(1,128)} %broadcast_in_dim.16), calls=%async_computation.5 | async-start | bytes 262144 | tf_op jit(solution)/shard_map/all_to_all | solution.py:346

commit v8 on v7

--- a/solution.py
+++ b/solution.py
@@ -341,9 +341,9 @@
 VMEM = pl.BlockSpec(memory_space=pltpu.VMEM)
 
 
-def spread(a, axis):
-    copies = jnp.broadcast_to(a[None], (lax.axis_size(axis), *a.shape))
-    return lax.all_to_all(copies, axis, 0, 0, tiled=True)
+def spread(a, axes, groups):
+    copies = jnp.broadcast_to(a[None], (len(groups[0]), *a.shape))
+    return lax.all_to_all(copies, axes, 0, 0, tiled=True, axis_index_groups=groups)
 
 
 def shards(nx, ny, queries, keys, values, w_query, w_key):
@@ -410,16 +410,26 @@
     grads = call(
         near_grads, f32(feats, head), (q, k, v, w_query, w_key, dnum, dden, state), flops=2, name="near_grads",
     )
-    parts = feats // n_ctx
+    both_axes = ("ctx", "kvh")
+    chips = nx * ny
+    chip_groups = [
+        [at(x, y, c) * n_kvh + z for x in range(nx) for y in range(ny)] for c in range(CORES) for z in range(n_kvh)
+    ]
+    rest_groups = [
+        [at(x, y, c) * n_kvh + z for c in range(CORES) for z in range(n_kvh)] for x in range(nx) for y in range(ny)
+    ]
+    parts = feats // chips
     grads = call(
         functools.partial(backward, nx, ny),
-        f32(n_ctx * (parts + 1), head),
+        f32(chips * (parts + 1), head),
         (same, other, w_key, back, got, grads, loss),
         scratch=(pltpu.VMEM((feats, head), F32),), flops=4, name="backward",
     )
-    mine = lax.all_to_all(grads.reshape(n_ctx, 1, -1), "ctx", 0, 0, tiled=True).sum(0)
-    mine = spread(mine, "kvh").sum(0)
-    g = spread(mine[:, : parts * head], "ctx").reshape(2, head, head)
+    mine = lax.all_to_all(
+        grads.reshape(chips, 1, -1), both_axes, 0, 0, tiled=True, axis_index_groups=chip_groups
+    ).sum(0)
+    mine = spread(mine, both_axes, rest_groups).sum(0)
+    g = spread(mine[0, : parts * head].reshape(parts, head), both_axes, chip_groups).reshape(2, head, head)
     return out.reshape(queries.shape), g[0], g[1], mine[0, parts * head]
 
 

time: 114 us -> 111 us (0.974)
  starting transfers between devices: 31.5 us -> 28.6 us
    all_to_all x1, starting transfers between devices: 6.78 us -> 3.86 us  [spread(): lax.all_to_all(copies, axes, 0, 0, tiled=True, axis_index_groups=groups)]
where the time goes in v8:
time: 111 us; the launch traced here: 110 us
  blocking collectives  33.1 us (30%)
  waiting for transfers between devices  31.1 us (28%)
  starting transfers between devices  28.6 us (26%)
  Pallas kernels  14.2 us (13%)
  local copies, waits for them, and re-layouts  1.91 us (2%)
    all_to_all x1, blocking collectives, spread(): lax.all_to_all(copies, axes, 0, 0, tiled=True, axis_index_groups=groups)  19.9 us
    pallas_call x8, Pallas kernels, call(): pl.pallas_call(body, out_shape=outs, in_specs=[VMEM] * len(args), out_spe...  14.2 us
    all_to_all x1, blocking collectives, shards(): lax.all_to_all(grads.reshape(chips, 1, -1), both_axes, 0, 0, tiled=True,...  13.1 us
    all_to_all x2, waiting for transfers between devices, shards(): lax.all_to_all(pay, 'ctx', 0, 0, tiled=True, axis_index_groups=x_groups)  12.4 us
    all_to_all x1, waiting for transfers between devices, spread(): lax.all_to_all(copies, axes, 0, 0, tiled=True, axis_index_groups=groups)  8.73 us
    all_to_all x1, starting transfers between devices, shards(): lax.all_to_all(kvs, 'ctx', 0, 0, tiled=True, axis_index_groups=y_groups)  7.79 us
    all_to_all x2, starting transfers between devices, shards(): lax.all_to_all(pay, 'ctx', 0, 0, tiled=True, axis_index_groups=x_groups)  7.46 us
    ppermute x3, waiting for transfers between devices, shards(): lax.ppermute(q, 'ctx', [(at(x, y, c), at(x - s, y, c)) for x, y, c in eve...  6.82 us
  transfers between devices with their start and end apart: 8, of which 7 were waited for; matrix products, arithmetic and copies ran while one was open for 0% of the time, Pallas kernels for 5%

profile of v8, /device:TPU:1, one launch (start us, length us, event | category | flops | bytes accessed | tf_op | source)
XLA Modules:
  0.0 109.8 jit_solution(17051525669621182527)
XLA Ops:
  0.6 1.6 %copies.1 = bf16[8,2,128,128]{3,2,1,0:T(8,128)(2,1)} custom-call(bf16[128,128]{1,0:T(8,128)(2,1)} %bitcast.20, bf16[128,128]{1,0:T(8,128)(2,1)} %bitcast.23), custom_call_target="tpu_custom_call" | custom-call | flops 1000000000 | bytes 20000000 | tf_op jit(solution)/shard_map/copies/pallas_call | solution.py:364
  2.3 7.8 %all-to-all-start = ((bf16[8,2,128,128]{3,2,1,0:T(8,128)(2,1)}), bf16[8,2,128,128]{3,2,1,0:T(8,128)(2,1)S(1)}, u32[]{:S(2)}, u32[]{:S(2)}) async-start(bf16[8,2,128,128]{3,2,1,0:T(8,128)(2,1)} %copies.1), calls=%async_computation | async-start | bytes 1048576 | tf_op jit(solution)/shard_map/all_to_all | solution.py:380
  10.1 1.3 %collective-permute-start = (bf16[256,128]{1,0:T(8,128)(2,1)S(1)}, bf16[256,128]{1,0:T(8,128)(2,1)S(1)}, u32[]{:S(2)}, u32[]{:S(2)}) collective-permute-start(bf16[256,128]{1,0:T(8,128)(2,1)S(1)} %bitcast.14), channel_id=1, source_target_pairs={{128,0},{136,8},{144,16},{152,24},{160,32},{168,40},{176,48},{184,... | collective-permute-start | bytes 196616 | tf_op jit(solution)/shard_map/ppermute | solution.py:382
  11.4 1.3 %collective-permute-start.1 = (bf16[256,128]{1,0:T(8,128)(2,1)S(1)}, bf16[256,128]{1,0:T(8,128)(2,1)S(1)}, u32[]{:S(2)}, u32[]{:S(2)}) collective-permute-start(bf16[256,128]{1,0:T(8,128)(2,1)S(1)} %bitcast.15), channel_id=1, source_target_pairs={{256,0},{264,8},{272,16},{280,24},{288,32},{296,40},{304,48},{312,... | collective-permute-start | bytes 196616 | tf_op jit(solution)/shard_map/ppermute | solution.py:382
  12.7 1.3 %collective-permute-start.2 = (bf16[256,128]{1,0:T(8,128)(2,1)S(1)}, bf16[256,128]{1,0:T(8,128)(2,1)S(1)}, u32[]{:S(2)}, u32[]{:S(2)}) collective-permute-start(bf16[256,128]{1,0:T(8,128)(2,1)S(1)} %bitcast.16), channel_id=1, source_target_pairs={{384,0},{392,8},{400,16},{408,24},{416,32},{424,40},{432,48},{440,... | collective-permute-start | bytes 196616 | tf_op jit(solution)/shard_map/ppermute | solution.py:382
  14.0 0.8 prepare.1
  15.1 2.8 %collective-permute-done.1.refs_1_ = bf16[256,128]{1,0:T(8,128)(2,1)S(1)} collective-permute-done((bf16[256,128]{1,0:T(8,128)(2,1)S(1)}, bf16[256,128]{1,0:T(8,128)(2,1)S(1)}, u32[]{:S(2)}, u32[]{:S(2)}) %collective-permute-start.1) | collective-permute-done | bytes 65568 | tf_op jit(solution)/shard_map/ppermute | solution.py:382
  17.9 3.8 %collective-permute-done.2.refs_2_ = bf16[256,128]{1,0:T(8,128)(2,1)S(1)} collective-permute-done((bf16[256,128]{1,0:T(8,128)(2,1)S(1)}, bf16[256,128]{1,0:T(8,128)(2,1)S(1)}, u32[]{:S(2)}, u32[]{:S(2)}) %collective-permute-start.2) | collective-permute-done | bytes 65568 | tf_op jit(solution)/shard_map/ppermute | solution.py:382
  21.7 3.1 %all-to-all-done.same_ref.refs_3_ = bf16[8,2,128,128]{3,2,1,0:T(8,128)(2,1)S(1)} async-done(((bf16[8,2,128,128]{3,2,1,0:T(8,128)(2,1)}), bf16[8,2,128,128]{3,2,1,0:T(8,128)(2,1)S(1)}, u32[]{:S(2)}, u32[]{:S(2)}) %all-to-all-start) | async-done | bytes 524320 | tf_op jit(solution)/shard_map/all_to_all | solution.py:380
  24.8 5.6 %collective-permute-start.3 = (bf16[8,2,128,128]{3,2,1,0:T(8,128)(2,1)S(1)}, bf16[8,2,128,128]{3,2,1,0:T(8,128)(2,1)S(1)}, u32[]{:S(2)}, u32[]{:S(2)}) collective-permute-start(bf16[8,2,128,128]{3,2,1,0:T(8,128)(2,1)S(1)} %all-to-all-done.same_ref.refs_3_), channel_id=1, source_target_pairs={{0,8},{8,0},{16,24},{24,16},{32,40},{40,32},{48,56},{56,48},{64,72... | collective-permute-start | bytes 1572872 | tf_op jit(solution)/shard_map/ppermute | solution.py:390
  30.4 2.0 %same_core.1 = (f32[256,256]{1,0:T(8,128)S(1)}, f32[256,256]{1,0:T(8,128)S(1)}, f32[3,256,256]{2,1,0:T(8,128)S(1)}) custom-call(bf16[256,128]{1,0:T(8,128)(2,1)S(1)} %collective-permute-done.refs_0_, bf16[256,128]{1,0:T(8,128)(2,1)S(1)} %collective-permute-done.1.refs_1_, bf16[256,128]{1,0:T(8,128)(2,1)S(1)} %collective-permute-done.2.refs_2_, ...), custom_call_target="tpu_custom_call" | custom-call | flops 3000000000 | bytes 20000000 | tf_op jit(solution)/shard_map/same_core/pallas_call | solution.py:364
  32.5 3.2 %forward.1 = bf16[4,528,128]{2,1,0:T(8,128)(2,1)} custom-call(bf16[256,128]{1,0:T(8,128)(2,1)S(1)} %collective-permute-done.refs_0_, bf16[256,128]{1,0:T(8,128)(2,1)S(1)} %collective-permute-done.1.refs_1_, bf16[256,128]{1,0:T(8,128)(2,1)S(1)} %collective-permute-done.2.refs_2_, bf16[8,2,128,128]{3,2,1,0:T(8,128)(2,1)S(1)} %collective-permute-done.3.other_ref.refs_3_, ...), custom_call_target="tpu_custom_call" | custom-call | flops 4000000000 | bytes 20000000 | tf_op jit(solution)/shard_map/forward/pallas_call | solution.py:364
  35.7 4.0 %all-to-all-start.1 = ((bf16[4,528,128]{2,1,0:T(8,128)(2,1)}), bf16[4,528,128]{2,1,0:T(8,128)(2,1)S(1)}, u32[]{:S(2)}, u32[]{:S(2)}) async-start(bf16[4,528,128]{2,1,0:T(8,128)(2,1)} %forward.1), calls=%async_computation.1 | async-start | bytes 1081344 | tf_op jit(solution)/shard_map/all_to_all | solution.py:400
  39.7 1.5 %own_teacher.1 = (f32[256,128]{1,0:T(8,128)S(1)}, f32[8,256]{1,0:T(8,128)S(1)}) custom-call(bf16[256,128]{1,0:T(8,128)(2,1)S(1)} %bitcast.18, bf16[8,2,128,128]{3,2,1,0:T(8,128)(2,1)S(1)} %all-to-all-done.same_ref.refs_3_, bf16[8,2,128,128]{3,2,1,0:T(8,128)(2,1)S(1)} %collective-permute-done.3.other_ref.refs_3_), custom_call_target="tpu_custom_call" | custom-call | flops 2000000000 | bytes 20000000 | tf_op jit(solution)/shard_map/own_teacher/pallas_call | solution.py:364
  41.2 8.0 %all-to-all-done.1.got_ref = bf16[4,528,128]{2,1,0:T(8,128)(2,1)S(1)} async-done(((bf16[4,528,128]{2,1,0:T(8,128)(2,1)}), bf16[4,528,128]{2,1,0:T(8,128)(2,1)S(1)}, u32[]{:S(2)}, u32[]{:S(2)}) %all-to-all-start.1) | async-done | bytes 540704 | tf_op jit(solution)/shard_map/all_to_all | solution.py:400
  49.2 1.9 %merge.1 = (bf16[256,128]{1,0:T(8,128)(2,1)}, f32[256,128]{1,0:T(8,128)S(1)}, f32[256,128]{1,0:T(8,128)S(1)}, f32[256,256]{1,0:T(8,128)S(1)}, f32[256,256]{1,0:T...) custom-call(f32[256,128]{1,0:T(8,128)S(1)} %get-tuple-element.27.acc_in, ...), custom_call_target="tpu_custom_call" | custom-call | flops 2000000000 | bytes 20000000 | tf_op jit(solution)/shard_map/merge/pallas_call | solution.py:364
  51.1 3.4 %all-to-all-start.2 = ((bf16[4,272,128]{2,1,0:T(8,128)(2,1)}), bf16[4,272,128]{2,1,0:T(8,128)(2,1)S(1)}, u32[]{:S(2)}, u32[]{:S(2)}) async-start(bf16[4,272,128]{2,1,0:T(8,128)(2,1)} %get-tuple-element.39), calls=%async_computation.2 | async-start | bytes 557056 | tf_op jit(solution)/shard_map/all_to_all | solution.py:409
  54.5 1.2 %near_grads.1.near_ref = f32[256,128]{1,0:T(8,128)S(1)} custom-call(bf16[256,128]{1,0:T(8,128)(2,1)S(1)} %bitcast.19, bf16[128,128]{1,0:T(8,128)(2,1)S(1)} %bitcast.22, bf16[128,128]{1,0:T(8,128)(2,1)S(1)} %bitcast.25, f32[128,128]{1,0:T(8,128)S(1)} %copy-done.1, f32[128,128]{1,0:T(8,128)S(1)} %copy-done.2, f32[256,128]{1,0:T(8,128)S(1)} %get-tuple-element.40.dnum_ref, ...), custom_call_target="tpu_custom_call" | custom-call | flops 2000000000 | bytes 20000000 | tf_op jit(solution)/shard_map/near_grads/pallas_call | solution.py:364
  55.7 4.4 %all-to-all-done.2.got_ref = bf16[4,272,128]{2,1,0:T(8,128)(2,1)S(1)} async-done(((bf16[4,272,128]{2,1,0:T(8,128)(2,1)}), bf16[4,272,128]{2,1,0:T(8,128)(2,1)S(1)}, u32[]{:S(2)}, u32[]{:S(2)}) %all-to-all-start.2) | async-done | bytes 278560 | tf_op jit(solution)/shard_map/all_to_all | solution.py:409
  60.1 1.9 %backward.1 = f32[288,128]{1,0:T(8,128)S(1)} custom-call(bf16[8,2,128,128]{3,2,1,0:T(8,128)(2,1)S(1)} %all-to-all-done.same_ref.refs_3_, bf16[8,2,128,128]{3,2,1,0:T(8,128)(2,1)S(1)} %collective-permute-done.3.other_ref.refs_3_, f32[128,128]{1,0:T(8,128)S(1)} %copy-done.2, f32[256,256]{1,0:T(8,128)S(1)} %get-tuple-element.38.back_in, ...), custom_call_target="tpu_custom_call" | custom-call | flops 4000000000 | bytes 20000000 | tf_op jit(solution)/shard_map/backward/pallas_call | solution.py:364
  62.0 13.1 %all_to_all.30 = f32[32,1,1152]{2,1,0:T(1,128)S(1)} all-to-all(f32[32,1,1152]{2,1,0:T(1,128)S(1)} %bitcast.13), channel_id=1, replica_groups={{0,16,32,48,64,80,96,112,128,144,160,176,192,208,224,240,256,272,288,30..., dimensions={0} | all-to-all | bytes 294912 | tf_op jit(solution)/shard_map/all_to_all | solution.py:428
  75.3 19.9 %all_to_all.31 = f32[16,1,1152]{2,1,0:T(1,128)S(1)} all-to-all(f32[16,1,1152]{2,1,0:T(1,128)S(1)} %broadcast_in_dim.6), channel_id=1, replica_groups={{0,1,2,3,4,5,6,7,8,9,10,11,12,13,14,15},{16,17,18,19,20,21,22,23,24,25,..., dimensions={0} | all-to-all | bytes 147456 | tf_op jit(solution)/shard_map/all_to_all | solution.py:346
  96.0 3.9 %all-to-all-start.5 = ((f32[32,8,128]{2,1,0:T(8,128)}), f32[32,8,128]{2,1,0:T(8,128)S(1)}, u32[]{:S(2)}, u32[]{:S(2)}) async-start(f32[32,8,128]{2,1,0:T(8,128)} %broadcast_in_dim.15), calls=%async_computation.5 | async-start | bytes 262144 | tf_op jit(solution)/shard_map/all_to_all | solution.py:346
  100.4 8.7 %all-to-all-done.5 = f32[32,8,128]{2,1,0:T(8,128)S(1)} async-done(((f32[32,8,128]{2,1,0:T(8,128)}), f32[32,8,128]{2,1,0:T(8,128)S(1)}, u32[]{:S(2)}, u32[]{:S(2)}) %all-to-all-start.5) | async-done | bytes 131104 | tf_op jit(solution)/shard_map/all_to_all | solution.py:346
  (20 shorter events, 2.3 us)
Async XLA Ops:
  2.3 7.8 %copy-start = (bf16[128,1,2,128]{3,2,1,0:T(2,128)(2,1)S(1)}, bf16[128,1,2,128]{3,2,1,0:T(2,128)(2,1)}, u32[]{:S(2)}) copy-start(bf16[128,1,2,128]{3,2,1,0:T(2,128)(2,1)} %param.5) | copy-start | bytes 196612
  2.3 11.7 %copy-start.1 = (f32[128,128]{1,0:T(8,128)S(1)}, f32[128,128]{1,0:T(8,128)}, u32[]{:S(2)}) copy-start(f32[128,128]{1,0:T(8,128)} %wq_ref.3) | copy-start | bytes 196612
  2.3 11.7 %copy-start.2 = (f32[128,128]{1,0:T(8,128)S(1)}, f32[128,128]{1,0:T(8,128)}, u32[]{:S(2)}) copy-start(f32[128,128]{1,0:T(8,128)} %wk_ref.5) | copy-start | bytes 196612
  2.3 11.7 %copy-start.3 = (bf16[128,1,128]{2,0,1:T(8,128)(2,1)S(1)}, bf16[128,1,128]{2,0,1:T(8,128)(2,1)}, u32[]{:S(2)}) copy-start(bf16[128,1,128]{2,0,1:T(8,128)(2,1)} %param.6) | copy-start | bytes 98308
  2.3 11.7 %copy-start.4 = (bf16[128,1,128]{2,0,1:T(8,128)(2,1)S(1)}, bf16[128,1,128]{2,0,1:T(8,128)(2,1)}, u32[]{:S(2)}) copy-start(bf16[128,1,128]{2,0,1:T(8,128)(2,1)} %param.7) | copy-start | bytes 98308
  2.3 22.5 %all-to-all-start = ((bf16[8,2,128,128]{3,2,1,0:T(8,128)(2,1)}), bf16[8,2,128,128]{3,2,1,0:T(8,128)(2,1)S(1)}, u32[]{:S(2)}, u32[]{:S(2)}) async-start(bf16[8,2,128,128]{3,2,1,0:T(8,128)(2,1)} %copies.1), calls=%async_computation | async-start | bytes 1048576 | tf_op jit(solution)/shard_map/all_to_all | solution.py:380
  10.1 5.0 %collective-permute-start = (bf16[256,128]{1,0:T(8,128)(2,1)S(1)}, bf16[256,128]{1,0:T(8,128)(2,1)S(1)}, u32[]{:S(2)}, u32[]{:S(2)}) collective-permute-start(bf16[256,128]{1,0:T(8,128)(2,1)S(1)} %bitcast.14), channel_id=1, source_target_pairs={{128,0},{136,8},{144,16},{152,24},{160,32},{168,40},{176,48},{184,... | collective-permute-start | bytes 196616 | tf_op jit(solution)/shard_map/ppermute | solution.py:382
  11.4 6.5 %collective-permute-start.1 = (bf16[256,128]{1,0:T(8,128)(2,1)S(1)}, bf16[256,128]{1,0:T(8,128)(2,1)S(1)}, u32[]{:S(2)}, u32[]{:S(2)}) collective-permute-start(bf16[256,128]{1,0:T(8,128)(2,1)S(1)} %bitcast.15), channel_id=1, source_target_pairs={{256,0},{264,8},{272,16},{280,24},{288,32},{296,40},{304,48},{312,... | collective-permute-start | bytes 196616 | tf_op jit(solution)/shard_map/ppermute | solution.py:382
  12.7 9.0 %collective-permute-start.2 = (bf16[256,128]{1,0:T(8,128)(2,1)S(1)}, bf16[256,128]{1,0:T(8,128)(2,1)S(1)}, u32[]{:S(2)}, u32[]{:S(2)}) collective-permute-start(bf16[256,128]{1,0:T(8,128)(2,1)S(1)} %bitcast.16), channel_id=1, source_target_pairs={{384,0},{392,8},{400,16},{408,24},{416,32},{424,40},{432,48},{440,... | collective-permute-start | bytes 196616 | tf_op jit(solution)/shard_map/ppermute | solution.py:382
  24.8 7.6 %collective-permute-start.3 = (bf16[8,2,128,128]{3,2,1,0:T(8,128)(2,1)S(1)}, bf16[8,2,128,128]{3,2,1,0:T(8,128)(2,1)S(1)}, u32[]{:S(2)}, u32[]{:S(2)}) collective-permute-start(bf16[8,2,128,128]{3,2,1,0:T(8,128)(2,1)S(1)} %all-to-all-done.same_ref.refs_3_), channel_id=1, source_target_pairs={{0,8},{8,0},{16,24},{24,16},{32,40},{40,32},{48,56},{56,48},{64,72... | collective-permute-start | bytes 1572872 | tf_op jit(solution)/shard_map/ppermute | solution.py:390
  35.7 13.5 %all-to-all-start.1 = ((bf16[4,528,128]{2,1,0:T(8,128)(2,1)}), bf16[4,528,128]{2,1,0:T(8,128)(2,1)S(1)}, u32[]{:S(2)}, u32[]{:S(2)}) async-start(bf16[4,528,128]{2,1,0:T(8,128)(2,1)} %forward.1), calls=%async_computation.1 | async-start | bytes 1081344 | tf_op jit(solution)/shard_map/all_to_all | solution.py:400
  51.1 9.1 %all-to-all-start.2 = ((bf16[4,272,128]{2,1,0:T(8,128)(2,1)}), bf16[4,272,128]{2,1,0:T(8,128)(2,1)S(1)}, u32[]{:S(2)}, u32[]{:S(2)}) async-start(bf16[4,272,128]{2,1,0:T(8,128)(2,1)} %get-tuple-element.39), calls=%async_computation.2 | async-start | bytes 557056 | tf_op jit(solution)/shard_map/all_to_all | solution.py:409
  96.0 13.1 %all-to-all-start.5 = ((f32[32,8,128]{2,1,0:T(8,128)}), f32[32,8,128]{2,1,0:T(8,128)S(1)}, u32[]{:S(2)}, u32[]{:S(2)}) async-start(f32[32,8,128]{2,1,0:T(8,128)} %broadcast_in_dim.15), calls=%async_computation.5 | async-start | bytes 262144 | tf_op jit(solution)/shard_map/all_to_all | solution.py:346

commit v9 on v8

--- a/solution.py
+++ b/solution.py
@@ -141,17 +141,11 @@
     )
 
 
-def own_teacher(ny, scale, q_ref, same_ref, other_ref, acc_ref, stats_ref):
-    _, y, core = place(ny)
-    n, rows = q_ref.shape[0], same_ref.shape[2]
-    col = lax.broadcasted_iota(jnp.int32, (n, ny * rows), 1)
-    row = lax.broadcasted_iota(jnp.int32, (n, ny * rows), 0) // (n // rows)
-    best, accl = teach(
-        q_ref[...],
-        flat(same_ref, 0), with_ones(flat(same_ref, 1)),
-        flat(other_ref, 0), with_ones(flat(other_ref, 1)),
-        scale, (col <= row + y * rows, col < (y + core) * rows),
-    )
+def own_teacher(q, same, other, y, core, rows, scale, acc_ref, stats_ref):
+    n, keys_n = q.shape[0], same[0].shape[0]
+    col = lax.broadcasted_iota(jnp.int32, (n, keys_n), 1)
+    row = lax.broadcasted_iota(jnp.int32, (n, keys_n), 0) // (n // rows)
+    best, accl = teach(q, *same, *other, scale, (col <= row + y * rows, col < (y + core) * rows))
     head = accl.shape[1] // 2
     acc_ref[...] = accl[:, :head]
     lane = lax.broadcasted_iota(jnp.int32, (n, head), 1)
@@ -180,7 +174,7 @@
 
 def forward(nx, ny, scale, *refs):
     later = refs[: nx - 1]
-    other_ref, wk_ref, state_in, full_in, accl_in, pay_ref = refs[nx - 1 :]
+    q_ref, same_ref, other_ref, wk_ref, state_in, full_in, accl_in, pay_ref, acc_ref, stats_ref = refs[nx - 1 :]
     x, y, core = place(ny)
     head = other_ref.shape[3]
     n = later[0].shape[0]
@@ -191,6 +185,11 @@
     state, full = add_states(keys, vals, w2, y + core, state_in[...], full_in[...])
     feats_n = full.shape[0]
     full_high = full[:, :head].astype(BF16)
+
+    own_teacher(
+        q_ref[...], (flat(same_ref, 0), with_ones(flat(same_ref, 1))), (keys, values1),
+        y, core, other_ref.shape[2], scale, acc_ref, stats_ref,
+    )
 
     def two(column):
         high = column.astype(BF16).astype(F32)
@@ -392,15 +391,12 @@
         functools.partial(same_core, nx, ny, scale),
         (f32(feats, feats), f32(feats, feats), f32(nx - 1, n, feats)), (*later, same, w_key), flops=3, name="same_core",
     )
-    pay = call(
+    pay, acc, stats = call(
         functools.partial(forward, nx, ny, scale),
-        bf16(nx, n + feats + 16, head),
-        (*later, other, w_key, state, full, sums), flops=4, name="forward",
+        (bf16(nx, n + feats + 16, head), f32(n, head), f32(8, n)),
+        (*later, q, same, other, w_key, state, full, sums), flops=6, name="forward",
     )
     got = lax.all_to_all(pay, "ctx", 0, 0, tiled=True, axis_index_groups=x_groups)
-    acc, stats = call(
-        functools.partial(own_teacher, ny, scale), (f32(n, head), f32(8, n)), (q, same, other), flops=2, name="own_teacher",
-    )
     out, dnum, dden, state, back, pay, loss = call(
         functools.partial(merge, nx, ny, scale, count),
         (bf16(n, head), f32(n, head), f32(n, head), f32(feats, feats), f32(feats, feats), bf16(nx, feats + 16, head), f32(8, head)),

time: 111 us -> 110 us (level)
  blocking collectives: 33.1 us -> 46.4 us
  waiting for transfers between devices: 31.1 us -> 23.1 us
  starting transfers between devices: 28.6 us -> 24.6 us
  Pallas kernels: 14.2 us -> 12.7 us
    all_to_all x0 -> x1, blocking collectives: none -> 13.2 us  [shards(): lax.all_to_all(pay, 'ctx', 0, 0, tiled=True, axis_index_groups=x_groups)]
    all_to_all x2 -> x1, waiting for transfers between devices: 12.4 us -> 4.39 us  [shards(): lax.all_to_all(pay, 'ctx', 0, 0, tiled=True, axis_index_groups=x_groups)]
    all_to_all x2 -> x1, starting transfers between devices: 7.46 us -> 3.45 us  [shards(): lax.all_to_all(pay, 'ctx', 0, 0, tiled=True, axis_index_groups=x_groups)]
    ppermute x3, waiting for transfers between devices: 6.82 us -> 3.1 us  [shards(): lax.ppermute(q, 'ctx', [(at(x, y, c), at(x - s, y, c)) for x, y, c in eve...]
    all_to_all x1, waiting for transfers between devices: 3.13 us -> 6.84 us  [shards(): lax.all_to_all(kvs, 'ctx', 0, 0, tiled=True, axis_index_groups=y_groups)]
    pallas_call x8 -> x7, Pallas kernels: 14.2 us -> 12.7 us  [call(): pl.pallas_call(body, out_shape=outs, in_specs=[VMEM] * len(args), out_spe...]
    all_to_all x1, blocking collectives: 19.9 us -> 21.1 us  [spread(): lax.all_to_all(copies, axes, 0, 0, tiled=True, axis_index_groups=groups)]
  transfers between devices with their start and end apart: 8 -> 7, of which waited for: 7 -> 6; matrix products, arithmetic and copies ran while one was open for 0% -> 0% of each run, Pallas kernels for 5% -> 4%
where the time goes in v9:
time: 110 us
  blocking collectives  46.4 us (42%)
  starting transfers between devices  24.6 us (22%)
  waiting for transfers between devices  23.1 us (21%)
  Pallas kernels  12.7 us (12%)
  local copies, waits for them, and re-layouts  1.9 us (2%)
    all_to_all x1, blocking collectives, spread(): lax.all_to_all(copies, axes, 0, 0, tiled=True, axis_index_groups=groups)  21.1 us
    all_to_all x1, blocking collectives, shards(): lax.all_to_all(pay, 'ctx', 0, 0, tiled=True, axis_index_groups=x_groups)  13.2 us
    pallas_call x7, Pallas kernels, call(): pl.pallas_call(body, out_shape=outs, in_specs=[VMEM] * len(args), out_spe...  12.7 us
    all_to_all x1, blocking collectives, shards(): lax.all_to_all(grads.reshape(chips, 1, -1), both_axes, 0, 0, tiled=True,...  12.2 us
    all_to_all x1, waiting for transfers between devices, spread(): lax.all_to_all(copies, axes, 0, 0, tiled=True, axis_index_groups=groups)  8.73 us
    all_to_all x1, starting transfers between devices, shards(): lax.all_to_all(kvs, 'ctx', 0, 0, tiled=True, axis_index_groups=y_groups)  7.79 us
    all_to_all x1, waiting for transfers between devices, shards(): lax.all_to_all(kvs, 'ctx', 0, 0, tiled=True, axis_index_groups=y_groups)  6.84 us
    ppermute x1, starting transfers between devices, shards(): other = lax.ppermute(same, 'ctx', swap)  5.59 us
  transfers between devices with their start and end apart: 7, of which 6 were waited for; matrix products, arithmetic and copies ran while one was open for 0% of the time, Pallas kernels for 4%

profile of v9, /device:TPU:1, one launch (start us, length us, event | category | flops | bytes accessed | tf_op | source)
XLA Modules:
  0.0 109.6 jit_solution(9301163357837653879)
XLA Ops:
  0.6 1.6 %copies.1 = bf16[8,2,128,128]{3,2,1,0:T(8,128)(2,1)} custom-call(bf16[128,128]{1,0:T(8,128)(2,1)} %bitcast.20, bf16[128,128]{1,0:T(8,128)(2,1)} %bitcast.23), custom_call_target="tpu_custom_call" | custom-call | flops 1000000000 | bytes 20000000 | tf_op jit(solution)/shard_map/copies/pallas_call | solution.py:363
  2.3 7.8 %all-to-all-start = ((bf16[8,2,128,128]{3,2,1,0:T(8,128)(2,1)}), bf16[8,2,128,128]{3,2,1,0:T(8,128)(2,1)S(1)}, u32[]{:S(2)}, u32[]{:S(2)}) async-start(bf16[8,2,128,128]{3,2,1,0:T(8,128)(2,1)} %copies.1), calls=%async_computation | async-start | bytes 1048576 | tf_op jit(solution)/shard_map/all_to_all | solution.py:379
  10.1 1.3 %collective-permute-start.2 = (bf16[256,128]{1,0:T(8,128)(2,1)S(1)}, bf16[256,128]{1,0:T(8,128)(2,1)S(1)}, u32[]{:S(2)}, u32[]{:S(2)}) collective-permute-start(bf16[256,128]{1,0:T(8,128)(2,1)S(1)} %bitcast.14), channel_id=1, source_target_pairs={{384,0},{392,8},{400,16},{408,24},{416,32},{424,40},{432,48},{440,... | collective-permute-start | bytes 196616 | tf_op jit(solution)/shard_map/ppermute | solution.py:381
  11.4 1.3 %collective-permute-start.1 = (bf16[256,128]{1,0:T(8,128)(2,1)S(1)}, bf16[256,128]{1,0:T(8,128)(2,1)S(1)}, u32[]{:S(2)}, u32[]{:S(2)}) collective-permute-start(bf16[256,128]{1,0:T(8,128)(2,1)S(1)} %bitcast.15), channel_id=1, source_target_pairs={{256,0},{264,8},{272,16},{280,24},{288,32},{296,40},{304,48},{312,... | collective-permute-start | bytes 196616 | tf_op jit(solution)/shard_map/ppermute | solution.py:381
  12.7 1.3 %collective-permute-start = (bf16[256,128]{1,0:T(8,128)(2,1)S(1)}, bf16[256,128]{1,0:T(8,128)(2,1)S(1)}, u32[]{:S(2)}, u32[]{:S(2)}) collective-permute-start(bf16[256,128]{1,0:T(8,128)(2,1)S(1)} %bitcast.16), channel_id=1, source_target_pairs={{128,0},{136,8},{144,16},{152,24},{160,32},{168,40},{176,48},{184,... | collective-permute-start | bytes 196616 | tf_op jit(solution)/shard_map/ppermute | solution.py:381
  14.0 0.9 prepare.1
  14.9 1.4 %collective-permute-done.2.refs_2_ = bf16[256,128]{1,0:T(8,128)(2,1)S(1)} collective-permute-done((bf16[256,128]{1,0:T(8,128)(2,1)S(1)}, bf16[256,128]{1,0:T(8,128)(2,1)S(1)}, u32[]{:S(2)}, u32[]{:S(2)}) %collective-permute-start.2) | collective-permute-done | bytes 65568 | tf_op jit(solution)/shard_map/ppermute | solution.py:381
  16.3 1.6 %collective-permute-done.1.refs_1_ = bf16[256,128]{1,0:T(8,128)(2,1)S(1)} collective-permute-done((bf16[256,128]{1,0:T(8,128)(2,1)S(1)}, bf16[256,128]{1,0:T(8,128)(2,1)S(1)}, u32[]{:S(2)}, u32[]{:S(2)}) %collective-permute-start.1) | collective-permute-done | bytes 65568 | tf_op jit(solution)/shard_map/ppermute | solution.py:381
  18.0 6.8 %all-to-all-done.refs_3_.refs_4_.same_ref = bf16[8,2,128,128]{3,2,1,0:T(8,128)(2,1)S(1)} async-done(((bf16[8,2,128,128]{3,2,1,0:T(8,128)(2,1)}), bf16[8,2,128,128]{3,2,1,0:T(8,128)(2,1)S(1)}, u32[]{:S(2)}, u32[]{:S(2)}) %all-to-all-start) | async-done | bytes 524320 | tf_op jit(solution)/shard_map/all_to_all | solution.py:379
  24.8 5.6 %collective-permute-start.3 = (bf16[8,2,128,128]{3,2,1,0:T(8,128)(2,1)S(1)}, bf16[8,2,128,128]{3,2,1,0:T(8,128)(2,1)S(1)}, u32[]{:S(2)}, u32[]{:S(2)}) collective-permute-start(bf16[8,2,128,128]{3,2,1,0:T(8,128)(2,1)S(1)} %all-to-all-done.refs_3_.refs_4_.same_ref), channel_id=1, source_target_pairs={{0,8},{8,0},{16,24},{24,16},{32,40},{40,32},{48,56},{56,48},{64,72... | collective-permute-start | bytes 1572872 | tf_op jit(solution)/shard_map/ppermute | solution.py:389
  30.4 2.0 %same_core.1 = (f32[256,256]{1,0:T(8,128)S(1)}, f32[256,256]{1,0:T(8,128)S(1)}, f32[3,256,256]{2,1,0:T(8,128)S(1)}) custom-call(bf16[256,128]{1,0:T(8,128)(2,1)S(1)} %collective-permute-done.refs_0_, bf16[256,128]{1,0:T(8,128)(2,1)S(1)} %collective-permute-done.1.refs_1_, bf16[256,128]{1,0:T(8,128)(2,1)S(1)} %collective-permute-done.2.refs_2_, ...), custom_call_target="tpu_custom_call" | custom-call | flops 3000000000 | bytes 20000000 | tf_op jit(solution)/shard_map/same_core/pallas_call | solution.py:363
  32.5 3.2 %forward.1 = (bf16[4,528,128]{2,1,0:T(8,128)(2,1)S(1)}, f32[256,128]{1,0:T(8,128)S(1)}, f32[8,256]{1,0:T(8,128)S(1)}) custom-call(bf16[256,128]{1,0:T(8,128)(2,1)S(1)} %collective-permute-done.refs_0_, bf16[256,128]{1,0:T(8,128)(2,1)S(1)} %collective-permute-done.1.refs_1_, bf16[256,128]{1,0:T(8,128)(2,1)S(1)} %collective-permute-done.2.refs_2_, ...), custom_call_target="tpu_custom_call" | custom-call | flops 6000000000 | bytes 20000000 | tf_op jit(solution)/shard_map/forward/pallas_call | solution.py:363
  35.7 13.2 %all_to_all.30.got_ref = bf16[4,528,128]{2,1,0:T(8,128)(2,1)S(1)} all-to-all(bf16[4,528,128]{2,1,0:T(8,128)(2,1)S(1)} %get-tuple-element.36), channel_id=1, replica_groups={{0,128,256,384},{8,136,264,392},{16,144,272,400},{24,152,280,408},{32,1..., dimensions={0} | all-to-all | bytes 1081344 | tf_op jit(solution)/shard_map/all_to_all | solution.py:399
  48.9 1.9 %merge.1 = (bf16[256,128]{1,0:T(8,128)(2,1)}, f32[256,128]{1,0:T(8,128)S(1)}, f32[256,128]{1,0:T(8,128)S(1)}, f32[256,256]{1,0:T(8,128)S(1)}, f32[256,256]{1,0:T...) custom-call(f32[256,128]{1,0:T(8,128)S(1)} %get-tuple-element.34.acc_in, ...), custom_call_target="tpu_custom_call" | custom-call | flops 2000000000 | bytes 20000000 | tf_op jit(solution)/shard_map/merge/pallas_call | solution.py:363
  50.7 3.4 %all-to-all-start.2 = ((bf16[4,272,128]{2,1,0:T(8,128)(2,1)}), bf16[4,272,128]{2,1,0:T(8,128)(2,1)S(1)}, u32[]{:S(2)}, u32[]{:S(2)}) async-start(bf16[4,272,128]{2,1,0:T(8,128)(2,1)} %get-tuple-element.41), calls=%async_computation.2 | async-start | bytes 557056 | tf_op jit(solution)/shard_map/all_to_all | solution.py:405
  54.2 1.2 %near_grads.1.near_ref = f32[256,128]{1,0:T(8,128)S(1)} custom-call(bf16[256,128]{1,0:T(8,128)(2,1)S(1)} %bitcast.19, bf16[128,128]{1,0:T(8,128)(2,1)S(1)} %bitcast.22, bf16[128,128]{1,0:T(8,128)(2,1)S(1)} %bitcast.25, f32[128,128]{1,0:T(8,128)S(1)} %copy-done.1, f32[128,128]{1,0:T(8,128)S(1)} %copy-done.2, f32[256,128]{1,0:T(8,128)S(1)} %get-tuple-element.42.dnum_ref, ...), custom_call_target="tpu_custom_call" | custom-call | flops 2000000000 | bytes 20000000 | tf_op jit(solution)/shard_map/near_grads/pallas_call | solution.py:363
  55.4 4.4 %all-to-all-done.2.got_ref = bf16[4,272,128]{2,1,0:T(8,128)(2,1)S(1)} async-done(((bf16[4,272,128]{2,1,0:T(8,128)(2,1)}), bf16[4,272,128]{2,1,0:T(8,128)(2,1)S(1)}, u32[]{:S(2)}, u32[]{:S(2)}) %all-to-all-start.2) | async-done | bytes 278560 | tf_op jit(solution)/shard_map/all_to_all | solution.py:405
  59.8 1.9 %backward.1 = f32[288,128]{1,0:T(8,128)S(1)} custom-call(bf16[8,2,128,128]{3,2,1,0:T(8,128)(2,1)S(1)} %all-to-all-done.refs_3_.refs_4_.same_ref, bf16[8,2,128,128]{3,2,1,0:T(8,128)(2,1)S(1)} %collective-permute-done.3.refs_5_.other_ref, f32[128,128]{1,0:T(8,128)S(1)} %copy-done.2, f32[256,256]{1,0:T(8,128)S(1)} %get-tuple-element.40.back_in, ...), custom_call_target="tpu_custom_call" | custom-call | flops 4000000000 | bytes 20000000 | tf_op jit(solution)/shard_map/backward/pallas_call | solution.py:363
  61.7 12.2 %all_to_all.31 = f32[32,1,1152]{2,1,0:T(1,128)S(1)} all-to-all(f32[32,1,1152]{2,1,0:T(1,128)S(1)} %bitcast.13), channel_id=1, replica_groups={{0,16,32,48,64,80,96,112,128,144,160,176,192,208,224,240,256,272,288,30..., dimensions={0} | all-to-all | bytes 294912 | tf_op jit(solution)/shard_map/all_to_all | solution.py:424
  74.0 21.1 %all_to_all.32 = f32[16,1,1152]{2,1,0:T(1,128)S(1)} all-to-all(f32[16,1,1152]{2,1,0:T(1,128)S(1)} %broadcast_in_dim.6), channel_id=1, replica_groups={{0,1,2,3,4,5,6,7,8,9,10,11,12,13,14,15},{16,17,18,19,20,21,22,23,24,25,..., dimensions={0} | all-to-all | bytes 147456 | tf_op jit(solution)/shard_map/all_to_all | solution.py:345
  95.2 0.7 broadcast_in_dim.15
  95.8 3.9 %all-to-all-start.5 = ((f32[32,8,128]{2,1,0:T(8,128)}), f32[32,8,128]{2,1,0:T(8,128)S(1)}, u32[]{:S(2)}, u32[]{:S(2)}) async-start(f32[32,8,128]{2,1,0:T(8,128)} %broadcast_in_dim.15), calls=%async_computation.5 | async-start | bytes 262144 | tf_op jit(solution)/shard_map/all_to_all | solution.py:345
  100.2 8.7 %all-to-all-done.5 = f32[32,8,128]{2,1,0:T(8,128)S(1)} async-done(((f32[32,8,128]{2,1,0:T(8,128)}), f32[32,8,128]{2,1,0:T(8,128)S(1)}, u32[]{:S(2)}, u32[]{:S(2)}) %all-to-all-start.5) | async-done | bytes 131104 | tf_op jit(solution)/shard_map/all_to_all | solution.py:345
  108.9 0.7 slice_bitcast_fusion
  (18 shorter events, 0.8 us)
Async XLA Ops:
  2.3 7.8 %copy-start = (bf16[128,1,2,128]{3,2,1,0:T(2,128)(2,1)S(1)}, bf16[128,1,2,128]{3,2,1,0:T(2,128)(2,1)}, u32[]{:S(2)}) copy-start(bf16[128,1,2,128]{3,2,1,0:T(2,128)(2,1)} %param.5) | copy-start | bytes 196612
  2.3 11.7 %copy-start.1 = (f32[128,128]{1,0:T(8,128)S(1)}, f32[128,128]{1,0:T(8,128)}, u32[]{:S(2)}) copy-start(f32[128,128]{1,0:T(8,128)} %wq_ref.3) | copy-start | bytes 196612
  2.3 11.7 %copy-start.2 = (f32[128,128]{1,0:T(8,128)S(1)}, f32[128,128]{1,0:T(8,128)}, u32[]{:S(2)}) copy-start(f32[128,128]{1,0:T(8,128)} %wk_ref.5) | copy-start | bytes 196612
  2.3 11.7 %copy-start.3 = (bf16[128,1,128]{2,0,1:T(8,128)(2,1)S(1)}, bf16[128,1,128]{2,0,1:T(8,128)(2,1)}, u32[]{:S(2)}) copy-start(bf16[128,1,128]{2,0,1:T(8,128)(2,1)} %param.6) | copy-start | bytes 98308
  2.3 11.7 %copy-start.4 = (bf16[128,1,128]{2,0,1:T(8,128)(2,1)S(1)}, bf16[128,1,128]{2,0,1:T(8,128)(2,1)}, u32[]{:S(2)}) copy-start(bf16[128,1,128]{2,0,1:T(8,128)(2,1)} %param.7) | copy-start | bytes 98308
  2.3 22.5 %all-to-all-start = ((bf16[8,2,128,128]{3,2,1,0:T(8,128)(2,1)}), bf16[8,2,128,128]{3,2,1,0:T(8,128)(2,1)S(1)}, u32[]{:S(2)}, u32[]{:S(2)}) async-start(bf16[8,2,128,128]{3,2,1,0:T(8,128)(2,1)} %copies.1), calls=%async_computation | async-start | bytes 1048576 | tf_op jit(solution)/shard_map/all_to_all | solution.py:379
  10.1 6.2 %collective-permute-start.2 = (bf16[256,128]{1,0:T(8,128)(2,1)S(1)}, bf16[256,128]{1,0:T(8,128)(2,1)S(1)}, u32[]{:S(2)}, u32[]{:S(2)}) collective-permute-start(bf16[256,128]{1,0:T(8,128)(2,1)S(1)} %bitcast.14), channel_id=1, source_target_pairs={{384,0},{392,8},{400,16},{408,24},{416,32},{424,40},{432,48},{440,... | collective-permute-start | bytes 196616 | tf_op jit(solution)/shard_map/ppermute | solution.py:381
  11.4 6.5 %collective-permute-start.1 = (bf16[256,128]{1,0:T(8,128)(2,1)S(1)}, bf16[256,128]{1,0:T(8,128)(2,1)S(1)}, u32[]{:S(2)}, u32[]{:S(2)}) collective-permute-start(bf16[256,128]{1,0:T(8,128)(2,1)S(1)} %bitcast.15), channel_id=1, source_target_pairs={{256,0},{264,8},{272,16},{280,24},{288,32},{296,40},{304,48},{312,... | collective-permute-start | bytes 196616 | tf_op jit(solution)/shard_map/ppermute | solution.py:381
  12.7 5.3 %collective-permute-start = (bf16[256,128]{1,0:T(8,128)(2,1)S(1)}, bf16[256,128]{1,0:T(8,128)(2,1)S(1)}, u32[]{:S(2)}, u32[]{:S(2)}) collective-permute-start(bf16[256,128]{1,0:T(8,128)(2,1)S(1)} %bitcast.16), channel_id=1, source_target_pairs={{128,0},{136,8},{144,16},{152,24},{160,32},{168,40},{176,48},{184,... | collective-permute-start | bytes 196616 | tf_op jit(solution)/shard_map/ppermute | solution.py:381
  24.8 7.6 %collective-permute-start.3 = (bf16[8,2,128,128]{3,2,1,0:T(8,128)(2,1)S(1)}, bf16[8,2,128,128]{3,2,1,0:T(8,128)(2,1)S(1)}, u32[]{:S(2)}, u32[]{:S(2)}) collective-permute-start(bf16[8,2,128,128]{3,2,1,0:T(8,128)(2,1)S(1)} %all-to-all-done.refs_3_.refs_4_.same_ref), channel_id=1, source_target_pairs={{0,8},{8,0},{16,24},{24,16},{32,40},{40,32},{48,56},{56,48},{64,72... | collective-permute-start | bytes 1572872 | tf_op jit(solution)/shard_map/ppermute | solution.py:389
  50.7 9.0 %all-to-all-start.2 = ((bf16[4,272,128]{2,1,0:T(8,128)(2,1)}), bf16[4,272,128]{2,1,0:T(8,128)(2,1)S(1)}, u32[]{:S(2)}, u32[]{:S(2)}) async-start(bf16[4,272,128]{2,1,0:T(8,128)(2,1)} %get-tuple-element.41), calls=%async_computation.2 | async-start | bytes 557056 | tf_op jit(solution)/shard_map/all_to_all | solution.py:405
  95.8 13.1 %all-to-all-start.5 = ((f32[32,8,128]{2,1,0:T(8,128)}), f32[32,8,128]{2,1,0:T(8,128)S(1)}, u32[]{:S(2)}, u32[]{:S(2)}) async-start(f32[32,8,128]{2,1,0:T(8,128)} %broadcast_in_dim.15), calls=%async_computation.5 | async-start | bytes 262144 | tf_op jit(solution)/shard_map/all_to_all | solution.py:345

commit v10 on v9

--- a/solution.py
+++ b/solution.py
@@ -279,25 +279,23 @@
         pay_ref[d, feats_n:] = rows
 
 
-def near_grads(q_ref, k_ref, v_ref, wq_ref, wk_ref, dnum_ref, dden_ref, state_ref, grads_ref):
-    q, kd, vd = q_ref[...], k_ref[...], v_ref[...]
+def near_grads(q, kd, vd, wq, wk, d_num, d_den, state):
     head, rows = kd.shape[1], kd.shape[0]
-    d_num, d_den = dnum_ref[...], dden_ref[...]
-    fq_t, sig_q, fk_t, sig_d = own_features(q, kd, wq_ref[...], wk_ref[...])
+    fq_t, sig_q, fk_t, sig_d = own_features(q, kd, wq, wk)
     d_attn = jnp.where(diagonal(q.shape[0], rows), dot2(d_num, vd, NT) + d_den[:, :rows], 0.0)
     lane = lax.broadcasted_iota(jnp.int32, d_den.shape, 1)
     d_aug = jnp.concatenate([d_num, jnp.where(lane == 0, d_den, 0.0)], 1)
-    d_fq = dot3(state_ref[...], d_aug, NT) + dot3(fk_t, d_attn, NT)
+    d_fq = dot3(state, d_aug, NT) + dot3(fk_t, d_attn, NT)
     d_pre = d_fq[:head] * sig_q - d_fq[head:] * (1.0 - sig_q)
-    grads_ref[:head] = dot2(d_pre, q)
+    grad_q = dot2(d_pre, q)
     d_fk = dot3(fq_t, d_attn)
     d_pre = d_fk[:head] * sig_d - d_fk[head:] * (1.0 - sig_d)
-    grads_ref[head:] = dot2(d_pre, kd)
+    return grad_q, dot2(d_pre, kd)
 
 
 def backward(
     nx, ny,
-    same_ref, other_ref, wk_ref, back_in, got_ref, near_ref, loss_ref,
+    same_ref, other_ref, q_ref, k_ref, v_ref, wq_ref, wk_ref, dnum_ref, dden_ref, state_ref, back_in, got_ref, loss_ref,
     grad_ref, sum_ref,
 ):
     x, y, core = place(ny)
@@ -322,13 +320,15 @@
     two = jnp.concatenate([own2, after2], 0)
     key = lax.broadcasted_iota(jnp.int32, (1, keys_n), 1)
     w2 = jnp.concatenate(halves(wk_ref[...].T), 1)
-    total = near_ref[head:]
+    grad_q, total = near_grads(
+        q_ref[...], k_ref[...], v_ref[...], wq_ref[...], wk_ref[...], dnum_ref[...], dden_ref[...], state_ref[...]
+    )
     for half, ref in enumerate((same_ref, other_ref)):
         z = dot(two, pair(flat(ref, 1)), NT)
         d = jnp.where(key < (y + half * core) * rows, z[: 2 * head] + own_n, 0.0) + (z[2 * head :] + after_n)
         _, _, sig = feature_parts(dot(w2, pair(flat(ref, 0)), NT))
         total += dot2(sig * d[:head] - d[head:], flat(ref, 0))
-    sum_ref[:head] = near_ref[:head].T
+    sum_ref[:head] = grad_q.T
     sum_ref[head:] = total.T
     chunks = grad_ref.shape[0] - 2 * head
     parts = 2 * head // chunks
@@ -403,9 +403,6 @@
         (acc, stats, got, fq, near), flops=2, name="merge",
     )
     got = lax.all_to_all(pay, "ctx", 0, 0, tiled=True, axis_index_groups=x_groups)
-    grads = call(
-        near_grads, f32(feats, head), (q, k, v, w_query, w_key, dnum, dden, state), flops=2, name="near_grads",
-    )
     both_axes = ("ctx", "kvh")
     chips = nx * ny
     chip_groups = [
@@ -418,7 +415,7 @@
     grads = call(
         functools.partial(backward, nx, ny),
         f32(chips * (parts + 1), head),
-        (same, other, w_key, back, got, grads, loss),
+        (same, other, q, k, v, w_query, w_key, dnum, dden, state, back, got, loss),
         scratch=(pltpu.VMEM((feats, head), F32),), flops=4, name="backward",
     )
     mine = lax.all_to_all(

time: 110 us -> 110 us (level)
  blocking collectives: 46.4 us -> 54.4 us
  waiting for transfers between devices: 23.1 us -> 18.7 us
  starting transfers between devices: 24.6 us -> 21.1 us
    all_to_all x1 -> x2, blocking collectives: 13.2 us -> 21.1 us  [shards(): lax.all_to_all(pay, 'ctx', 0, 0, tiled=True, axis_index_groups=x_groups)]
    all_to_all x1 -> x0, waiting for transfers between devices: 4.39 us -> none  [shards(): lax.all_to_all(pay, 'ctx', 0, 0, tiled=True, axis_index_groups=x_groups)]
    all_to_all x1 -> x0, starting transfers between devices: 3.45 us -> none  [shards(): lax.all_to_all(pay, 'ctx', 0, 0, tiled=True, axis_index_groups=x_groups)]
    pallas_call x7 -> x6, Pallas kernels: 12.7 us -> 12.2 us  [call(): pl.pallas_call(body, out_shape=outs, in_specs=[VMEM] * len(args), out_spe...]
  transfers between devices with their start and end apart: 7 -> 6, of which waited for: 6 -> 5; matrix products, arithmetic and copies ran while one was open for 0% -> 0% of each run, Pallas kernels for 4% -> 3%
where the time goes in v10:
time: 110 us; the launch traced here: 109 us
  blocking collectives  54.4 us (49%)
  starting transfers between devices  21.1 us (19%)
  waiting for transfers between devices  18.7 us (17%)
  Pallas kernels  12.2 us (11%)
  local copies, waits for them, and re-layouts  1.9 us (2%)
    all_to_all x2, blocking collectives, shards(): lax.all_to_all(pay, 'ctx', 0, 0, tiled=True, axis_index_groups=x_groups)  21.1 us
    all_to_all x1, blocking collectives, spread(): lax.all_to_all(copies, axes, 0, 0, tiled=True, axis_index_groups=groups)  21.1 us
    pallas_call x6, Pallas kernels, call(): pl.pallas_call(body, out_shape=outs, in_specs=[VMEM] * len(args), out_spe...  12.2 us
    all_to_all x1, blocking collectives, shards(): lax.all_to_all(grads.reshape(chips, 1, -1), both_axes, 0, 0, tiled=True,...  12.2 us
    all_to_all x1, waiting for transfers between devices, spread(): lax.all_to_all(copies, axes, 0, 0, tiled=True, axis_index_groups=groups)  8.73 us
    all_to_all x1, starting transfers between devices, shards(): lax.all_to_all(kvs, 'ctx', 0, 0, tiled=True, axis_index_groups=y_groups)  7.79 us
    all_to_all x1, waiting for transfers between devices, shards(): lax.all_to_all(kvs, 'ctx', 0, 0, tiled=True, axis_index_groups=y_groups)  6.84 us
    ppermute x1, starting transfers between devices, shards(): other = lax.ppermute(same, 'ctx', swap)  5.59 us
  transfers between devices with their start and end apart: 6, of which 5 were waited for; matrix products, arithmetic and copies ran while one was open for 0% of the time, Pallas kernels for 3%

profile of v10, /device:TPU:1, one launch (start us, length us, event | category | flops | bytes accessed | tf_op | source)
XLA Modules:
  0.0 109.3 jit_solution(12035359142058550965)
XLA Ops:
  0.6 1.6 %copies.1 = bf16[8,2,128,128]{3,2,1,0:T(8,128)(2,1)} custom-call(bf16[128,128]{1,0:T(8,128)(2,1)} %bitcast.20, bf16[128,128]{1,0:T(8,128)(2,1)} %bitcast.23), custom_call_target="tpu_custom_call" | custom-call | flops 1000000000 | bytes 20000000 | tf_op jit(solution)/shard_map/copies/pallas_call | solution.py:363
  2.3 7.8 %all-to-all-start = ((bf16[8,2,128,128]{3,2,1,0:T(8,128)(2,1)}), bf16[8,2,128,128]{3,2,1,0:T(8,128)(2,1)S(1)}, u32[]{:S(2)}, u32[]{:S(2)}) async-start(bf16[8,2,128,128]{3,2,1,0:T(8,128)(2,1)} %copies.1), calls=%async_computation | async-start | bytes 1048576 | tf_op jit(solution)/shard_map/all_to_all | solution.py:379
  10.1 1.3 %collective-permute-start.2 = (bf16[256,128]{1,0:T(8,128)(2,1)S(1)}, bf16[256,128]{1,0:T(8,128)(2,1)S(1)}, u32[]{:S(2)}, u32[]{:S(2)}) collective-permute-start(bf16[256,128]{1,0:T(8,128)(2,1)S(1)} %bitcast.14), channel_id=1, source_target_pairs={{384,0},{392,8},{400,16},{408,24},{416,32},{424,40},{432,48},{440,... | collective-permute-start | bytes 196616 | tf_op jit(solution)/shard_map/ppermute | solution.py:381
  11.4 1.3 %collective-permute-start.1 = (bf16[256,128]{1,0:T(8,128)(2,1)S(1)}, bf16[256,128]{1,0:T(8,128)(2,1)S(1)}, u32[]{:S(2)}, u32[]{:S(2)}) collective-permute-start(bf16[256,128]{1,0:T(8,128)(2,1)S(1)} %bitcast.15), channel_id=1, source_target_pairs={{256,0},{264,8},{272,16},{280,24},{288,32},{296,40},{304,48},{312,... | collective-permute-start | bytes 196616 | tf_op jit(solution)/shard_map/ppermute | solution.py:381
  12.7 1.3 %collective-permute-start = (bf16[256,128]{1,0:T(8,128)(2,1)S(1)}, bf16[256,128]{1,0:T(8,128)(2,1)S(1)}, u32[]{:S(2)}, u32[]{:S(2)}) collective-permute-start(bf16[256,128]{1,0:T(8,128)(2,1)S(1)} %bitcast.16), channel_id=1, source_target_pairs={{128,0},{136,8},{144,16},{152,24},{160,32},{168,40},{176,48},{184,... | collective-permute-start | bytes 196616 | tf_op jit(solution)/shard_map/ppermute | solution.py:381
  14.0 0.8 prepare.1
  14.9 1.4 %collective-permute-done.2.refs_2_ = bf16[256,128]{1,0:T(8,128)(2,1)S(1)} collective-permute-done((bf16[256,128]{1,0:T(8,128)(2,1)S(1)}, bf16[256,128]{1,0:T(8,128)(2,1)S(1)}, u32[]{:S(2)}, u32[]{:S(2)}) %collective-permute-start.2) | collective-permute-done | bytes 65568 | tf_op jit(solution)/shard_map/ppermute | solution.py:381
  16.3 1.6 %collective-permute-done.1.refs_1_ = bf16[256,128]{1,0:T(8,128)(2,1)S(1)} collective-permute-done((bf16[256,128]{1,0:T(8,128)(2,1)S(1)}, bf16[256,128]{1,0:T(8,128)(2,1)S(1)}, u32[]{:S(2)}, u32[]{:S(2)}) %collective-permute-start.1) | collective-permute-done | bytes 65568 | tf_op jit(solution)/shard_map/ppermute | solution.py:381
  18.0 6.8 %all-to-all-done.refs_3_.refs_4_.same_ref = bf16[8,2,128,128]{3,2,1,0:T(8,128)(2,1)S(1)} async-done(((bf16[8,2,128,128]{3,2,1,0:T(8,128)(2,1)}), bf16[8,2,128,128]{3,2,1,0:T(8,128)(2,1)S(1)}, u32[]{:S(2)}, u32[]{:S(2)}) %all-to-all-start) | async-done | bytes 524320 | tf_op jit(solution)/shard_map/all_to_all | solution.py:379
  24.9 5.6 %collective-permute-start.3 = (bf16[8,2,128,128]{3,2,1,0:T(8,128)(2,1)S(1)}, bf16[8,2,128,128]{3,2,1,0:T(8,128)(2,1)S(1)}, u32[]{:S(2)}, u32[]{:S(2)}) collective-permute-start(bf16[8,2,128,128]{3,2,1,0:T(8,128)(2,1)S(1)} %all-to-all-done.refs_3_.refs_4_.same_ref), channel_id=1, source_target_pairs={{0,8},{8,0},{16,24},{24,16},{32,40},{40,32},{48,56},{56,48},{64,72... | collective-permute-start | bytes 1572872 | tf_op jit(solution)/shard_map/ppermute | solution.py:389
  30.5 2.0 %same_core.1 = (f32[256,256]{1,0:T(8,128)S(1)}, f32[256,256]{1,0:T(8,128)S(1)}, f32[3,256,256]{2,1,0:T(8,128)S(1)}) custom-call(bf16[256,128]{1,0:T(8,128)(2,1)S(1)} %collective-permute-done.refs_0_, bf16[256,128]{1,0:T(8,128)(2,1)S(1)} %collective-permute-done.1.refs_1_, bf16[256,128]{1,0:T(8,128)(2,1)S(1)} %collective-permute-done.2.refs_2_, ...), custom_call_target="tpu_custom_call" | custom-call | flops 3000000000 | bytes 20000000 | tf_op jit(solution)/shard_map/same_core/pallas_call | solution.py:363
  32.5 3.2 %forward.1 = (bf16[4,528,128]{2,1,0:T(8,128)(2,1)S(1)}, f32[256,128]{1,0:T(8,128)S(1)}, f32[8,256]{1,0:T(8,128)S(1)}) custom-call(bf16[256,128]{1,0:T(8,128)(2,1)S(1)} %collective-permute-done.refs_0_, bf16[256,128]{1,0:T(8,128)(2,1)S(1)} %collective-permute-done.1.refs_1_, bf16[256,128]{1,0:T(8,128)(2,1)S(1)} %collective-permute-done.2.refs_2_, ...), custom_call_target="tpu_custom_call" | custom-call | flops 6000000000 | bytes 20000000 | tf_op jit(solution)/shard_map/forward/pallas_call | solution.py:363
  35.7 13.2 %all_to_all.30.got_ref = bf16[4,528,128]{2,1,0:T(8,128)(2,1)S(1)} all-to-all(bf16[4,528,128]{2,1,0:T(8,128)(2,1)S(1)} %get-tuple-element.36), channel_id=1, replica_groups={{0,128,256,384},{8,136,264,392},{16,144,272,400},{24,152,280,408},{32,1..., dimensions={0} | all-to-all | bytes 1081344 | tf_op jit(solution)/shard_map/all_to_all | solution.py:399
  48.9 1.7 %merge.1 = (bf16[256,128]{1,0:T(8,128)(2,1)}, f32[256,128]{1,0:T(8,128)S(1)}, f32[256,128]{1,0:T(8,128)S(1)}, f32[256,256]{1,0:T(8,128)S(1)}, f32[256,256]{1,0:T...) custom-call(f32[256,128]{1,0:T(8,128)S(1)} %get-tuple-element.34.acc_in, ...), custom_call_target="tpu_custom_call" | custom-call | flops 2000000000 | bytes 20000000 | tf_op jit(solution)/shard_map/merge/pallas_call | solution.py:363
  50.5 8.0 %all_to_all.31.got_ref = bf16[4,272,128]{2,1,0:T(8,128)(2,1)S(1)} all-to-all(bf16[4,272,128]{2,1,0:T(8,128)(2,1)S(1)} %get-tuple-element.44), channel_id=1, replica_groups={{0,128,256,384},{8,136,264,392},{16,144,272,400},{24,152,280,408},{32,1..., dimensions={0} | all-to-all | bytes 557056 | tf_op jit(solution)/shard_map/all_to_all | solution.py:405
  58.5 2.9 %backward.1 = f32[288,128]{1,0:T(8,128)S(1)} custom-call(bf16[8,2,128,128]{3,2,1,0:T(8,128)(2,1)S(1)} %all-to-all-done.refs_3_.refs_4_.same_ref, bf16[8,2,128,128]{3,2,1,0:T(8,128)(2,1)S(1)} %collective-permute-done.3.refs_5_.other_ref, bf16[256,128]{1,0:T(8,128)(2,1)S(1)} %bitcast.19, bf16[128,128]{1,0:T(8,128)(2,1)S(1)} %bitcast.22, ...), custom_call_target="tpu_custom_call" | custom-call | flops 4000000000 | bytes 20000000 | tf_op jit(solution)/shard_map/backward/pallas_call | solution.py:363
  61.4 12.2 %all_to_all.32 = f32[32,1,1152]{2,1,0:T(1,128)S(1)} all-to-all(f32[32,1,1152]{2,1,0:T(1,128)S(1)} %bitcast.13), channel_id=1, replica_groups={{0,16,32,48,64,80,96,112,128,144,160,176,192,208,224,240,256,272,288,30..., dimensions={0} | all-to-all | bytes 294912 | tf_op jit(solution)/shard_map/all_to_all | solution.py:421
  73.5 0.1 reduce_sum.20
  73.7 21.1 %all_to_all.33 = f32[16,1,1152]{2,1,0:T(1,128)S(1)} all-to-all(f32[16,1,1152]{2,1,0:T(1,128)S(1)} %broadcast_in_dim.6), channel_id=1, replica_groups={{0,1,2,3,4,5,6,7,8,9,10,11,12,13,14,15},{16,17,18,19,20,21,22,23,24,25,..., dimensions={0} | all-to-all | bytes 147456 | tf_op jit(solution)/shard_map/all_to_all | solution.py:345
  94.9 0.7 broadcast_in_dim.15
  95.5 3.8 %all-to-all-start.5 = ((f32[32,8,128]{2,1,0:T(8,128)}), f32[32,8,128]{2,1,0:T(8,128)S(1)}, u32[]{:S(2)}, u32[]{:S(2)}) async-start(f32[32,8,128]{2,1,0:T(8,128)} %broadcast_in_dim.15), calls=%async_computation.5 | async-start | bytes 262144 | tf_op jit(solution)/shard_map/all_to_all | solution.py:345
  99.4 0.5 slice.21
  99.9 8.7 %all-to-all-done.5 = f32[32,8,128]{2,1,0:T(8,128)S(1)} async-done(((f32[32,8,128]{2,1,0:T(8,128)}), f32[32,8,128]{2,1,0:T(8,128)S(1)}, u32[]{:S(2)}, u32[]{:S(2)}) %all-to-all-start.5) | async-done | bytes 131104 | tf_op jit(solution)/shard_map/all_to_all | solution.py:345
  108.6 0.7 slice_bitcast_fusion
  (16 shorter events, 0.2 us)
Async XLA Ops:
  2.3 7.8 %copy-start = (bf16[128,1,2,128]{3,2,1,0:T(2,128)(2,1)S(1)}, bf16[128,1,2,128]{3,2,1,0:T(2,128)(2,1)}, u32[]{:S(2)}) copy-start(bf16[128,1,2,128]{3,2,1,0:T(2,128)(2,1)} %param.5) | copy-start | bytes 196612
  2.3 11.7 %copy-start.1 = (f32[128,128]{1,0:T(8,128)S(1)}, f32[128,128]{1,0:T(8,128)}, u32[]{:S(2)}) copy-start(f32[128,128]{1,0:T(8,128)} %wk_ref.3) | copy-start | bytes 196612
  2.3 11.7 %copy-start.2 = (f32[128,128]{1,0:T(8,128)S(1)}, f32[128,128]{1,0:T(8,128)}, u32[]{:S(2)}) copy-start(f32[128,128]{1,0:T(8,128)} %wq_ref.3) | copy-start | bytes 196612
  2.3 11.7 %copy-start.3 = (bf16[128,1,128]{2,0,1:T(8,128)(2,1)S(1)}, bf16[128,1,128]{2,0,1:T(8,128)(2,1)}, u32[]{:S(2)}) copy-start(bf16[128,1,128]{2,0,1:T(8,128)(2,1)} %param.6) | copy-start | bytes 98308
  2.3 11.7 %copy-start.4 = (bf16[128,1,128]{2,0,1:T(8,128)(2,1)S(1)}, bf16[128,1,128]{2,0,1:T(8,128)(2,1)}, u32[]{:S(2)}) copy-start(bf16[128,1,128]{2,0,1:T(8,128)(2,1)} %param.7) | copy-start | bytes 98308
  2.3 22.5 %all-to-all-start = ((bf16[8,2,128,128]{3,2,1,0:T(8,128)(2,1)}), bf16[8,2,128,128]{3,2,1,0:T(8,128)(2,1)S(1)}, u32[]{:S(2)}, u32[]{:S(2)}) async-start(bf16[8,2,128,128]{3,2,1,0:T(8,128)(2,1)} %copies.1), calls=%async_computation | async-start | bytes 1048576 | tf_op jit(solution)/shard_map/all_to_all | solution.py:379
  10.1 6.2 %collective-permute-start.2 = (bf16[256,128]{1,0:T(8,128)(2,1)S(1)}, bf16[256,128]{1,0:T(8,128)(2,1)S(1)}, u32[]{:S(2)}, u32[]{:S(2)}) collective-permute-start(bf16[256,128]{1,0:T(8,128)(2,1)S(1)} %bitcast.14), channel_id=1, source_target_pairs={{384,0},{392,8},{400,16},{408,24},{416,32},{424,40},{432,48},{440,... | collective-permute-start | bytes 196616 | tf_op jit(solution)/shard_map/ppermute | solution.py:381
  11.4 6.5 %collective-permute-start.1 = (bf16[256,128]{1,0:T(8,128)(2,1)S(1)}, bf16[256,128]{1,0:T(8,128)(2,1)S(1)}, u32[]{:S(2)}, u32[]{:S(2)}) collective-permute-start(bf16[256,128]{1,0:T(8,128)(2,1)S(1)} %bitcast.15), channel_id=1, source_target_pairs={{256,0},{264,8},{272,16},{280,24},{288,32},{296,40},{304,48},{312,... | collective-permute-start | bytes 196616 | tf_op jit(solution)/shard_map/ppermute | solution.py:381
  12.7 5.3 %collective-permute-start = (bf16[256,128]{1,0:T(8,128)(2,1)S(1)}, bf16[256,128]{1,0:T(8,128)(2,1)S(1)}, u32[]{:S(2)}, u32[]{:S(2)}) collective-permute-start(bf16[256,128]{1,0:T(8,128)(2,1)S(1)} %bitcast.16), channel_id=1, source_target_pairs={{128,0},{136,8},{144,16},{152,24},{160,32},{168,40},{176,48},{184,... | collective-permute-start | bytes 196616 | tf_op jit(solution)/shard_map/ppermute | solution.py:381
  24.9 7.6 %collective-permute-start.3 = (bf16[8,2,128,128]{3,2,1,0:T(8,128)(2,1)S(1)}, bf16[8,2,128,128]{3,2,1,0:T(8,128)(2,1)S(1)}, u32[]{:S(2)}, u32[]{:S(2)}) collective-permute-start(bf16[8,2,128,128]{3,2,1,0:T(8,128)(2,1)S(1)} %all-to-all-done.refs_3_.refs_4_.same_ref), channel_id=1, source_target_pairs={{0,8},{8,0},{16,24},{24,16},{32,40},{40,32},{48,56},{56,48},{64,72... | collective-permute-start | bytes 1572872 | tf_op jit(solution)/shard_map/ppermute | solution.py:389
  95.5 13.1 %all-to-all-start.5 = ((f32[32,8,128]{2,1,0:T(8,128)}), f32[32,8,128]{2,1,0:T(8,128)S(1)}, u32[]{:S(2)}, u32[]{:S(2)}) async-start(f32[32,8,128]{2,1,0:T(8,128)} %broadcast_in_dim.15), calls=%async_computation.5 | async-start | bytes 262144 | tf_op jit(solution)/shard_map/all_to_all | solution.py:345

commit v11 on v9

--- a/solution.py
+++ b/solution.py
@@ -174,7 +174,7 @@
 
 def forward(nx, ny, scale, *refs):
     later = refs[: nx - 1]
-    q_ref, same_ref, other_ref, wk_ref, state_in, full_in, accl_in, pay_ref, acc_ref, stats_ref = refs[nx - 1 :]
+    q_ref, same_ref, other_ref, wk_ref, state_in, full_in, accl_in, acc_ref, stats_ref, own_ref, *page_refs = refs[nx - 1 :]
     x, y, core = place(ny)
     head = other_ref.shape[3]
     n = later[0].shape[0]
@@ -196,8 +196,8 @@
         return [high, column - high]
 
     high, low = halves(state[:, :head])
-    pay_ref[x, :feats_n] = low
-    pay_ref[x, n : n + feats_n] = high
+    own_ref[:feats_n] = low
+    own_ref[n : n + feats_n] = high
     zero = jnp.zeros((n, 1), F32)
     columns = [[zero, zero, zero, *two(state[:, head : head + 1])]]
     sums = []
@@ -211,50 +211,42 @@
         total = before[:, head : head + 1] * mine + accl[:, head : head + 1] * other
         columns.append([new, *two(total), *two(full[:, head : head + 1])])
     rows = to_rows(columns, head)
-    pay_ref[x, n + feats_n :] = rows[0]
+    own_ref[n + feats_n :] = rows[0]
     for s in range(1, nx):
-
-        @pl.when(x + s < nx)
-        def _(s=s):
-            pay_ref[x + s, :n] = sums[s - 1]
-            pay_ref[x + s, n : n + feats_n] = full_high
-            pay_ref[x + s, n + feats_n :] = rows[s]
-
-    for d in range(nx):
-
-        @pl.when(d < x)
-        def _(d=d):
-            pay_ref[d] = jnp.zeros(pay_ref.shape[1:], BF16)
-
-
-def merge(
-    nx, ny, scale, count,
-    acc_in, stats_in, got_ref, fq_ref, near_ref,
-    out_ref, dnum_ref, dden_ref, state_ref, back_ref, pay_ref, loss_ref,
-):
+        page_refs[s - 1][:n] = sums[s - 1]
+        page_refs[s - 1][n : n + feats_n] = full_high
+        page_refs[s - 1][n + feats_n :] = rows[s]
+
+
+def merge(nx, ny, scale, count, *refs):
+    got = refs[:nx]
+    (
+        acc_in, stats_in, fq_ref, near_ref,
+        out_ref, dnum_ref, dden_ref, state_ref, back_ref, pay_ref, loss_ref,
+    ) = refs[nx:]
     x, _, _ = place(ny)
     n, feats_n = fq_ref.shape
     head = out_ref.shape[1]
     c = scale * LOG2E
-    pages = [row_numbers(got_ref[d, n + feats_n :]) for d in range(nx)]
+    pages = [row_numbers(page[n + feats_n :]) for page in got]
     own = stats_in[0:1]
-    bests = [jnp.where(d < x, pages[d][0:1], -1e30) for d in range(nx)]
+    bests = [jnp.where(s <= x, pages[s][0:1], -1e30) for s in range(1, nx)]
     best = functools.reduce(jnp.maximum, bests, own)
     factors = [jnp.exp2((own - best) * c)]
     total = stats_in[1:2] * factors[0]
-    norm = jnp.zeros_like(total)
-    for d in range(nx):
-        factors.append(jnp.where(d < x, jnp.exp2((bests[d] - best) * c), 0.0))
-        total += (pages[d][1:2] + pages[d][2:3]) * factors[d + 1]
-        norm += pages[d][3:4] + pages[d][4:5]
+    norm = pages[0][3:4] + pages[0][4:5]
+    for s in range(1, nx):
+        factors.append(jnp.where(s <= x, jnp.exp2((bests[s - 1] - best) * c), 0.0))
+        total += (pages[s][1:2] + pages[s][2:3]) * factors[s]
+        norm += pages[s][3:4] + pages[s][4:5]
     columns = to_columns([f / total for f in factors] + [norm], head)
     targets = acc_in[...] * columns[:, 0:1]
-    state = got_ref[x, :feats_n].astype(F32)
-    for d in range(nx):
-        targets += got_ref[d, :n].astype(F32) * columns[:, d + 1 : d + 2]
-        state += got_ref[d, n : n + feats_n].astype(F32)
+    state = got[0][:feats_n].astype(F32) + got[0][n : n + feats_n].astype(F32)
+    for s in range(1, nx):
+        targets += got[s][:n].astype(F32) * columns[:, s : s + 1]
+        state += got[s][n : n + feats_n].astype(F32)
     targets = targets.astype(BF16).astype(F32)
-    norm = columns[:, nx + 1 : nx + 2]
+    norm = columns[:, nx : nx + 1]
     state = jnp.concatenate([state, jnp.broadcast_to(norm, state.shape)], 1)
     state_ref[...] = state
     fq = fq_ref[...]
@@ -391,16 +383,19 @@
         functools.partial(same_core, nx, ny, scale),
         (f32(feats, feats), f32(feats, feats), f32(nx - 1, n, feats)), (*later, same, w_key), flops=3, name="same_core",
     )
-    pay, acc, stats = call(
+    acc, stats, mine, *pages = call(
         functools.partial(forward, nx, ny, scale),
-        (bf16(nx, n + feats + 16, head), f32(n, head), f32(8, n)),
+        (f32(n, head), f32(8, n), *[bf16(n + feats + 16, head)] * nx),
         (*later, q, same, other, w_key, state, full, sums), flops=6, name="forward",
     )
-    got = lax.all_to_all(pay, "ctx", 0, 0, tiled=True, axis_index_groups=x_groups)
+    got = [mine] + [
+        lax.ppermute(a, "ctx", [(at(x, y, c), at(x + s, y, c)) for x, y, c in every if x + s < nx])
+        for s, a in enumerate(pages, 1)
+    ]
     out, dnum, dden, state, back, pay, loss = call(
         functools.partial(merge, nx, ny, scale, count),
         (bf16(n, head), f32(n, head), f32(n, head), f32(feats, feats), f32(feats, feats), bf16(nx, feats + 16, head), f32(8, head)),
-        (acc, stats, got, fq, near), flops=2, name="merge",
+        (*got, acc, stats, fq, near), flops=2, name="merge",
     )
     got = lax.all_to_all(pay, "ctx", 0, 0, tiled=True, axis_index_groups=x_groups)
     grads = call(

time: 110 us -> 110 us (level)
  blocking collectives: 46.4 us -> 33.3 us
  starting transfers between devices: 24.6 us -> 34.6 us
  waiting for transfers between devices: 23.1 us -> 25.9 us
    all_to_all x1 -> x0, blocking collectives: 13.2 us -> none  [shards(): lax.all_to_all(pay, 'ctx', 0, 0, tiled=True, axis_index_groups=x_groups)]
    ppermute x0 -> x3, starting transfers between devices: none -> 8.78 us  [shards(): lax.ppermute(a, 'ctx', [(at(x, y, c), at(x + s, y, c)) for x, y, c in eve...]
    ppermute x0 -> x3, waiting for transfers between devices: none -> 2.82 us  [shards(): lax.ppermute(a, 'ctx', [(at(x, y, c), at(x + s, y, c)) for x, y, c in eve...]
    all_to_all x1, starting transfers between devices: 3.45 us -> 4.68 us  [shards(): lax.all_to_all(pay, 'ctx', 0, 0, tiled=True, axis_index_groups=x_groups)]
  transfers between devices with their start and end apart: 7 -> 10, of which waited for: 6 -> 8; matrix products, arithmetic and copies ran while one was open for 0% -> 0% of each run, Pallas kernels for 4% -> 4%
where the time goes in v11:
time: 110 us; the launch traced here: 109 us
  starting transfers between devices  34.6 us (31%)
  blocking collectives  33.3 us (30%)
  waiting for transfers between devices  25.9 us (24%)
  Pallas kernels  12.7 us (12%)
  local copies, waits for them, and re-layouts  1.9 us (2%)
    all_to_all x1, blocking collectives, spread(): lax.all_to_all(copies, axes, 0, 0, tiled=True, axis_index_groups=groups)  21.2 us
    pallas_call x7, Pallas kernels, call(): pl.pallas_call(body, out_shape=outs, in_specs=[VMEM] * len(args), out_spe...  12.7 us
    all_to_all x1, blocking collectives, shards(): lax.all_to_all(grads.reshape(chips, 1, -1), both_axes, 0, 0, tiled=True,...  12.2 us
    ppermute x3, starting transfers between devices, shards(): lax.ppermute(a, 'ctx', [(at(x, y, c), at(x + s, y, c)) for x, y, c in eve...  8.78 us
    all_to_all x1, waiting for transfers between devices, spread(): lax.all_to_all(copies, axes, 0, 0, tiled=True, axis_index_groups=groups)  8.73 us
    all_to_all x1, starting transfers between devices, shards(): lax.all_to_all(kvs, 'ctx', 0, 0, tiled=True, axis_index_groups=y_groups)  7.79 us
    all_to_all x1, waiting for transfers between devices, shards(): lax.all_to_all(kvs, 'ctx', 0, 0, tiled=True, axis_index_groups=y_groups)  6.84 us
    ppermute x1, starting transfers between devices, shards(): other = lax.ppermute(same, 'ctx', swap)  5.59 us
  transfers between devices with their start and end apart: 10, of which 8 were waited for; matrix products, arithmetic and copies ran while one was open for 0% of the time, Pallas kernels for 4%

profile of v11, /device:TPU:1, one launch (start us, length us, event | category | flops | bytes accessed | tf_op | source)
XLA Modules:
  0.0 109.4 jit_solution(3007041780093660443)
XLA Ops:
  0.6 1.6 %copies.1 = bf16[8,2,128,128]{3,2,1,0:T(8,128)(2,1)} custom-call(bf16[128,128]{1,0:T(8,128)(2,1)} %bitcast.20, bf16[128,128]{1,0:T(8,128)(2,1)} %bitcast.23), custom_call_target="tpu_custom_call" | custom-call | flops 1000000000 | bytes 20000000 | tf_op jit(solution)/shard_map/copies/pallas_call | solution.py:355
  2.3 7.8 %all-to-all-start = ((bf16[8,2,128,128]{3,2,1,0:T(8,128)(2,1)}), bf16[8,2,128,128]{3,2,1,0:T(8,128)(2,1)S(1)}, u32[]{:S(2)}, u32[]{:S(2)}) async-start(bf16[8,2,128,128]{3,2,1,0:T(8,128)(2,1)} %copies.1), calls=%async_computation | async-start | bytes 1048576 | tf_op jit(solution)/shard_map/all_to_all | solution.py:371
  10.1 1.3 %collective-permute-start.2 = (bf16[256,128]{1,0:T(8,128)(2,1)S(1)}, bf16[256,128]{1,0:T(8,128)(2,1)S(1)}, u32[]{:S(2)}, u32[]{:S(2)}) collective-permute-start(bf16[256,128]{1,0:T(8,128)(2,1)S(1)} %bitcast.14), channel_id=1, source_target_pairs={{384,0},{392,8},{400,16},{408,24},{416,32},{424,40},{432,48},{440,... | collective-permute-start | bytes 196616 | tf_op jit(solution)/shard_map/ppermute | solution.py:373
  11.4 1.3 %collective-permute-start.1 = (bf16[256,128]{1,0:T(8,128)(2,1)S(1)}, bf16[256,128]{1,0:T(8,128)(2,1)S(1)}, u32[]{:S(2)}, u32[]{:S(2)}) collective-permute-start(bf16[256,128]{1,0:T(8,128)(2,1)S(1)} %bitcast.15), channel_id=1, source_target_pairs={{256,0},{264,8},{272,16},{280,24},{288,32},{296,40},{304,48},{312,... | collective-permute-start | bytes 196616 | tf_op jit(solution)/shard_map/ppermute | solution.py:373
  12.7 1.3 %collective-permute-start = (bf16[256,128]{1,0:T(8,128)(2,1)S(1)}, bf16[256,128]{1,0:T(8,128)(2,1)S(1)}, u32[]{:S(2)}, u32[]{:S(2)}) collective-permute-start(bf16[256,128]{1,0:T(8,128)(2,1)S(1)} %bitcast.16), channel_id=1, source_target_pairs={{128,0},{136,8},{144,16},{152,24},{160,32},{168,40},{176,48},{184,... | collective-permute-start | bytes 196616 | tf_op jit(solution)/shard_map/ppermute | solution.py:373
  14.9 1.4 %collective-permute-done.2.refs_2_ = bf16[256,128]{1,0:T(8,128)(2,1)S(1)} collective-permute-done((bf16[256,128]{1,0:T(8,128)(2,1)S(1)}, bf16[256,128]{1,0:T(8,128)(2,1)S(1)}, u32[]{:S(2)}, u32[]{:S(2)}) %collective-permute-start.2) | collective-permute-done | bytes 65568 | tf_op jit(solution)/shard_map/ppermute | solution.py:373
  16.3 1.6 %collective-permute-done.1.refs_1_ = bf16[256,128]{1,0:T(8,128)(2,1)S(1)} collective-permute-done((bf16[256,128]{1,0:T(8,128)(2,1)S(1)}, bf16[256,128]{1,0:T(8,128)(2,1)S(1)}, u32[]{:S(2)}, u32[]{:S(2)}) %collective-permute-start.1) | collective-permute-done | bytes 65568 | tf_op jit(solution)/shard_map/ppermute | solution.py:373
  18.0 6.8 %all-to-all-done.refs_3_.refs_4_.same_ref = bf16[8,2,128,128]{3,2,1,0:T(8,128)(2,1)S(1)} async-done(((bf16[8,2,128,128]{3,2,1,0:T(8,128)(2,1)}), bf16[8,2,128,128]{3,2,1,0:T(8,128)(2,1)S(1)}, u32[]{:S(2)}, u32[]{:S(2)}) %all-to-all-start) | async-done | bytes 524320 | tf_op jit(solution)/shard_map/all_to_all | solution.py:371
  24.8 5.6 %collective-permute-start.3 = (bf16[8,2,128,128]{3,2,1,0:T(8,128)(2,1)S(1)}, bf16[8,2,128,128]{3,2,1,0:T(8,128)(2,1)S(1)}, u32[]{:S(2)}, u32[]{:S(2)}) collective-permute-start(bf16[8,2,128,128]{3,2,1,0:T(8,128)(2,1)S(1)} %all-to-all-done.refs_3_.refs_4_.same_ref), channel_id=1, source_target_pairs={{0,8},{8,0},{16,24},{24,16},{32,40},{40,32},{48,56},{56,48},{64,72... | collective-permute-start | bytes 1572872 | tf_op jit(solution)/shard_map/ppermute | solution.py:381
  30.4 2.0 %same_core.1 = (f32[256,256]{1,0:T(8,128)S(1)}, f32[256,256]{1,0:T(8,128)S(1)}, f32[3,256,256]{2,1,0:T(8,128)S(1)}) custom-call(bf16[256,128]{1,0:T(8,128)(2,1)S(1)} %collective-permute-done.refs_0_, bf16[256,128]{1,0:T(8,128)(2,1)S(1)} %collective-permute-done.1.refs_1_, bf16[256,128]{1,0:T(8,128)(2,1)S(1)} %collective-permute-done.2.refs_2_, ...), custom_call_target="tpu_custom_call" | custom-call | flops 3000000000 | bytes 20000000 | tf_op jit(solution)/shard_map/same_core/pallas_call | solution.py:355
  32.5 3.2 %forward.1 = (f32[256,128]{1,0:T(8,128)S(1)}, f32[8,256]{1,0:T(8,128)S(1)}, bf16[528,128]{1,0:T(8,128)(2,1)S(1)}, bf16[528,128]{1,0:T(8,128)(2,1)S(1)}, bf16[528...) custom-call(bf16[256,128]{1,0:T(8,128)(2,1)S(1)} %collective-permute-done.refs_0_, ...), custom_call_target="tpu_custom_call" | custom-call | flops 6000000000 | bytes 20000000 | tf_op jit(solution)/shard_map/forward/pallas_call | solution.py:355
  35.7 3.1 %collective-permute-start.4 = (bf16[528,128]{1,0:T(8,128)(2,1)S(1)}, bf16[528,128]{1,0:T(8,128)(2,1)S(1)}, u32[]{:S(2)}, u32[]{:S(2)}) collective-permute-start(bf16[528,128]{1,0:T(8,128)(2,1)S(1)} %get-tuple-element.38), channel_id=1, source_target_pairs={{0,128},{8,136},{16,144},{24,152},{32,160},{40,168},{48,176},{56,1... | collective-permute-start | bytes 405512 | tf_op jit(solution)/shard_map/ppermute | solution.py:392
  38.8 4.4 %collective-permute-start.5 = (bf16[528,128]{1,0:T(8,128)(2,1)S(1)}, bf16[528,128]{1,0:T(8,128)(2,1)S(1)}, u32[]{:S(2)}, u32[]{:S(2)}) collective-permute-start(bf16[528,128]{1,0:T(8,128)(2,1)S(1)} %get-tuple-element.39), channel_id=1, source_target_pairs={{0,256},{8,264},{16,272},{24,280},{32,288},{40,296},{48,304},{56,3... | collective-permute-start | bytes 405512 | tf_op jit(solution)/shard_map/ppermute | solution.py:392
  43.2 1.3 %collective-permute-start.6 = (bf16[528,128]{1,0:T(8,128)(2,1)S(1)}, bf16[528,128]{1,0:T(8,128)(2,1)S(1)}, u32[]{:S(2)}, u32[]{:S(2)}) collective-permute-start(bf16[528,128]{1,0:T(8,128)(2,1)S(1)} %get-tuple-element.40), channel_id=1, source_target_pairs={{0,384},{8,392},{16,400},{24,408},{32,416},{40,424},{48,432},{56,4... | collective-permute-start | bytes 405512 | tf_op jit(solution)/shard_map/ppermute | solution.py:392
  44.5 1.3 %collective-permute-done.5.refs_2_ = bf16[528,128]{1,0:T(8,128)(2,1)S(1)} collective-permute-done((bf16[528,128]{1,0:T(8,128)(2,1)S(1)}, bf16[528,128]{1,0:T(8,128)(2,1)S(1)}, u32[]{:S(2)}, u32[]{:S(2)}) %collective-permute-start.5) | collective-permute-done | bytes 135200 | tf_op jit(solution)/shard_map/ppermute | solution.py:392
  45.9 1.5 %collective-permute-done.6.refs_3_ = bf16[528,128]{1,0:T(8,128)(2,1)S(1)} collective-permute-done((bf16[528,128]{1,0:T(8,128)(2,1)S(1)}, bf16[528,128]{1,0:T(8,128)(2,1)S(1)}, u32[]{:S(2)}, u32[]{:S(2)}) %collective-permute-start.6) | collective-permute-done | bytes 135200 | tf_op jit(solution)/shard_map/ppermute | solution.py:392
  47.3 1.9 %merge.1 = (bf16[256,128]{1,0:T(8,128)(2,1)}, f32[256,128]{1,0:T(8,128)S(1)}, f32[256,128]{1,0:T(8,128)S(1)}, f32[256,256]{1,0:T(8,128)S(1)}, f32[256,256]{1,0:T...) custom-call(bf16[528,128]{1,0:T(8,128)(2,1)S(1)} %get-tuple-element.37.refs_0_, ...), custom_call_target="tpu_custom_call" | custom-call | flops 2000000000 | bytes 20000000 | tf_op jit(solution)/shard_map/merge/pallas_call | solution.py:355
  49.2 4.7 %all-to-all-start.1 = ((bf16[4,272,128]{2,1,0:T(8,128)(2,1)}), bf16[4,272,128]{2,1,0:T(8,128)(2,1)S(1)}, u32[]{:S(2)}, u32[]{:S(2)}) async-start(bf16[4,272,128]{2,1,0:T(8,128)(2,1)} %get-tuple-element.47), calls=%async_computation.1 | async-start | bytes 557056 | tf_op jit(solution)/shard_map/all_to_all | solution.py:400
  55.1 4.4 %all-to-all-done.1.got_ref = bf16[4,272,128]{2,1,0:T(8,128)(2,1)S(1)} async-done(((bf16[4,272,128]{2,1,0:T(8,128)(2,1)}), bf16[4,272,128]{2,1,0:T(8,128)(2,1)S(1)}, u32[]{:S(2)}, u32[]{:S(2)}) %all-to-all-start.1) | async-done | bytes 278560 | tf_op jit(solution)/shard_map/all_to_all | solution.py:400
  59.5 1.9 %backward.1 = f32[288,128]{1,0:T(8,128)S(1)} custom-call(bf16[8,2,128,128]{3,2,1,0:T(8,128)(2,1)S(1)} %all-to-all-done.refs_3_.refs_4_.same_ref, bf16[8,2,128,128]{3,2,1,0:T(8,128)(2,1)S(1)} %collective-permute-done.3.refs_5_.other_ref, f32[128,128]{1,0:T(8,128)S(1)} %copy-done.2, f32[256,256]{1,0:T(8,128)S(1)} %get-tuple-element.46.back_in, ...), custom_call_target="tpu_custom_call" | custom-call | flops 4000000000 | bytes 20000000 | tf_op jit(solution)/shard_map/backward/pallas_call | solution.py:355
  61.4 12.2 %all_to_all.25 = f32[32,1,1152]{2,1,0:T(1,128)S(1)} all-to-all(f32[32,1,1152]{2,1,0:T(1,128)S(1)} %bitcast.13), channel_id=1, replica_groups={{0,16,32,48,64,80,96,112,128,144,160,176,192,208,224,240,256,272,288,30..., dimensions={0} | all-to-all | bytes 294912 | tf_op jit(solution)/shard_map/all_to_all | solution.py:419
  73.7 21.2 %all_to_all.26 = f32[16,1,1152]{2,1,0:T(1,128)S(1)} all-to-all(f32[16,1,1152]{2,1,0:T(1,128)S(1)} %broadcast_in_dim.6), channel_id=1, replica_groups={{0,1,2,3,4,5,6,7,8,9,10,11,12,13,14,15},{16,17,18,19,20,21,22,23,24,25,..., dimensions={0} | all-to-all | bytes 147456 | tf_op jit(solution)/shard_map/all_to_all | solution.py:337
  95.6 3.9 %all-to-all-start.4 = ((f32[32,8,128]{2,1,0:T(8,128)}), f32[32,8,128]{2,1,0:T(8,128)S(1)}, u32[]{:S(2)}, u32[]{:S(2)}) async-start(f32[32,8,128]{2,1,0:T(8,128)} %broadcast_in_dim.15), calls=%async_computation.4 | async-start | bytes 262144 | tf_op jit(solution)/shard_map/all_to_all | solution.py:337
  100.0 8.7 %all-to-all-done.4 = f32[32,8,128]{2,1,0:T(8,128)S(1)} async-done(((f32[32,8,128]{2,1,0:T(8,128)}), f32[32,8,128]{2,1,0:T(8,128)S(1)}, u32[]{:S(2)}, u32[]{:S(2)}) %all-to-all-start.4) | async-done | bytes 131104 | tf_op jit(solution)/shard_map/all_to_all | solution.py:337
  (23 shorter events, 4.2 us)
Async XLA Ops:
  2.3 7.8 %copy-start = (bf16[128,1,2,128]{3,2,1,0:T(2,128)(2,1)S(1)}, bf16[128,1,2,128]{3,2,1,0:T(2,128)(2,1)}, u32[]{:S(2)}) copy-start(bf16[128,1,2,128]{3,2,1,0:T(2,128)(2,1)} %param.5) | copy-start | bytes 196612
  2.3 11.7 %copy-start.1 = (f32[128,128]{1,0:T(8,128)S(1)}, f32[128,128]{1,0:T(8,128)}, u32[]{:S(2)}) copy-start(f32[128,128]{1,0:T(8,128)} %wq_ref.3) | copy-start | bytes 196612
  2.3 11.7 %copy-start.2 = (f32[128,128]{1,0:T(8,128)S(1)}, f32[128,128]{1,0:T(8,128)}, u32[]{:S(2)}) copy-start(f32[128,128]{1,0:T(8,128)} %wk_ref.5) | copy-start | bytes 196612
  2.3 11.7 %copy-start.3 = (bf16[128,1,128]{2,0,1:T(8,128)(2,1)S(1)}, bf16[128,1,128]{2,0,1:T(8,128)(2,1)}, u32[]{:S(2)}) copy-start(bf16[128,1,128]{2,0,1:T(8,128)(2,1)} %param.6) | copy-start | bytes 98308
  2.3 11.7 %copy-start.4 = (bf16[128,1,128]{2,0,1:T(8,128)(2,1)S(1)}, bf16[128,1,128]{2,0,1:T(8,128)(2,1)}, u32[]{:S(2)}) copy-start(bf16[128,1,128]{2,0,1:T(8,128)(2,1)} %param.7) | copy-start | bytes 98308
  2.3 22.5 %all-to-all-start = ((bf16[8,2,128,128]{3,2,1,0:T(8,128)(2,1)}), bf16[8,2,128,128]{3,2,1,0:T(8,128)(2,1)S(1)}, u32[]{:S(2)}, u32[]{:S(2)}) async-start(bf16[8,2,128,128]{3,2,1,0:T(8,128)(2,1)} %copies.1), calls=%async_computation | async-start | bytes 1048576 | tf_op jit(solution)/shard_map/all_to_all | solution.py:371
  10.1 6.2 %collective-permute-start.2 = (bf16[256,128]{1,0:T(8,128)(2,1)S(1)}, bf16[256,128]{1,0:T(8,128)(2,1)S(1)}, u32[]{:S(2)}, u32[]{:S(2)}) collective-permute-start(bf16[256,128]{1,0:T(8,128)(2,1)S(1)} %bitcast.14), channel_id=1, source_target_pairs={{384,0},{392,8},{400,16},{408,24},{416,32},{424,40},{432,48},{440,... | collective-permute-start | bytes 196616 | tf_op jit(solution)/shard_map/ppermute | solution.py:373
  11.4 6.5 %collective-permute-start.1 = (bf16[256,128]{1,0:T(8,128)(2,1)S(1)}, bf16[256,128]{1,0:T(8,128)(2,1)S(1)}, u32[]{:S(2)}, u32[]{:S(2)}) collective-permute-start(bf16[256,128]{1,0:T(8,128)(2,1)S(1)} %bitcast.15), channel_id=1, source_target_pairs={{256,0},{264,8},{272,16},{280,24},{288,32},{296,40},{304,48},{312,... | collective-permute-start | bytes 196616 | tf_op jit(solution)/shard_map/ppermute | solution.py:373
  12.7 5.3 %collective-permute-start = (bf16[256,128]{1,0:T(8,128)(2,1)S(1)}, bf16[256,128]{1,0:T(8,128)(2,1)S(1)}, u32[]{:S(2)}, u32[]{:S(2)}) collective-permute-start(bf16[256,128]{1,0:T(8,128)(2,1)S(1)} %bitcast.16), channel_id=1, source_target_pairs={{128,0},{136,8},{144,16},{152,24},{160,32},{168,40},{176,48},{184,... | collective-permute-start | bytes 196616 | tf_op jit(solution)/shard_map/ppermute | solution.py:373
  24.8 7.6 %collective-permute-start.3 = (bf16[8,2,128,128]{3,2,1,0:T(8,128)(2,1)S(1)}, bf16[8,2,128,128]{3,2,1,0:T(8,128)(2,1)S(1)}, u32[]{:S(2)}, u32[]{:S(2)}) collective-permute-start(bf16[8,2,128,128]{3,2,1,0:T(8,128)(2,1)S(1)} %all-to-all-done.refs_3_.refs_4_.same_ref), channel_id=1, source_target_pairs={{0,8},{8,0},{16,24},{24,16},{32,40},{40,32},{48,56},{56,48},{64,72... | collective-permute-start | bytes 1572872 | tf_op jit(solution)/shard_map/ppermute | solution.py:381
  35.7 8.8 %collective-permute-start.4 = (bf16[528,128]{1,0:T(8,128)(2,1)S(1)}, bf16[528,128]{1,0:T(8,128)(2,1)S(1)}, u32[]{:S(2)}, u32[]{:S(2)}) collective-permute-start(bf16[528,128]{1,0:T(8,128)(2,1)S(1)} %get-tuple-element.38), channel_id=1, source_target_pairs={{0,128},{8,136},{16,144},{24,152},{32,160},{40,168},{48,176},{56,1... | collective-permute-start | bytes 405512 | tf_op jit(solution)/shard_map/ppermute | solution.py:392
  38.8 7.0 %collective-permute-start.5 = (bf16[528,128]{1,0:T(8,128)(2,1)S(1)}, bf16[528,128]{1,0:T(8,128)(2,1)S(1)}, u32[]{:S(2)}, u32[]{:S(2)}) collective-permute-start(bf16[528,128]{1,0:T(8,128)(2,1)S(1)} %get-tuple-element.39), channel_id=1, source_target_pairs={{0,256},{8,264},{16,272},{24,280},{32,288},{40,296},{48,304},{56,3... | collective-permute-start | bytes 405512 | tf_op jit(solution)/shard_map/ppermute | solution.py:392
  43.2 4.1 %collective-permute-start.6 = (bf16[528,128]{1,0:T(8,128)(2,1)S(1)}, bf16[528,128]{1,0:T(8,128)(2,1)S(1)}, u32[]{:S(2)}, u32[]{:S(2)}) collective-permute-start(bf16[528,128]{1,0:T(8,128)(2,1)S(1)} %get-tuple-element.40), channel_id=1, source_target_pairs={{0,384},{8,392},{16,400},{24,408},{32,416},{40,424},{48,432},{56,4... | collective-permute-start | bytes 405512 | tf_op jit(solution)/shard_map/ppermute | solution.py:392
  49.2 10.3 %all-to-all-start.1 = ((bf16[4,272,128]{2,1,0:T(8,128)(2,1)}), bf16[4,272,128]{2,1,0:T(8,128)(2,1)S(1)}, u32[]{:S(2)}, u32[]{:S(2)}) async-start(bf16[4,272,128]{2,1,0:T(8,128)(2,1)} %get-tuple-element.47), calls=%async_computation.1 | async-start | bytes 557056 | tf_op jit(solution)/shard_map/all_to_all | solution.py:400
  95.6 13.1 %all-to-all-start.4 = ((f32[32,8,128]{2,1,0:T(8,128)}), f32[32,8,128]{2,1,0:T(8,128)S(1)}, u32[]{:S(2)}, u32[]{:S(2)}) async-start(f32[32,8,128]{2,1,0:T(8,128)} %broadcast_in_dim.15), calls=%async_computation.4 | async-start | bytes 262144 | tf_op jit(solution)/shard_map/all_to_all | solution.py:337

commit v12 on v9

--- a/solution.py
+++ b/solution.py
@@ -91,10 +91,16 @@
     return jnp.concatenate(rows + [jnp.zeros((head - len(rows), rows[0].shape[1]), F32)], 0).T
 
 
-def copies(k_ref, v_ref, out_ref):
-    for d in range(out_ref.shape[0]):
-        out_ref[d, 0] = k_ref[...]
-        out_ref[d, 1] = v_ref[...]
+def copies(k_ref, v_ref, out_ref, sems):
+    moves = [
+        pltpu.make_async_copy(ref, out_ref.at[d, i], sems.at[d, i])
+        for d in range(out_ref.shape[0])
+        for i, ref in enumerate((k_ref, v_ref))
+    ]
+    for move in moves:
+        move.start()
+    for move in moves:
+        move.wait()
 
 
 def own_features(q, k, wq, wk):
@@ -375,7 +381,15 @@
 
     q = queries.reshape(n, head)
     k, v = keys.reshape(rows, head), values.reshape(rows, head)
-    kvs = call(copies, bf16(ny, 2, rows, head), (k, v), name="copies", vmem=60)
+    kvs = pl.pallas_call(
+        copies,
+        out_shape=bf16(ny, 2, rows, head),
+        in_specs=[VMEM] * 2,
+        out_specs=pl.BlockSpec(memory_space=pl.ANY),
+        scratch_shapes=[pltpu.SemaphoreType.DMA((ny, 2))],
+        compiler_params=pltpu.CompilerParams(vmem_limit_bytes=60 * 1024 * 1024),
+        name="copies",
+    )(k, v)
     same = lax.all_to_all(kvs, "ctx", 0, 0, tiled=True, axis_index_groups=y_groups)
     later = [
         lax.ppermute(q, "ctx", [(at(x, y, c), at(x - s, y, c)) for x, y, c in every if x >= s])
@@ -425,8 +439,9 @@
         grads.reshape(chips, 1, -1), both_axes, 0, 0, tiled=True, axis_index_groups=chip_groups
     ).sum(0)
     mine = spread(mine, both_axes, rest_groups).sum(0)
+    mine, loss = lax.optimization_barrier((mine, mine[0, parts * head]))
     g = spread(mine[0, : parts * head].reshape(parts, head), both_axes, chip_groups).reshape(2, head, head)
-    return out.reshape(queries.shape), g[0], g[1], mine[0, parts * head]
+    return out.reshape(queries.shape), g[0], g[1], loss
 
 
 def solution(mesh):

time: 110 us -> 110 us (level)
  blocking collectives: 46.4 us -> 58.8 us
  waiting for transfers between devices: 23.1 us -> 14.3 us
  starting transfers between devices: 24.6 us -> 20.7 us
    all_to_all x1 -> x2, blocking collectives: 21.1 us -> 33.5 us  [spread(): lax.all_to_all(copies, axes, 0, 0, tiled=True, axis_index_groups=groups)]
    all_to_all x1 -> x0, waiting for transfers between devices: 8.73 us -> none  [spread(): lax.all_to_all(copies, axes, 0, 0, tiled=True, axis_index_groups=groups)]
    all_to_all x1 -> x0, starting transfers between devices: 3.85 us -> none  [spread(): lax.all_to_all(copies, axes, 0, 0, tiled=True, axis_index_groups=groups)]
    pallas_call x0 -> x1, Pallas kernels: none -> 1.72 us  [shards(): pl.pallas_call(copies, out_shape=bf16(ny, 2, rows, head), in_specs=[VMEM]...]
    pallas_call x7 -> x6, Pallas kernels: 12.7 us -> 11 us  [call(): pl.pallas_call(body, out_shape=outs, in_specs=[VMEM] * len(args), out_spe...]
  transfers between devices with their start and end apart: 7 -> 6, of which waited for: 6 -> 5; matrix products, arithmetic and copies ran while one was open for 0% -> 0% of each run, Pallas kernels for 4% -> 4%
where the time goes in v12:
time: 110 us; the launch traced here: 109 us
  blocking collectives  58.8 us (53%)
  starting transfers between devices  20.7 us (19%)
  waiting for transfers between devices  14.3 us (13%)
  Pallas kernels  12.7 us (12%)
  local copies, waits for them, and re-layouts  1.26 us (1%)
    all_to_all x2, blocking collectives, spread(): lax.all_to_all(copies, axes, 0, 0, tiled=True, axis_index_groups=groups)  33.5 us
    all_to_all x1, blocking collectives, shards(): lax.all_to_all(pay, 'ctx', 0, 0, tiled=True, axis_index_groups=x_groups)  13.2 us
    all_to_all x1, blocking collectives, shards(): lax.all_to_all(grads.reshape(chips, 1, -1), both_axes, 0, 0, tiled=True,...  12.2 us
    pallas_call x6, Pallas kernels, call(): pl.pallas_call(body, out_shape=outs, in_specs=[VMEM] * len(args), out_spe...  11 us
    all_to_all x1, starting transfers between devices, shards(): lax.all_to_all(kvs, 'ctx', 0, 0, tiled=True, axis_index_groups=y_groups)  7.79 us
    all_to_all x1, waiting for transfers between devices, shards(): lax.all_to_all(kvs, 'ctx', 0, 0, tiled=True, axis_index_groups=y_groups)  6.84 us
    ppermute x1, starting transfers between devices, shards(): other = lax.ppermute(same, 'ctx', swap)  5.59 us
    all_to_all x1, waiting for transfers between devices, shards(): lax.all_to_all(pay, 'ctx', 0, 0, tiled=True, axis_index_groups=x_groups)  4.39 us
  transfers between devices with their start and end apart: 6, of which 5 were waited for; matrix products, arithmetic and copies ran while one was open for 0% of the time, Pallas kernels for 4%

profile of v12, /device:TPU:1, one launch (start us, length us, event | category | flops | bytes accessed | tf_op | source)
XLA Modules:
  0.0 108.8 jit_solution(9333017887178748065)
XLA Ops:
  0.6 1.7 %copies.1 = bf16[8,2,128,128]{3,2,1,0:T(8,128)(2,1)} custom-call(bf16[128,128]{1,0:T(8,128)(2,1)} %bitcast.14, bf16[128,128]{1,0:T(8,128)(2,1)} %bitcast.17), custom_call_target="tpu_custom_call" | custom-call | tf_op jit(solution)/shard_map/copies/pallas_call | solution.py:384
  2.4 7.8 %all-to-all-start = ((bf16[8,2,128,128]{3,2,1,0:T(8,128)(2,1)}), bf16[8,2,128,128]{3,2,1,0:T(8,128)(2,1)S(1)}, u32[]{:S(2)}, u32[]{:S(2)}) async-start(bf16[8,2,128,128]{3,2,1,0:T(8,128)(2,1)} %copies.1), calls=%async_computation | async-start | bytes 1048576 | tf_op jit(solution)/shard_map/all_to_all | solution.py:393
  10.2 1.3 %collective-permute-start.2 = (bf16[256,128]{1,0:T(8,128)(2,1)S(1)}, bf16[256,128]{1,0:T(8,128)(2,1)S(1)}, u32[]{:S(2)}, u32[]{:S(2)}) collective-permute-start(bf16[256,128]{1,0:T(8,128)(2,1)S(1)} %bitcast.20), channel_id=1, source_target_pairs={{384,0},{392,8},{400,16},{408,24},{416,32},{424,40},{432,48},{440,... | collective-permute-start | bytes 196616 | tf_op jit(solution)/shard_map/ppermute | solution.py:395
  11.5 1.3 %collective-permute-start.1 = (bf16[256,128]{1,0:T(8,128)(2,1)S(1)}, bf16[256,128]{1,0:T(8,128)(2,1)S(1)}, u32[]{:S(2)}, u32[]{:S(2)}) collective-permute-start(bf16[256,128]{1,0:T(8,128)(2,1)S(1)} %bitcast.21), channel_id=1, source_target_pairs={{256,0},{264,8},{272,16},{280,24},{288,32},{296,40},{304,48},{312,... | collective-permute-start | bytes 196616 | tf_op jit(solution)/shard_map/ppermute | solution.py:395
  12.8 1.3 %collective-permute-start = (bf16[256,128]{1,0:T(8,128)(2,1)S(1)}, bf16[256,128]{1,0:T(8,128)(2,1)S(1)}, u32[]{:S(2)}, u32[]{:S(2)}) collective-permute-start(bf16[256,128]{1,0:T(8,128)(2,1)S(1)} %bitcast.22), channel_id=1, source_target_pairs={{128,0},{136,8},{144,16},{152,24},{160,32},{168,40},{176,48},{184,... | collective-permute-start | bytes 196616 | tf_op jit(solution)/shard_map/ppermute | solution.py:395
  14.2 0.9 prepare.1
  15.0 1.4 %collective-permute-done.2.refs_2_ = bf16[256,128]{1,0:T(8,128)(2,1)S(1)} collective-permute-done((bf16[256,128]{1,0:T(8,128)(2,1)S(1)}, bf16[256,128]{1,0:T(8,128)(2,1)S(1)}, u32[]{:S(2)}, u32[]{:S(2)}) %collective-permute-start.2) | collective-permute-done | bytes 65568 | tf_op jit(solution)/shard_map/ppermute | solution.py:395
  16.4 1.6 %collective-permute-done.1.refs_1_ = bf16[256,128]{1,0:T(8,128)(2,1)S(1)} collective-permute-done((bf16[256,128]{1,0:T(8,128)(2,1)S(1)}, bf16[256,128]{1,0:T(8,128)(2,1)S(1)}, u32[]{:S(2)}, u32[]{:S(2)}) %collective-permute-start.1) | collective-permute-done | bytes 65568 | tf_op jit(solution)/shard_map/ppermute | solution.py:395
  18.1 6.8 %all-to-all-done.refs_3_.refs_4_.same_ref = bf16[8,2,128,128]{3,2,1,0:T(8,128)(2,1)S(1)} async-done(((bf16[8,2,128,128]{3,2,1,0:T(8,128)(2,1)}), bf16[8,2,128,128]{3,2,1,0:T(8,128)(2,1)S(1)}, u32[]{:S(2)}, u32[]{:S(2)}) %all-to-all-start) | async-done | bytes 524320 | tf_op jit(solution)/shard_map/all_to_all | solution.py:393
  25.0 5.6 %collective-permute-start.3 = (bf16[8,2,128,128]{3,2,1,0:T(8,128)(2,1)S(1)}, bf16[8,2,128,128]{3,2,1,0:T(8,128)(2,1)S(1)}, u32[]{:S(2)}, u32[]{:S(2)}) collective-permute-start(bf16[8,2,128,128]{3,2,1,0:T(8,128)(2,1)S(1)} %all-to-all-done.refs_3_.refs_4_.same_ref), channel_id=1, source_target_pairs={{0,8},{8,0},{16,24},{24,16},{32,40},{40,32},{48,56},{56,48},{64,72... | collective-permute-start | bytes 1572872 | tf_op jit(solution)/shard_map/ppermute | solution.py:403
  30.6 2.0 %same_core.1 = (f32[256,256]{1,0:T(8,128)S(1)}, f32[256,256]{1,0:T(8,128)S(1)}, f32[3,256,256]{2,1,0:T(8,128)S(1)}) custom-call(bf16[256,128]{1,0:T(8,128)(2,1)S(1)} %collective-permute-done.refs_0_, bf16[256,128]{1,0:T(8,128)(2,1)S(1)} %collective-permute-done.1.refs_1_, bf16[256,128]{1,0:T(8,128)(2,1)S(1)} %collective-permute-done.2.refs_2_, ...), custom_call_target="tpu_custom_call" | custom-call | flops 3000000000 | bytes 20000000 | tf_op jit(solution)/shard_map/same_core/pallas_call | solution.py:369
  32.6 3.2 %forward.1 = (bf16[4,528,128]{2,1,0:T(8,128)(2,1)S(1)}, f32[256,128]{1,0:T(8,128)S(1)}, f32[8,256]{1,0:T(8,128)S(1)}) custom-call(bf16[256,128]{1,0:T(8,128)(2,1)S(1)} %collective-permute-done.refs_0_, bf16[256,128]{1,0:T(8,128)(2,1)S(1)} %collective-permute-done.1.refs_1_, bf16[256,128]{1,0:T(8,128)(2,1)S(1)} %collective-permute-done.2.refs_2_, ...), custom_call_target="tpu_custom_call" | custom-call | flops 6000000000 | bytes 20000000 | tf_op jit(solution)/shard_map/forward/pallas_call | solution.py:369
  35.8 13.2 %all_to_all.30.got_ref = bf16[4,528,128]{2,1,0:T(8,128)(2,1)S(1)} all-to-all(bf16[4,528,128]{2,1,0:T(8,128)(2,1)S(1)} %get-tuple-element.38), channel_id=1, replica_groups={{0,128,256,384},{8,136,264,392},{16,144,272,400},{24,152,280,408},{32,1..., dimensions={0} | all-to-all | bytes 1081344 | tf_op jit(solution)/shard_map/all_to_all | solution.py:413
  49.0 1.9 %merge.1 = (bf16[256,128]{1,0:T(8,128)(2,1)}, f32[256,128]{1,0:T(8,128)S(1)}, f32[256,128]{1,0:T(8,128)S(1)}, f32[256,256]{1,0:T(8,128)S(1)}, f32[256,256]{1,0:T...) custom-call(f32[256,128]{1,0:T(8,128)S(1)} %get-tuple-element.36.acc_in, ...), custom_call_target="tpu_custom_call" | custom-call | flops 2000000000 | bytes 20000000 | tf_op jit(solution)/shard_map/merge/pallas_call | solution.py:369
  50.8 3.4 %all-to-all-start.2 = ((bf16[4,272,128]{2,1,0:T(8,128)(2,1)}), bf16[4,272,128]{2,1,0:T(8,128)(2,1)S(1)}, u32[]{:S(2)}, u32[]{:S(2)}) async-start(bf16[4,272,128]{2,1,0:T(8,128)(2,1)} %get-tuple-element.43), calls=%async_computation.2 | async-start | bytes 557056 | tf_op jit(solution)/shard_map/all_to_all | solution.py:419
  54.3 1.2 %near_grads.1.near_ref = f32[256,128]{1,0:T(8,128)S(1)} custom-call(bf16[256,128]{1,0:T(8,128)(2,1)S(1)} %bitcast.25, bf16[128,128]{1,0:T(8,128)(2,1)S(1)} %bitcast.16, bf16[128,128]{1,0:T(8,128)(2,1)S(1)} %bitcast.19, f32[128,128]{1,0:T(8,128)S(1)} %copy-done.3, f32[128,128]{1,0:T(8,128)S(1)} %copy-done.4, f32[256,128]{1,0:T(8,128)S(1)} %get-tuple-element.44.dnum_ref, ...), custom_call_target="tpu_custom_call" | custom-call | flops 2000000000 | bytes 20000000 | tf_op jit(solution)/shard_map/near_grads/pallas_call | solution.py:369
  55.5 4.4 %all-to-all-done.2.got_ref = bf16[4,272,128]{2,1,0:T(8,128)(2,1)S(1)} async-done(((bf16[4,272,128]{2,1,0:T(8,128)(2,1)}), bf16[4,272,128]{2,1,0:T(8,128)(2,1)S(1)}, u32[]{:S(2)}, u32[]{:S(2)}) %all-to-all-start.2) | async-done | bytes 278560 | tf_op jit(solution)/shard_map/all_to_all | solution.py:419
  59.9 1.9 %backward.1 = f32[288,128]{1,0:T(8,128)S(1)} custom-call(bf16[8,2,128,128]{3,2,1,0:T(8,128)(2,1)S(1)} %all-to-all-done.refs_3_.refs_4_.same_ref, bf16[8,2,128,128]{3,2,1,0:T(8,128)(2,1)S(1)} %collective-permute-done.3.refs_5_.other_ref, f32[128,128]{1,0:T(8,128)S(1)} %copy-done.4, f32[256,256]{1,0:T(8,128)S(1)} %get-tuple-element.42.back_in, ...), custom_call_target="tpu_custom_call" | custom-call | flops 4000000000 | bytes 20000000 | tf_op jit(solution)/shard_map/backward/pallas_call | solution.py:369
  61.8 12.2 %all_to_all.31 = f32[32,1,1152]{2,1,0:T(1,128)S(1)} all-to-all(f32[32,1,1152]{2,1,0:T(1,128)S(1)} %bitcast.13), channel_id=1, replica_groups={{0,16,32,48,64,80,96,112,128,144,160,176,192,208,224,240,256,272,288,30..., dimensions={0} | all-to-all | bytes 294912 | tf_op jit(solution)/shard_map/all_to_all | solution.py:438
  74.0 0.1 reduce_sum.20
  74.1 21.1 %all_to_all.32 = f32[16,1,1152]{2,1,0:T(1,128)S(1)} all-to-all(f32[16,1,1152]{2,1,0:T(1,128)S(1)} %broadcast_in_dim.6), channel_id=1, replica_groups={{0,1,2,3,4,5,6,7,8,9,10,11,12,13,14,15},{16,17,18,19,20,21,22,23,24,25,..., dimensions={0} | all-to-all | bytes 147456 | tf_op jit(solution)/shard_map/all_to_all | solution.py:351
  95.3 0.5 slice.18
  95.8 12.4 %all_to_all.33 = f32[32,8,128]{2,1,0:T(8,128)S(1)} all-to-all(f32[32,8,128]{2,1,0:T(8,128)S(1)} %broadcast_in_dim.15), channel_id=1, replica_groups={{0,16,32,48,64,80,96,112,128,144,160,176,192,208,224,240,256,272,288,30..., dimensions={0} | all-to-all | bytes 262144 | tf_op jit(solution)/shard_map/all_to_all | solution.py:351
  108.2 0.7 slice_bitcast_fusion
  (17 shorter events, 0.2 us)
Async XLA Ops:
  2.4 7.9 %copy-start.2 = (bf16[128,1,2,128]{3,2,1,0:T(2,128)(2,1)S(1)}, bf16[128,1,2,128]{3,2,1,0:T(2,128)(2,1)}, u32[]{:S(2)}) copy-start(bf16[128,1,2,128]{3,2,1,0:T(2,128)(2,1)} %param.5) | copy-start | bytes 196612
  2.4 11.8 %copy-start = (bf16[128,1,128]{2,0,1:T(8,128)(2,1)S(1)}, bf16[128,1,128]{2,0,1:T(8,128)(2,1)}, u32[]{:S(2)}) copy-start(bf16[128,1,128]{2,0,1:T(8,128)(2,1)} %param.6) | copy-start | bytes 98308
  2.4 11.7 %copy-start.1 = (bf16[128,1,128]{2,0,1:T(8,128)(2,1)S(1)}, bf16[128,1,128]{2,0,1:T(8,128)(2,1)}, u32[]{:S(2)}) copy-start(bf16[128,1,128]{2,0,1:T(8,128)(2,1)} %param.7) | copy-start | bytes 98308
  2.4 11.7 %copy-start.3 = (f32[128,128]{1,0:T(8,128)S(1)}, f32[128,128]{1,0:T(8,128)}, u32[]{:S(2)}) copy-start(f32[128,128]{1,0:T(8,128)} %wq_ref.3) | copy-start | bytes 196612
  2.4 11.7 %copy-start.4 = (f32[128,128]{1,0:T(8,128)S(1)}, f32[128,128]{1,0:T(8,128)}, u32[]{:S(2)}) copy-start(f32[128,128]{1,0:T(8,128)} %wk_ref.5) | copy-start | bytes 196612
  2.4 22.5 %all-to-all-start = ((bf16[8,2,128,128]{3,2,1,0:T(8,128)(2,1)}), bf16[8,2,128,128]{3,2,1,0:T(8,128)(2,1)S(1)}, u32[]{:S(2)}, u32[]{:S(2)}) async-start(bf16[8,2,128,128]{3,2,1,0:T(8,128)(2,1)} %copies.1), calls=%async_computation | async-start | bytes 1048576 | tf_op jit(solution)/shard_map/all_to_all | solution.py:393
  10.2 6.2 %collective-permute-start.2 = (bf16[256,128]{1,0:T(8,128)(2,1)S(1)}, bf16[256,128]{1,0:T(8,128)(2,1)S(1)}, u32[]{:S(2)}, u32[]{:S(2)}) collective-permute-start(bf16[256,128]{1,0:T(8,128)(2,1)S(1)} %bitcast.20), channel_id=1, source_target_pairs={{384,0},{392,8},{400,16},{408,24},{416,32},{424,40},{432,48},{440,... | collective-permute-start | bytes 196616 | tf_op jit(solution)/shard_map/ppermute | solution.py:395
  11.5 6.5 %collective-permute-start.1 = (bf16[256,128]{1,0:T(8,128)(2,1)S(1)}, bf16[256,128]{1,0:T(8,128)(2,1)S(1)}, u32[]{:S(2)}, u32[]{:S(2)}) collective-permute-start(bf16[256,128]{1,0:T(8,128)(2,1)S(1)} %bitcast.21), channel_id=1, source_target_pairs={{256,0},{264,8},{272,16},{280,24},{288,32},{296,40},{304,48},{312,... | collective-permute-start | bytes 196616 | tf_op jit(solution)/shard_map/ppermute | solution.py:395
  12.8 5.3 %collective-permute-start = (bf16[256,128]{1,0:T(8,128)(2,1)S(1)}, bf16[256,128]{1,0:T(8,128)(2,1)S(1)}, u32[]{:S(2)}, u32[]{:S(2)}) collective-permute-start(bf16[256,128]{1,0:T(8,128)(2,1)S(1)} %bitcast.22), channel_id=1, source_target_pairs={{128,0},{136,8},{144,16},{152,24},{160,32},{168,40},{176,48},{184,... | collective-permute-start | bytes 196616 | tf_op jit(solution)/shard_map/ppermute | solution.py:395
  25.0 7.6 %collective-permute-start.3 = (bf16[8,2,128,128]{3,2,1,0:T(8,128)(2,1)S(1)}, bf16[8,2,128,128]{3,2,1,0:T(8,128)(2,1)S(1)}, u32[]{:S(2)}, u32[]{:S(2)}) collective-permute-start(bf16[8,2,128,128]{3,2,1,0:T(8,128)(2,1)S(1)} %all-to-all-done.refs_3_.refs_4_.same_ref), channel_id=1, source_target_pairs={{0,8},{8,0},{16,24},{24,16},{32,40},{40,32},{48,56},{56,48},{64,72... | collective-permute-start | bytes 1572872 | tf_op jit(solution)/shard_map/ppermute | solution.py:403
  50.8 9.0 %all-to-all-start.2 = ((bf16[4,272,128]{2,1,0:T(8,128)(2,1)}), bf16[4,272,128]{2,1,0:T(8,128)(2,1)S(1)}, u32[]{:S(2)}, u32[]{:S(2)}) async-start(bf16[4,272,128]{2,1,0:T(8,128)(2,1)} %get-tuple-element.43), calls=%async_computation.2 | async-start | bytes 557056 | tf_op jit(solution)/shard_map/all_to_all | solution.py:419
